TPU v7x, 256 devices: a whole 4x4x8 slice. The times are simulated.
256 devices in a mesh: src: 32 (over z_hi, x, core), tgt: 8 (over y, z_lo).
Axes of the slice: x: 4, y: 4, z: 8 (z_hi: 4, z_lo: 2; z = z_hi * 2 + z_lo), core: 2. Of those that a mesh axis runs over, the one named last changes fastest.
Arguments:
- source_feats: bfloat16 [32, 512, 384], P('src', 'tgt'), may hold values from -64 to 64
- source_tiles: bfloat16 [32, 512, 128], P('src', 'tgt'), may hold values from -0.5 to 0.5
- source_links: int32 [32, 8, 2], P('src', 'tgt'), may hold values from 0 to 7, as said below
- target_feats: bfloat16 [8, 2048, 384], P('tgt', 'src'), may hold values from -64 to 64
- target_tiles: bfloat16 [8, 2048, 128], P('tgt', 'src'), may hold values from -0.5 to 0.5
- target_links: int32 [8, 32, 2], P('tgt', 'src'), may hold values from 0 to 31, as said below
- near_first: bfloat16 [384, 384], replicated, may hold values from -0.3125 to 0.3125
- self_first: bfloat16 [384, 384], replicated, may hold values from -0.3125 to 0.3125
- near_second: bfloat16 [384, 384], replicated, may hold values from -0.3125 to 0.3125
- self_second: bfloat16 [384, 384], replicated, may hold values from -0.3125 to 0.3125
Outputs:
- source_potential: float32 [16384], P('src')
- target_potential: float32 [16384], P('tgt')
Inputs may be any that keep to these rules, and one draw needn't show every extreme that they name: `source_links`: the first entry of partition p is 7 - p; the other entries may repeat. `target_links`: the first entry of partition q is 31 - q; the other entries may repeat.
All inputs are finite; a program needn't handle non-finite values.
Results may differ from a plain program's by a relative error of at most 0.0036.
Values may be sent and summed in bfloat16 or wider, within the bound.
No kernel may reach another device: no remote copies, remote signals or barrier semaphores. Data moves between devices by JAX's collectives and lax.ppermute only.
A program may use at most 64 MiB of HBM per device.

v0:
```python
import math

import jax
import jax.numpy as jnp
from jax import lax
from jax.sharding import PartitionSpec as P

D = 384


def neighbour_sum(blocks, panels, links):
    part_count, row_count = (panels.shape[0], panels.shape[1])
    picked = blocks[links]
    shaped = panels.reshape(part_count, row_count, links.shape[1], row_count)
    summed = jnp.einsum("prkc,pkcd->prd", shaped, picked, preferred_element_type=jnp.float32)
    return summed.astype(jnp.bfloat16)


def layer_step(summed, hidden, near_weight, self_weight, layer_index):
    mixed = jnp.einsum("prd,de->pre", summed, near_weight, preferred_element_type=jnp.float32)
    mixed = mixed + jnp.einsum(
        "prd,de->pre", hidden, self_weight, preferred_element_type=jnp.float32
    )
    if layer_index == 0:
        mixed = jax.nn.relu(mixed)
    return mixed.astype(jnp.bfloat16)


def source_side(features, panels, links, weights):
    row_count = panels.shape[1]
    hidden = features
    part_links = links[0]
    for layer_index in range(2):
        whole = lax.all_gather(hidden, "tgt", axis=1, tiled=True)
        blocks = whole.reshape(-1, row_count, D)
        summed = neighbour_sum(blocks, panels, part_links)
        hidden = layer_step(
            summed, hidden, weights[2 * layer_index], weights[2 * layer_index + 1], layer_index
        )
    return lax.all_gather(hidden, "tgt", axis=1, tiled=True).reshape(-1, D)


def target_side(features, panels, links, weights):
    row_count = panels.shape[1]
    hidden = features
    part_links = links[0]
    for layer_index in range(2):
        whole = lax.all_gather(hidden, "src", axis=1, tiled=True)
        blocks = whole.reshape(-1, row_count, D)
        summed = neighbour_sum(blocks, panels, part_links)
        hidden = layer_step(
            summed, hidden, weights[2 * layer_index], weights[2 * layer_index + 1], layer_index
        )
    return lax.all_gather(hidden, "src", axis=1, tiled=True).reshape(-1, D)


def row_lse(top, total):
    larger = lax.pmax(top, "tgt")
    summed = lax.psum(total * jnp.exp(top - larger), "tgt")
    return larger + jnp.log(summed)


def col_lse(top, total):
    larger = lax.pmax(top, "src")
    summed = lax.psum(total * jnp.exp(top - larger), "src")
    return larger + jnp.log(summed)


def on_device(
    source_feats,
    source_tiles,
    source_links,
    target_feats,
    target_tiles,
    target_links,
    near_first,
    self_first,
    near_second,
    self_second,
):
    weights = (near_first, self_first, near_second, self_second)
    emb_source = source_side(source_feats, source_tiles, source_links, weights)
    emb_target = target_side(target_feats, target_tiles, target_links, weights)
    source_rows = emb_source.shape[0]
    target_cols = emb_target.shape[0]
    total_source = source_rows * lax.axis_size("src")
    total_target = target_cols * lax.axis_size("tgt")
    score_blocks = 0.2 * jnp.einsum(
        "rd,cd->rc", emb_source, emb_target, preferred_element_type=jnp.float32
    )
    target_potential = jnp.zeros((target_cols,), jnp.float32)
    source_potential = jnp.zeros((source_rows,), jnp.float32)
    for sweep_index in range(2):
        shifted = score_blocks + target_potential[None, :]
        top = jnp.max(shifted, axis=1)
        total = jnp.sum(jnp.exp(shifted - top[:, None]), axis=1)
        source_potential = math.log(total_target) - row_lse(top, total)
        shifted = score_blocks + source_potential[:, None]
        col_top = jnp.max(shifted, axis=0)
        col_total = jnp.sum(jnp.exp(shifted - col_top[None, :]), axis=0)
        target_potential = math.log(total_source) - col_lse(col_top, col_total)
    return (source_potential, target_potential)


def solution(mesh):
    return jax.shard_map(
        on_device,
        mesh=mesh,
        in_specs=(
            P("src", "tgt", None),
            P("src", "tgt", None),
            P("src", "tgt", None),
            P("tgt", "src", None),
            P("tgt", "src", None),
            P("tgt", "src", None),
            P(),
            P(),
            P(),
            P(),
        ),
        out_specs=(P("src"), P("tgt")),
        check_vma=False,
    )
```

profile of v0, /device:TPU:1, one launch (start us, length us, event | category | flops | bytes accessed | tf_op | source)
XLA Modules:
  0.0 601.1 jit_solution(15205281891374754381)
XLA Ops:
  7.2 0.0 copy-start
  7.2 0.0 all-gather.8.cloned.1.call-start
  7.2 0.7 all-gather.8.cloned.1.call-update
  7.9 0.0 all-gather.10.cloned.1.call-start
  8.0 0.8 copy.15
  8.8 0.7 fusion.23
  9.5 1.0 fusion.18
  10.5 57.5 %all-gather.8.cloned.1.call-done = bf16[1,2048,384]{2,1,0:T(8,128)(2,1)} async-done(((bf16[1,64,384]{2,1,0:T(8,128)(2,1)}), bf16[1,2048,384]{2,1,0:T(8,128)(2,1)}) %all-gather.8.cloned.1.call-update) | async-done | bytes 1572880 | tf_op jit(solution)/shard_map/all_gather | solution.py:48
  68.0 2.0 gather_fusion.2
  70.0 2.0 fusion.16
  71.9 0.0 all-gather.10.cloned.1.call-update
  72.0 0.0 all-gather.12.cloned.1.call-start
  72.0 1.2 fusion.26
  73.2 49.2 %all-gather.10.cloned.1.call-done = bf16[2048,384]{1,0:T(8,128)(2,1)} async-done(((bf16[64,384]{1,0:T(8,128)(2,1)}), bf16[2048,384]{1,0:T(8,128)(2,1)}) %all-gather.10.cloned.1.call-update) | async-done | bytes 1572880 | tf_op jit(solution)/shard_map/all_gather | solution.py:48
  122.4 2.0 gather_fusion.3
  124.4 2.0 fusion.17
  126.4 0.0 all-gather.12.cloned.1.call-update
  126.4 0.8 copy.14
  127.3 0.7 fusion.22
  127.9 24.4 %all_gather.18 = bf16[1,512,384]{2,1,0:T(8,128)(2,1)S(1)} all-gather(bf16[1,64,384]{2,1,0:T(8,128)(2,1)} %param.10), channel_id=1, replica_groups=mesh['src'=32,'tgt'=8] {'tgt'}, dimensions={1}, use_global_device_ids=true | all-gather | bytes 442368 | tf_op jit(solution)/shard_map/all_gather | solution.py:34
  152.3 0.6 gather_fusion
  152.9 1.0 fusion.20
  153.9 1.4 fusion.14
  155.3 24.7 %all-gather = bf16[512,384]{1,0:T(8,128)(2,1)S(1)} all-gather(bf16[64,384]{1,0:T(8,128)(2,1)S(1)} %fusion.14), channel_id=2, replica_groups=mesh['src'=32,'tgt'=8] {'tgt'}, dimensions={0}, use_global_device_ids=true | all-gather | bytes 442368 | tf_op jit(solution)/shard_map/all_gather | solution.py:34
  180.0 0.6 gather_fusion.1
  180.5 0.2 fusion.25
  180.7 0.4 fusion.15
  181.2 24.2 %all-gather.1 = bf16[512,384]{1,0:T(8,128)(2,1)S(1)} all-gather(bf16[64,384]{1,0:T(8,128)(2,1)S(1)} %fusion.15), channel_id=3, replica_groups=mesh['src'=32,'tgt'=8] {'tgt'}, dimensions={0}, use_global_device_ids=true | all-gather | bytes 442368 | tf_op jit(solution)/shard_map/all_gather | solution.py:40
  205.3 4.6 fusion.24
  209.9 15.4 %pmax.28 = f32[512]{0:T(512)S(1)} all-reduce(f32[512]{0:T(512)S(1)} %get-tuple-element.2), channel_id=1, replica_groups=mesh['src'=32,'tgt'=8] {'tgt'}, use_global_device_ids=true, to_apply=%region_1.2 | all-reduce | flops 512 | bytes 4096 | tf_op jit(solution)/shard_map/pmax | solution.py:58
  225.3 2.9 exponential_reduce_fusion.3
  228.2 12.6 %psum.28 = f32[512]{0:T(512)S(1)} all-reduce(f32[512]{0:T(512)S(1)} %exponential_multiply_fusion.3), channel_id=1, replica_groups=mesh['src'=32,'tgt'=8] {'tgt'}, use_global_device_ids=true, to_apply=%region_3.4 | all-reduce | flops 512 | bytes 4096 | tf_op jit(solution)/shard_map/psum | solution.py:59
  240.8 2.7 add_reduce_fusion.2
  243.5 0.7 copy-done.1
  244.3 0.8 exponential_reduce_fusion.2
  245.0 93.4 %pmax.29 = f32[2048]{0:T(1024)S(1)} all-reduce(f32[2048]{0:T(1024)S(1)} %add_reduce_fusion.2), channel_id=1, replica_groups=mesh['src'=32,'tgt'=8] {'src'}, use_global_device_ids=true, to_apply=%region_5.6 | all-reduce | flops 2048 | bytes 16384 | tf_op jit(solution)/shard_map/pmax | solution.py:64
  338.4 71.0 %psum.29 = f32[2048]{0:T(1024)S(1)} all-reduce(f32[2048]{0:T(1024)S(1)} %exponential_multiply_fusion.1), channel_id=1, replica_groups=mesh['src'=32,'tgt'=8] {'src'}, use_global_device_ids=true, to_apply=%region_7.8 | all-reduce | flops 2048 | bytes 16384 | tf_op jit(solution)/shard_map/psum | solution.py:65
  409.4 2.7 add_reduce_fusion.1
  412.1 0.7 copy-done.2
  412.9 0.8 exponential_reduce_fusion.1
  413.7 14.2 %pmax.30 = f32[512]{0:T(512)S(1)} all-reduce(f32[512]{0:T(512)S(1)} %add_reduce_fusion.1), channel_id=1, replica_groups=mesh['src'=32,'tgt'=8] {'tgt'}, use_global_device_ids=true, to_apply=%region_9.10 | all-reduce | flops 512 | bytes 4096 | tf_op jit(solution)/shard_map/pmax | solution.py:58
  427.9 12.9 %psum.30 = f32[512]{0:T(512)S(1)} all-reduce(f32[512]{0:T(512)S(1)} %exponential_multiply_fusion.2), channel_id=1, replica_groups=mesh['src'=32,'tgt'=8] {'tgt'}, use_global_device_ids=true, to_apply=%region_11.12 | all-reduce | flops 512 | bytes 4096 | tf_op jit(solution)/shard_map/psum | solution.py:59
  440.8 2.7 add_reduce_fusion
  443.5 0.7 copy-done.3
  444.2 0.8 exponential_reduce_fusion
  445.0 77.9 %pmax.31 = f32[2048]{0:T(1024)S(1)} all-reduce(f32[2048]{0:T(1024)S(1)} %add_reduce_fusion), channel_id=1, replica_groups=mesh['src'=32,'tgt'=8] {'src'}, use_global_device_ids=true, to_apply=%region_13.14 | all-reduce | flops 2048 | bytes 16384 | tf_op jit(solution)/shard_map/pmax | solution.py:64
  523.0 70.9 %psum.31 = f32[2048]{0:T(1024)S(1)} all-reduce(f32[2048]{0:T(1024)S(1)} %exponential_multiply_fusion), channel_id=1, replica_groups=mesh['src'=32,'tgt'=8] {'src'}, use_global_device_ids=true, to_apply=%region_15.16 | all-reduce | flops 2048 | bytes 16384 | tf_op jit(solution)/shard_map/psum | solution.py:65
  593.9 0.6 add_subtract_fusion
  (20 shorter events, 0.1 us)
Async XLA Ops:
  7.2 2.3 copy-start
  7.2 173.4 %copy-start.4 = (bf16[384,384]{1,0:T(8,128)(2,1)S(1)}, bf16[384,384]{1,0:T(8,128)(2,1)}, u32[]{:S(2)}) copy-start(bf16[384,384]{1,0:T(8,128)(2,1)} %param.19) | copy-start | bytes 884740
  7.2 173.5 %copy-start.5 = (bf16[384,384]{1,0:T(8,128)(2,1)S(1)}, bf16[384,384]{1,0:T(8,128)(2,1)}, u32[]{:S(2)}) copy-start(bf16[384,384]{1,0:T(8,128)(2,1)} %param.18) | copy-start | bytes 884740
  7.2 60.8 %all-gather.8.cloned.1.call-start = ((), (), s32[]{:S(2)}) async-start(), calls=%async_computation | async-start | bytes 1622016 | tf_op jit(solution)/shard_map/all_gather | solution.py:48
  7.9 114.5 %all-gather.10.cloned.1.call-start = ((), (), s32[]{:S(2)}) async-start(), calls=%async_computation.1 | async-start | bytes 1622016 | tf_op jit(solution)/shard_map/all_gather | solution.py:48
  72.0 133.4 %all-gather.12.cloned.1.call-start = ((), (), s32[]{:S(2)}) async-start(), calls=%async_computation.2 | async-start | bytes 1622016 | tf_op jit(solution)/shard_map/all_gather | solution.py:54
  240.8 3.4 copy-start.1
  409.4 3.5 copy-start.2
  440.8 3.5 copy-start.3
  440.8 4.2 copy-start.6
Sparse Core Ops, SparseCore 0:
  10.6 57.3 all-gather.7
  72.1 50.2 all-gather.9
  126.6 51.1 all-gather.11
where the time goes:
time: 602 us; the launch traced here: 601 us
  blocking collectives  442 us (73%)
  waiting for transfers between devices  107 us (18%)
  other arithmetic  15.3 us (3%)
  between operations  14 us (2%)
  matrix products  13.7 us (2%)
  local copies, waits for them, and re-layouts  8.97 us (1%)
    pmax x2, blocking collectives, col_lse(): larger = lax.pmax(top, 'src')  171 us
    psum x2, blocking collectives, col_lse(): summed = lax.psum(total * jnp.exp(top - larger), 'src')  142 us
    all_gather x2, waiting for transfers between devices, target_side(): whole = lax.all_gather(hidden, 'src', axis=1, tiled=True)  107 us
    all_gather x2, blocking collectives, source_side(): whole = lax.all_gather(hidden, 'tgt', axis=1, tiled=True)  49.1 us
    pmax x2, blocking collectives, row_lse(): larger = lax.pmax(top, 'tgt')  29.6 us
    psum x2, blocking collectives, row_lse(): summed = lax.psum(total * jnp.exp(top - larger), 'tgt')  25.4 us
    all_gather x1, blocking collectives, source_side(): return lax.all_gather(hidden, 'tgt', axis=1, tiled=True).reshape(-1, D)  24.2 us
  transfers between devices with their start and end apart: 3, of which 2 were waited for; matrix products, arithmetic and copies ran while one was open for 2% of the time, Pallas kernels for 0%

commit v1 on v0

v1 whole, which is shorter than its diff:
```python
import functools
import math

import jax
import jax.numpy as jnp
from jax import lax
from jax.experimental import pallas as pl
from jax.experimental.pallas import tpu as pltpu
from jax.sharding import Mesh, PartitionSpec as P

D = 384
PART = 64
PACK = 272
ROWS = 512
COLS = 2048
LANES = 128
ROW_BLOCKS = ROWS // LANES
COL_BLOCKS = COLS // LANES
N_TGT = 8
N_PEERS = 16
LOG_N = math.log(16384.0)
VMEM_LIMIT = 32 * 1024 * 1024

VMEM = functools.partial(pl.BlockSpec, memory_space=pltpu.VMEM)
SMEM = functools.partial(pl.BlockSpec, memory_space=pltpu.SMEM)


def pack(features, tiles, links):
    link = jnp.broadcast_to(links[0, 0, 1].astype(jnp.bfloat16), (16, LANES))
    feats = features[0]
    pieces = [feats[:, at : at + LANES] for at in range(0, D, LANES)]
    return jnp.concatenate(pieces + [tiles[0], link], axis=0)[None]


def graph_layers(packed, first, second, near1, self1, near2, self2, x_ref, s_ref, h_ref, emit):
    count = x_ref.shape[0] // PART
    for k in range(count):
        ref, at = packed(k)
        for piece in range(D // LANES):
            x_ref[k * PART : (k + 1) * PART, piece * LANES : (piece + 1) * LANES] = ref[
                at, piece * PART : (piece + 1) * PART, :
            ]

    def neighbour_sums(src):
        for k in range(count):
            ref, at = packed(k)
            near = src[pl.ds(first(k) * PART, PART), :]
            other = src[pl.ds(pl.multiple_of(second(k) * PART, PART), PART), :]
            panel = ref[at, 3 * PART : 4 * PART, :]
            both = jnp.concatenate([near, other], axis=0)
            total = jnp.dot(panel, both, preferred_element_type=jnp.float32)
            s_ref[k * PART : (k + 1) * PART, :] = total.astype(jnp.bfloat16)

    step = 256
    neighbour_sums(x_ref)
    for at in range(0, count * PART, step):
        rows = pl.ds(at, step)
        mixed = jnp.dot(s_ref[rows, :], near1[...], preferred_element_type=jnp.float32)
        mixed += jnp.dot(x_ref[rows, :], self1[...], preferred_element_type=jnp.float32)
        h_ref[rows, :] = jnp.maximum(mixed, 0.0).astype(jnp.bfloat16)
    neighbour_sums(h_ref)
    for at in range(0, count * PART, step):
        rows = pl.ds(at, step)
        mixed = jnp.dot(s_ref[rows, :], near2[...], preferred_element_type=jnp.float32)
        mixed += jnp.dot(h_ref[rows, :], self2[...], preferred_element_type=jnp.float32)
        emit(at, mixed.astype(jnp.bfloat16))


def source_kernel(links, packed, near1, self1, near2, self2, out, x_ref, s_ref, h_ref):
    def emit(at, value):
        out[at : at + value.shape[0], :] = value

    graph_layers(
        lambda k: (packed, k),
        lambda k: 7 - k,
        lambda k: links[k],
        near1, self1, near2, self2, x_ref, s_ref, h_ref, emit,
    )


def slot_xor(k):
    b0, b1, b2, b3, b4 = ((k >> bit) & 1 for bit in range(5))
    return ((b0 ^ (3 * b1)) << 3) | ((b2 ^ (3 * b3)) << 1) | b4


SLOT_OF = {slot_xor(k): k for k in range(32)}


def slot_of(v):
    z1, z0, x1, x0, c = ((v >> bit) & 1 for bit in (4, 3, 2, 1, 0))
    return (z0 ^ z1) | (z1 << 1) | ((x0 ^ x1) << 2) | (x1 << 3) | (c << 4)


def spread(row):
    return jnp.transpose(jnp.broadcast_to(row, (LANES, LANES)))


def target_kernel(
    links, own, other, near1, self1, near2, self2, emb_source,
    scores, send,
    x_ref, s_ref, h_ref, e_ref,
):
    me = links[32]

    def emit(at, value):
        for piece in range(value.shape[0] // PART):
            q = me ^ slot_xor(at // PART + piece)
            e_ref[pl.ds(pl.multiple_of(q * PART, PART), PART), :] = value[piece * PART : (piece + 1) * PART, :]

    graph_layers(
        lambda k: (own, k) if k < 16 else (other, k - 16),
        lambda k: k ^ SLOT_OF[31],
        lambda k: links[k],
        near1, self1, near2, self2, x_ref, s_ref, h_ref, emit,
    )

    for i in range(COL_BLOCKS // 2):
        part = lax.dot_general(
            emb_source[...],
            e_ref[i * 256 : (i + 1) * 256, :],
            (((1,), (1,)), ((), ())),
            preferred_element_type=jnp.float32,
        )
        part = 0.2 * part
        scores[2 * i] = part[:, :LANES]
        scores[2 * i + 1] = part[:, LANES:]

    for b in range(ROW_BLOCKS):
        rows = pl.ds(b * LANES, LANES)
        top = scores[0, rows, :]
        for i in range(1, COL_BLOCKS):
            top = jnp.maximum(top, scores[i, rows, :])
        total = jnp.exp(scores[0, rows, :] - top)
        for i in range(1, COL_BLOCKS):
            total += jnp.exp(scores[i, rows, :] - top)
        top, total = jnp.transpose(top), jnp.transpose(total)
        larger = jnp.max(top, axis=0, keepdims=True)
        total = jnp.sum(total * jnp.exp(top - larger), axis=0, keepdims=True)
        for d in range(N_TGT):
            send[d, b : b + 1, :] = larger
            send[d, b + 4 : b + 5, :] = total


def column_kernel(scores, got, weights, tops, lse, potential, shift):
    top, total = got[0, 0:4, :], got[0, 4:8, :]
    larger = top
    for d in range(1, N_TGT):
        larger = jnp.maximum(larger, got[d, 0:4, :])
    total = total * jnp.exp(top - larger)
    for d in range(1, N_TGT):
        total += got[d, 4:8, :] * jnp.exp(got[d, 0:4, :] - larger)
    source = LOG_N - (larger + jnp.log(total))
    potential[0:4, :] = source
    potential[4:8, :] = source
    for b in range(ROW_BLOCKS):
        shift[pl.ds(b * LANES, LANES), :] = spread(source[b : b + 1, :])

    @pl.loop(0, COL_BLOCKS)
    def _(i):
        x = (scores[i] + shift[...]).reshape(ROWS // 8, 8, LANES)
        top = jnp.max(x, axis=0)
        e = jnp.exp(x - top[None])
        weights[i] = e.reshape(ROWS, LANES)
        total = jnp.sum(e, axis=0)
        tops[i] = top
        larger = jnp.max(top, axis=0, keepdims=True)
        total = jnp.sum(total * jnp.exp(top - larger), axis=0, keepdims=True)
        lse[pl.ds(i, 1), :] = larger + jnp.log(total)


def row_kernel(weights, tops, got, send, potential, scale):
    larger = got[0]
    for d in range(1, N_PEERS):
        larger = jnp.maximum(larger, got[d])
    total = jnp.exp(got[0] - larger)
    for d in range(1, N_PEERS):
        total += jnp.exp(got[d] - larger)
    target = LOG_N - (larger + jnp.log(total))
    potential[...] = target
    for i in range(COL_BLOCKS):
        scale[i] = jnp.exp(tops[i] + target[i : i + 1, :])
    for b in range(ROW_BLOCKS):
        rows = pl.ds(b * LANES, LANES)
        total = jnp.zeros((LANES // 8, 8, LANES), jnp.float32)
        for i in range(COL_BLOCKS):
            total += weights[i, rows, :].reshape(LANES // 8, 8, LANES) * scale[i][None]
        total = jnp.transpose(total.reshape(LANES, LANES))
        total = jnp.sum(total, axis=0, keepdims=True)
        for d in range(N_TGT):
            send[d, b : b + 1, :] = total
            send[d, b + 4 : b + 5, :] = total


def last_kernel(weights, scale, got, before, sums, potential, factor):
    total = got[0, 0:4, :]
    for d in range(1, N_TGT):
        total += got[d, 0:4, :]
    source = before[0:4, :] + (LOG_N - jnp.log(total))
    potential[0:4, :] = source
    potential[4:8, :] = source
    ratio = 16384.0 / total
    for b in range(ROW_BLOCKS):
        factor[pl.ds(b * LANES, LANES), :] = spread(ratio[b : b + 1, :])

    @pl.loop(0, COL_BLOCKS)
    def _(i):
        e = (weights[i] * factor[...]).reshape(ROWS // 8, 8, LANES)
        sums[pl.ds(i, 1), :] = jnp.sum(jnp.sum(e, axis=0) * scale[i], axis=0, keepdims=True)


def call(kernel, outs, scratch, ins):
    return pl.pallas_call(
        kernel,
        out_shape=[jax.ShapeDtypeStruct(shape, dtype) for shape, dtype in outs],
        in_specs=ins,
        out_specs=[VMEM() for _ in outs],
        scratch_shapes=scratch,
        compiler_params=pltpu.CompilerParams(vmem_limit_bytes=VMEM_LIMIT),
    )


def swap(value, axis, size, xor):
    return lax.ppermute(value, axis, [(i, i ^ xor) for i in range(size)])


def exchange(value, axes):
    return lax.all_to_all(value, axes, 0, 0)


def on_device(
    source_feats, source_tiles, source_links, target_feats, target_tiles, target_links,
    near_first, self_first, near_second, self_second,
):
    f32, bf16 = jnp.float32, jnp.bfloat16
    weights = (near_first, self_first, near_second, self_second)
    me = lax.axis_index(("zh", "x", "c"))

    held = pack(target_feats, target_tiles, target_links)
    for axis, xor in (("zh", 1), ("zh", 3), ("x", 1), ("x", 3)):
        held = jnp.concatenate([held, swap(held, axis, 4, xor)], axis=0)
    other = swap(held, "c", 2, 1)

    packed = pack(source_feats, source_tiles, source_links)
    packed = exchange(jnp.broadcast_to(packed, (N_TGT, PACK, LANES)), ("y", "zl"))
    source_second = packed[:, 4 * PART, 0].astype(jnp.int32)
    (emb_source,) = call(
        source_kernel,
        [((ROWS, D), bf16)],
        [pltpu.VMEM((ROWS, D), bf16)] * 3,
        [SMEM()] + [VMEM()] * 5,
    )(source_second, packed, *weights)

    target_second = jnp.concatenate([held[:, 4 * PART, 0], other[:, 4 * PART, 0]]).astype(jnp.int32)
    target_slots = jnp.concatenate([slot_of(target_second ^ me), me[None]])
    scores, send = call(
        target_kernel,
        [((COL_BLOCKS, ROWS, LANES), f32), ((N_TGT, 8, LANES), f32)],
        [pltpu.VMEM((COLS, D), bf16)] * 4,
        [SMEM()] + [VMEM()] * 7,
    )(target_slots, held, other, *weights, emb_source)

    got = exchange(send, ("y", "zl"))
    spread_weights, tops, lse, source_first = call(
        column_kernel,
        [
            ((COL_BLOCKS, ROWS, LANES), f32),
            ((COL_BLOCKS, 8, LANES), f32),
            ((COL_BLOCKS, LANES), f32),
            ((8, LANES), f32),
        ],
        [pltpu.VMEM((ROWS, LANES), f32)],
        [VMEM()] * 2,
    )(scores, got)

    lse = jnp.logaddexp(lse, swap(lse, "c", 2, 1))
    got = exchange(jnp.broadcast_to(lse, (N_PEERS, COL_BLOCKS, LANES)), ("zh", "x"))
    send, target_first, scale = call(
        row_kernel,
        [((N_TGT, 8, LANES), f32), ((COL_BLOCKS, LANES), f32), ((COL_BLOCKS, 8, LANES), f32)],
        [],
        [VMEM()] * 3,
    )(spread_weights, tops, got)

    got = exchange(send, ("y", "zl"))
    sums, source_potential = call(
        last_kernel,
        [((COL_BLOCKS, LANES), f32), ((8, LANES), f32)],
        [pltpu.VMEM((ROWS, LANES), f32)],
        [VMEM()] * 4,
    )(spread_weights, scale, got, source_first)

    sums = sums + swap(sums, "c", 2, 1)
    got = exchange(jnp.broadcast_to(sums, (N_PEERS, COL_BLOCKS, LANES)), ("zh", "x"))
    target_potential = target_first + (LOG_N - jnp.log(jnp.sum(got, axis=0)))
    return source_potential[0:4].reshape(ROWS), target_potential.reshape(COLS)


def solution(mesh):
    fine = Mesh(mesh.devices.reshape(4, 4, 2, 4, 2), ("zh", "x", "c", "y", "zl"))
    src, tgt = ("zh", "x", "c"), ("y", "zl")
    return jax.shard_map(
        on_device,
        mesh=fine,
        in_specs=(P(src, tgt, None),) * 3 + (P(tgt, src, None),) * 3 + (P(),) * 4,
        out_specs=(P(src), P(tgt)),
        check_vma=False,
    )
```

time: 602 us -> 120 us (0.20)
  blocking collectives: 442 us -> 30.9 us
  waiting for transfers between devices: 107 us -> 25 us
  starting transfers between devices: 0.12 us -> 32.1 us
  Pallas kernels: 0 us -> 15.6 us
  matrix products: 13.7 us -> 0 us
  between operations: 14 us -> 0.8 us
  other arithmetic: 15.3 us -> 2.47 us
    pmax x4 -> x0, blocking collectives: 201 us -> none  [the longest x2 171 us: col_lse(): larger = lax.pmax(top, 'src')]
    psum x4 -> x0, blocking collectives: 167 us -> none  [the longest x2 142 us: col_lse(): summed = lax.psum(total * jnp.exp(top - larger), 'src')]
    all_gather x3 -> x0, waiting for transfers between devices: 107 us -> none  [the longest x2 107 us: target_side(): whole = lax.all_gather(hidden, 'src', axis=1, tiled=True)]
    all_gather x3 -> x0, blocking collectives: 73.2 us -> none  [the longest x2 49.1 us: source_side(): whole = lax.all_gather(hidden, 'tgt', axis=1, tiled=True)]
    all_to_all x0 -> x3, blocking collectives: none -> 30.9 us  [exchange(): return lax.all_to_all(value, axes, 0, 0)]
    ppermute x0 -> x7, starting transfers between devices: none -> 18.9 us  [swap(): return lax.ppermute(value, axis, [(i, i ^ xor) for i in range(size)])]
    ppermute x0 -> x7, waiting for transfers between devices: none -> 16.1 us  [swap(): return lax.ppermute(value, axis, [(i, i ^ xor) for i in range(size)])]
    pallas_call x0 -> x5, Pallas kernels: none -> 15.6 us  [the longest x1 9.1 us: on_device(): call(target_kernel, [((COL_BLOCKS, ROWS, LANES), f32), ((N_TGT, 8, LANES)...]
  transfers between devices with their start and end apart: 3 -> 9, of which waited for: 2 -> 5; matrix products, arithmetic and copies ran while one was open for 2% -> 6% of each run, Pallas kernels for 0% -> 2%
where the time goes in v1:
time: 120 us; the launch traced here: 119 us
  starting transfers between devices  32.1 us (27%)
  blocking collectives  30.9 us (26%)
  waiting for transfers between devices  25 us (21%)
  Pallas kernels  15.6 us (13%)
  local copies, waits for them, and re-layouts  11.8 us (10%)
  other arithmetic  2.47 us (2%)
    all_to_all x3, blocking collectives, exchange(): return lax.all_to_all(value, axes, 0, 0)  30.9 us
    ppermute x7, starting transfers between devices, swap(): return lax.ppermute(value, axis, [(i, i ^ xor) for i in range(size)])  18.9 us
    ppermute x7, waiting for transfers between devices, swap(): return lax.ppermute(value, axis, [(i, i ^ xor) for i in range(size)])  16.1 us
    all_to_all x2, starting transfers between devices, exchange(): return lax.all_to_all(value, axes, 0, 0)  13.2 us
    pallas_call x1, Pallas kernels, on_device(): call(target_kernel, [((COL_BLOCKS, ROWS, LANES), f32), ((N_TGT, 8, LANES)...  9.1 us
    all_to_all x2, waiting for transfers between devices, exchange(): return lax.all_to_all(value, axes, 0, 0)  8.83 us
    unnamed x20, local copies, waits for them, and re-layouts  5.89 us
    pallas_call x1, Pallas kernels, on_device(): call(source_kernel, [((ROWS, D), bf16)], [pltpu.VMEM((ROWS, D), bf16)] *...  2.4 us
  transfers between devices with their start and end apart: 9, of which 5 were waited for; matrix products, arithmetic and copies ran while one was open for 6% of the time, Pallas kernels for 2%

profile of v1, /device:TPU:1, one launch (start us, length us, event | category | flops | bytes accessed | tf_op | source)
XLA Modules:
  0.0 118.6 jit_solution(12009611876722110234)
XLA Ops:
  0.6 0.7 convert.7
  1.3 0.6 slice.41
  1.9 0.7 constant_dynamic-update-slice_fusion.4
  2.6 0.7 constant_dynamic-update-slice_fusion.3
  3.3 0.7 constant_dynamic-update-slice_fusion.2
  4.0 0.7 constant_dynamic-update-slice_fusion.1
  4.8 0.7 constant_dynamic-update-slice_fusion
  5.4 3.9 %collective-permute-start = (bf16[1,272,128]{2,1,0:T(8,128)(2,1)S(1)}, bf16[1,272,128]{2,1,0:T(8,128)(2,1)S(1)}, u32[]{:S(2)}, u32[]{:S(2)}) collective-permute-start(bf16[1,272,128]{2,1,0:T(8,128)(2,1)S(1)} %bitcast.15), channel_id=1, source_target_pairs={{0,64},{64,0},{128,192},{192,128},{1,65},{65,1},{129,193},{193,129... | collective-permute-start | bytes 208904 | tf_op jit(solution)/shard_map/ppermute | solution.py:223
  9.3 0.7 constant_dynamic-update-slice_fusion.14
  10.0 0.7 constant_dynamic-update-slice_fusion.13
  10.8 0.7 convert.8
  11.4 0.6 slice.47
  12.0 4.6 %collective-permute-start.1 = (bf16[2,272,128]{2,1,0:T(8,128)(2,1)S(1)}, bf16[2,272,128]{2,1,0:T(8,128)(2,1)S(1)}, u32[]{:S(2)}, u32[]{:S(2)}) collective-permute-start(bf16[2,272,128]{2,1,0:T(8,128)(2,1)S(1)} %pad_maximum_fusion.2), channel_id=1, source_target_pairs={{0,192},{64,128},{128,64},{192,0},{1,193},{65,129},{129,65},{193,1... | collective-permute-start | bytes 417800 | tf_op jit(solution)/shard_map/ppermute | solution.py:223
  16.6 0.7 constant_dynamic-update-slice_fusion.12
  17.4 2.1 %collective-permute-done.1 = bf16[2,272,128]{2,1,0:T(8,128)(2,1)S(1)} collective-permute-done((bf16[2,272,128]{2,1,0:T(8,128)(2,1)S(1)}, bf16[2,272,128]{2,1,0:T(8,128)(2,1)S(1)}, u32[]{:S(2)}, u32[]{:S(2)}) %collective-permute-start.1) | collective-permute-done | bytes 139296 | tf_op jit(solution)/shard_map/ppermute | solution.py:223
  19.5 1.3 %collective-permute-start.2 = (bf16[4,272,128]{2,1,0:T(8,128)(2,1)S(1)}, bf16[4,272,128]{2,1,0:T(8,128)(2,1)S(1)}, u32[]{:S(2)}, u32[]{:S(2)}) collective-permute-start(bf16[4,272,128]{2,1,0:T(8,128)(2,1)S(1)} %pad_maximum_fusion.1), channel_id=1, source_target_pairs={{0,16},{16,0},{32,48},{48,32},{1,17},{17,1},{33,49},{49,33},{2,18}... | collective-permute-start | bytes 835592 | tf_op jit(solution)/shard_map/ppermute | solution.py:223
  20.8 0.7 constant_dynamic-update-slice_fusion.11
  21.5 0.7 constant_dynamic-update-slice_fusion.10
  22.2 0.9 broadcast_in_dim.28
  23.1 9.7 %all-to-all-start = ((bf16[8,272,128]{2,1,0:T(8,128)(2,1)}), bf16[8,272,128]{2,1,0:T(8,128)(2,1)S(1)}, u32[]{:S(2)}, u32[]{:S(2)}) async-start(bf16[8,272,128]{2,1,0:T(8,128)(2,1)} %broadcast_in_dim.28), calls=%async_computation | async-start | bytes 1114112 | tf_op jit(solution)/shard_map/all_to_all | solution.py:227
  32.8 0.1 pad_maximum_fusion
  32.9 0.0 copy-start.1
  32.9 1.9 %collective-permute-start.3 = (bf16[8,272,128]{2,1,0:T(8,128)(2,1)S(1)}, bf16[8,272,128]{2,1,0:T(8,128)(2,1)S(1)}, u32[]{:S(2)}, u32[]{:S(2)}) collective-permute-start(bf16[8,272,128]{2,1,0:T(8,128)(2,1)S(1)} %pad_maximum_fusion), channel_id=1, source_target_pairs={{0,48},{16,32},{32,16},{48,0},{1,49},{17,33},{33,17},{49,1},{2,50}... | collective-permute-start | bytes 1671176 | tf_op jit(solution)/shard_map/ppermute | solution.py:223
  34.9 12.4 %collective-permute-done.3 = bf16[8,272,128]{2,1,0:T(8,128)(2,1)S(1)} collective-permute-done((bf16[8,272,128]{2,1,0:T(8,128)(2,1)S(1)}, bf16[8,272,128]{2,1,0:T(8,128)(2,1)S(1)}, u32[]{:S(2)}, u32[]{:S(2)}) %collective-permute-start.3) | collective-permute-done | bytes 557088 | tf_op jit(solution)/shard_map/ppermute | solution.py:223
  47.3 0.1 constant_dynamic-update-slice_fusion.5.own
  47.4 2.2 %collective-permute-start.4 = (bf16[16,272,128]{2,1,0:T(8,128)(2,1)S(1)}, bf16[16,272,128]{2,1,0:T(8,128)(2,1)}, u32[]{:S(2)}, u32[]{:S(2)}) collective-permute-start(bf16[16,272,128]{2,1,0:T(8,128)(2,1)S(1)} %constant_dynamic-update-slice_fusion.5.own), channel_id=1, source_target_pairs={{0,8},{8,0},{1,9},{9,1},{2,10},{10,2},{3,11},{11,3},{4,12},{12,4},... | collective-permute-start | bytes 3342344 | tf_op jit(solution)/shard_map/ppermute | solution.py:223
  49.6 0.2 fusion.links
  49.9 2.4 %shard_map.113.emb_source = bf16[512,384]{1,0:T(8,128)(2,1)S(1)} custom-call(s32[8]{0:T(128)S(1)} %fusion.links, bf16[8,272,128]{2,1,0:T(8,128)(2,1)S(1)} %all-to-all-done.packed, bf16[384,384]{1,0:T(8,128)(2,1)S(1)} %copy-done, bf16[384,384]{1,0:T(8,128)(2,1)S(1)} %copy-done.1, bf16[384,384]{1,0:T(8,128)(2,1)S(1)} %copy-done.2, bf16[384,384]{1,0:T(8,128)(2,1)S(1)} %copy-done.3), custom_call_target="tpu_custom_call" | custom-call | tf_op jit(solution)/shard_map/pallas_call | solution.py:246
  52.3 0.2 slice_reduce_fusion.1
  52.5 1.0 slice_reduce_fusion
  53.5 0.1 shift-left_or_fusion
  53.6 0.1 pad_add_fusion.links
  53.6 9.1 %shard_map.114 = (f32[16,512,128]{2,1,0:T(8,128)S(1)}, f32[8,8,128]{2,1,0:T(8,128)S(1)}) custom-call(s32[33]{0:T(128)S(1)} %pad_add_fusion.links, bf16[16,272,128]{2,1,0:T(8,128)(2,1)S(1)} %constant_dynamic-update-slice_fusion.5.own, bf16[16,272,128]{2,1,0:T(8,128)(2,1)} %collective-permute-done.4.other, bf16[384,384]{1,0:T(8,128)(2,1)S(1)} %copy-done, ...), custom_call_target="tpu_custom_call" | custom-call | tf_op jit(solution)/shard_map/pallas_call | solution.py:255
  62.7 10.0 %all_to_all.25.got = f32[8,8,128]{2,1,0:T(8,128)S(1)} all-to-all(f32[8,8,128]{2,1,0:T(8,128)S(1)} %get-tuple-element.14), channel_id=1, replica_groups=mesh['zh'=4,'x'=4,'c'=2,'y'=4,'zl'=2] {'y','zl'}, dimensions={0} | all-to-all | bytes 65536 | tf_op jit(solution)/shard_map/all_to_all | solution.py:227
  72.8 2.3 %shard_map.115 = (f32[16,512,128]{2,1,0:T(8,128)S(1)}, f32[16,8,128]{2,1,0:T(8,128)S(1)}, f32[16,128]{1,0:T(8,128)S(1)}, f32[8,128]{1,0:T(8,128)S(1)}) custom-call(f32[16,512,128]{2,1,0:T(8,128)S(1)} %get-tuple-element.13.scores, f32[8,8,128]{2,1,0:T(8,128)S(1)} %all_to_all.25.got), custom_call_target="tpu_custom_call" | custom-call | tf_op jit(solution)/shard_map/pallas_call | solution.py:263
  75.1 1.6 %collective-permute-start.5 = (f32[16,128]{1,0:T(8,128)S(1)}, f32[16,128]{1,0:T(8,128)S(1)}, u32[]{:S(2)}, u32[]{:S(2)}) collective-permute-start(f32[16,128]{1,0:T(8,128)S(1)} %get-tuple-element.17), channel_id=1, source_target_pairs={{0,8},{8,0},{1,9},{9,1},{2,10},{10,2},{3,11},{11,3},{4,12},{12,4},... | collective-permute-start | bytes 24584 | tf_op jit(solution)/shard_map/ppermute | solution.py:223
  76.6 0.8 collective-permute-done.5
  77.5 13.4 %all_to_all.26.got = f32[16,16,128]{2,1,0:T(8,128)S(1)} all-to-all(f32[16,16,128]{2,1,0:T(8,128)S(1)} %broadcast_in_dim.29), channel_id=1, replica_groups=mesh['zh'=4,'x'=4,'c'=2,'y'=4,'zl'=2] {'zh','x'}, dimensions={0} | all-to-all | bytes 262144 | tf_op jit(solution)/shard_map/all_to_all | solution.py:227
  90.9 0.4 shard_map.116
  91.3 7.5 %all_to_all.27.got = f32[8,8,128]{2,1,0:T(8,128)S(1)} all-to-all(f32[8,8,128]{2,1,0:T(8,128)S(1)} %get-tuple-element.19), channel_id=1, replica_groups=mesh['zh'=4,'x'=4,'c'=2,'y'=4,'zl'=2] {'y','zl'}, dimensions={0} | all-to-all | bytes 65536 | tf_op jit(solution)/shard_map/all_to_all | solution.py:227
  98.8 1.4 %shard_map.117 = (f32[16,128]{1,0:T(8,128)S(1)}, f32[8,128]{1,0:T(8,128)S(1)}) custom-call(f32[16,512,128]{2,1,0:T(8,128)S(1)} %get-tuple-element.15.weights, f32[16,8,128]{2,1,0:T(8,128)S(1)} %get-tuple-element.18.scale, f32[8,8,128]{2,1,0:T(8,128)S(1)} %all_to_all.27.got, f32[8,128]{1,0:T(8,128)S(1)} %get-tuple-element.20.before), custom_call_target="tpu_custom_call" | custom-call | tf_op jit(solution)/shard_map/pallas_call | solution.py:285
  100.2 3.4 %collective-permute-start.6 = (f32[16,128]{1,0:T(8,128)S(1)}, f32[16,128]{1,0:T(8,128)S(1)}, u32[]{:S(2)}, u32[]{:S(2)}) collective-permute-start(f32[16,128]{1,0:T(8,128)S(1)} %get-tuple-element.23), channel_id=1, source_target_pairs={{0,8},{8,0},{1,9},{9,1},{2,10},{10,2},{3,11},{11,3},{4,12},{12,4},... | collective-permute-start | bytes 24584 | tf_op jit(solution)/shard_map/ppermute | solution.py:223
  103.6 0.8 collective-permute-done.6
  104.4 0.7 broadcast_in_dim.30
  105.1 3.5 %all-to-all-start.4 = ((f32[16,16,128]{2,1,0:T(8,128)}), f32[16,16,128]{2,1,0:T(8,128)S(1)}, u32[]{:S(2)}, u32[]{:S(2)}) async-start(f32[16,16,128]{2,1,0:T(8,128)} %broadcast_in_dim.30), calls=%async_computation.4 | async-start | bytes 262144 | tf_op jit(solution)/shard_map/all_to_all | solution.py:227
  108.6 0.6 slice_bitcast_fusion
  109.2 8.8 %all-to-all-done.4 = f32[16,16,128]{2,1,0:T(8,128)S(1)} async-done(((f32[16,16,128]{2,1,0:T(8,128)}), f32[16,16,128]{2,1,0:T(8,128)S(1)}, u32[]{:S(2)}, u32[]{:S(2)}) %all-to-all-start.4) | async-done | bytes 131104 | tf_op jit(solution)/shard_map/all_to_all | solution.py:227
  118.0 0.6 add_bitcast_fusion
  (21 shorter events, 0.2 us)
Async XLA Ops:
  5.4 6.6 %collective-permute-start = (bf16[1,272,128]{2,1,0:T(8,128)(2,1)S(1)}, bf16[1,272,128]{2,1,0:T(8,128)(2,1)S(1)}, u32[]{:S(2)}, u32[]{:S(2)}) collective-permute-start(bf16[1,272,128]{2,1,0:T(8,128)(2,1)S(1)} %bitcast.15), channel_id=1, source_target_pairs={{0,64},{64,0},{128,192},{192,128},{1,65},{65,1},{129,193},{193,129... | collective-permute-start | bytes 208904 | tf_op jit(solution)/shard_map/ppermute | solution.py:223
  12.0 7.4 %collective-permute-start.1 = (bf16[2,272,128]{2,1,0:T(8,128)(2,1)S(1)}, bf16[2,272,128]{2,1,0:T(8,128)(2,1)S(1)}, u32[]{:S(2)}, u32[]{:S(2)}) collective-permute-start(bf16[2,272,128]{2,1,0:T(8,128)(2,1)S(1)} %pad_maximum_fusion.2), channel_id=1, source_target_pairs={{0,192},{64,128},{128,64},{192,0},{1,193},{65,129},{129,65},{193,1... | collective-permute-start | bytes 417800 | tf_op jit(solution)/shard_map/ppermute | solution.py:223
  19.5 13.3 %collective-permute-start.2 = (bf16[4,272,128]{2,1,0:T(8,128)(2,1)S(1)}, bf16[4,272,128]{2,1,0:T(8,128)(2,1)S(1)}, u32[]{:S(2)}, u32[]{:S(2)}) collective-permute-start(bf16[4,272,128]{2,1,0:T(8,128)(2,1)S(1)} %pad_maximum_fusion.1), channel_id=1, source_target_pairs={{0,16},{16,0},{32,48},{48,32},{1,17},{17,1},{33,49},{49,33},{2,18}... | collective-permute-start | bytes 835592 | tf_op jit(solution)/shard_map/ppermute | solution.py:223
  23.1 26.5 %all-to-all-start = ((bf16[8,272,128]{2,1,0:T(8,128)(2,1)}), bf16[8,272,128]{2,1,0:T(8,128)(2,1)S(1)}, u32[]{:S(2)}, u32[]{:S(2)}) async-start(bf16[8,272,128]{2,1,0:T(8,128)(2,1)} %broadcast_in_dim.28), calls=%async_computation | async-start | bytes 1114112 | tf_op jit(solution)/shard_map/all_to_all | solution.py:227
  32.9 17.0 %copy-start = (bf16[384,384]{1,0:T(8,128)(2,1)S(1)}, bf16[384,384]{1,0:T(8,128)(2,1)}, u32[]{:S(2)}) copy-start(bf16[384,384]{1,0:T(8,128)(2,1)} %near1.3) | copy-start | bytes 884740
  32.9 17.0 %copy-start.1 = (bf16[384,384]{1,0:T(8,128)(2,1)S(1)}, bf16[384,384]{1,0:T(8,128)(2,1)}, u32[]{:S(2)}) copy-start(bf16[384,384]{1,0:T(8,128)(2,1)} %self1.3) | copy-start | bytes 884740
  32.9 17.0 %copy-start.2 = (bf16[384,384]{1,0:T(8,128)(2,1)S(1)}, bf16[384,384]{1,0:T(8,128)(2,1)}, u32[]{:S(2)}) copy-start(bf16[384,384]{1,0:T(8,128)(2,1)} %near2.3) | copy-start | bytes 884740
  32.9 17.0 %copy-start.3 = (bf16[384,384]{1,0:T(8,128)(2,1)S(1)}, bf16[384,384]{1,0:T(8,128)(2,1)}, u32[]{:S(2)}) copy-start(bf16[384,384]{1,0:T(8,128)(2,1)} %self2.3) | copy-start | bytes 884740
  32.9 14.4 %collective-permute-start.3 = (bf16[8,272,128]{2,1,0:T(8,128)(2,1)S(1)}, bf16[8,272,128]{2,1,0:T(8,128)(2,1)S(1)}, u32[]{:S(2)}, u32[]{:S(2)}) collective-permute-start(bf16[8,272,128]{2,1,0:T(8,128)(2,1)S(1)} %pad_maximum_fusion), channel_id=1, source_target_pairs={{0,48},{16,32},{32,16},{48,0},{1,49},{17,33},{33,17},{49,1},{2,50}... | collective-permute-start | bytes 1671176 | tf_op jit(solution)/shard_map/ppermute | solution.py:223
  47.4 5.1 %collective-permute-start.4 = (bf16[16,272,128]{2,1,0:T(8,128)(2,1)S(1)}, bf16[16,272,128]{2,1,0:T(8,128)(2,1)}, u32[]{:S(2)}, u32[]{:S(2)}) collective-permute-start(bf16[16,272,128]{2,1,0:T(8,128)(2,1)S(1)} %constant_dynamic-update-slice_fusion.5.own), channel_id=1, source_target_pairs={{0,8},{8,0},{1,9},{9,1},{2,10},{10,2},{3,11},{11,3},{4,12},{12,4},... | collective-permute-start | bytes 3342344 | tf_op jit(solution)/shard_map/ppermute | solution.py:223
  75.1 2.4 %collective-permute-start.5 = (f32[16,128]{1,0:T(8,128)S(1)}, f32[16,128]{1,0:T(8,128)S(1)}, u32[]{:S(2)}, u32[]{:S(2)}) collective-permute-start(f32[16,128]{1,0:T(8,128)S(1)} %get-tuple-element.17), channel_id=1, source_target_pairs={{0,8},{8,0},{1,9},{9,1},{2,10},{10,2},{3,11},{11,3},{4,12},{12,4},... | collective-permute-start | bytes 24584 | tf_op jit(solution)/shard_map/ppermute | solution.py:223
  100.2 4.2 %collective-permute-start.6 = (f32[16,128]{1,0:T(8,128)S(1)}, f32[16,128]{1,0:T(8,128)S(1)}, u32[]{:S(2)}, u32[]{:S(2)}) collective-permute-start(f32[16,128]{1,0:T(8,128)S(1)} %get-tuple-element.23), channel_id=1, source_target_pairs={{0,8},{8,0},{1,9},{9,1},{2,10},{10,2},{3,11},{11,3},{4,12},{12,4},... | collective-permute-start | bytes 24584 | tf_op jit(solution)/shard_map/ppermute | solution.py:223
  105.1 12.9 %all-to-all-start.4 = ((f32[16,16,128]{2,1,0:T(8,128)}), f32[16,16,128]{2,1,0:T(8,128)S(1)}, u32[]{:S(2)}, u32[]{:S(2)}) async-start(f32[16,16,128]{2,1,0:T(8,128)} %broadcast_in_dim.30), calls=%async_computation.4 | async-start | bytes 262144 | tf_op jit(solution)/shard_map/all_to_all | solution.py:227

commit v2 on v1

--- a/solution.py
+++ b/solution.py
@@ -17,6 +17,7 @@
 ROW_BLOCKS = ROWS // LANES
 COL_BLOCKS = COLS // LANES
 N_TGT = 8
+STEP = 512
 N_PEERS = 16
 LOG_N = math.log(16384.0)
 VMEM_LIMIT = 32 * 1024 * 1024
@@ -25,11 +26,16 @@
 SMEM = functools.partial(pl.BlockSpec, memory_space=pltpu.SMEM)
 
 
-def pack(features, tiles, links):
-    link = jnp.broadcast_to(links[0, 0, 1].astype(jnp.bfloat16), (16, LANES))
-    feats = features[0]
-    pieces = [feats[:, at : at + LANES] for at in range(0, D, LANES)]
-    return jnp.concatenate(pieces + [tiles[0], link], axis=0)[None]
+def pack_kernel(t_links, s_links, t_feats, t_tiles, s_feats, s_tiles, held, packed):
+    def put(ref, at, feats, tiles, link):
+        for piece in range(D // LANES):
+            ref[at, piece * PART : (piece + 1) * PART, :] = feats[0, :, piece * LANES : (piece + 1) * LANES]
+        ref[at, 3 * PART : 4 * PART, :] = tiles[0]
+        ref[at, 4 * PART : PACK, :] = jnp.full((16, LANES), link.astype(jnp.float32)).astype(jnp.bfloat16)
+
+    put(held, 0, t_feats, t_tiles, t_links[0, 0, 1])
+    for d in range(N_TGT):
+        put(packed, d, s_feats, s_tiles, s_links[0, 0, 1])
 
 
 def graph_layers(packed, first, second, near1, self1, near2, self2, x_ref, s_ref, h_ref, emit):
@@ -51,19 +57,17 @@
             total = jnp.dot(panel, both, preferred_element_type=jnp.float32)
             s_ref[k * PART : (k + 1) * PART, :] = total.astype(jnp.bfloat16)
 
-    step = 256
+    def mix(src, at, near, own):
+        left = jnp.concatenate([s_ref[at : at + STEP, :], src[at : at + STEP, :]], axis=1)
+        right = jnp.concatenate([near[...], own[...]], axis=0)
+        return jnp.dot(left, right, preferred_element_type=jnp.float32)
+
     neighbour_sums(x_ref)
-    for at in range(0, count * PART, step):
-        rows = pl.ds(at, step)
-        mixed = jnp.dot(s_ref[rows, :], near1[...], preferred_element_type=jnp.float32)
-        mixed += jnp.dot(x_ref[rows, :], self1[...], preferred_element_type=jnp.float32)
-        h_ref[rows, :] = jnp.maximum(mixed, 0.0).astype(jnp.bfloat16)
+    for at in range(0, count * PART, STEP):
+        h_ref[at : at + STEP, :] = jnp.maximum(mix(x_ref, at, near1, self1), 0.0).astype(jnp.bfloat16)
     neighbour_sums(h_ref)
-    for at in range(0, count * PART, step):
-        rows = pl.ds(at, step)
-        mixed = jnp.dot(s_ref[rows, :], near2[...], preferred_element_type=jnp.float32)
-        mixed += jnp.dot(h_ref[rows, :], self2[...], preferred_element_type=jnp.float32)
-        emit(at, mixed.astype(jnp.bfloat16))
+    for at in range(0, count * PART, STEP):
+        emit(at, mix(h_ref, at, near2, self2).astype(jnp.bfloat16))
 
 
 def source_kernel(links, packed, near1, self1, near2, self2, out, x_ref, s_ref, h_ref):
@@ -96,11 +100,11 @@
 
 
 def target_kernel(
-    links, own, other, near1, self1, near2, self2, emb_source,
+    place, own_links, other_links, own, other, near1, self1, near2, self2, emb_source,
     scores, send,
     x_ref, s_ref, h_ref, e_ref,
 ):
-    me = links[32]
+    me = place[0]
 
     def emit(at, value):
         for piece in range(value.shape[0] // PART):
@@ -110,35 +114,37 @@
     graph_layers(
         lambda k: (own, k) if k < 16 else (other, k - 16),
         lambda k: k ^ SLOT_OF[31],
-        lambda k: links[k],
+        lambda k: slot_of((own_links[k] if k < 16 else other_links[k - 16]) ^ me),
         near1, self1, near2, self2, x_ref, s_ref, h_ref, emit,
     )
 
-    for i in range(COL_BLOCKS // 2):
-        part = lax.dot_general(
-            emb_source[...],
-            e_ref[i * 256 : (i + 1) * 256, :],
-            (((1,), (1,)), ((), ())),
-            preferred_element_type=jnp.float32,
-        )
-        part = 0.2 * part
-        scores[2 * i] = part[:, :LANES]
-        scores[2 * i + 1] = part[:, LANES:]
-
-    for b in range(ROW_BLOCKS):
-        rows = pl.ds(b * LANES, LANES)
-        top = scores[0, rows, :]
-        for i in range(1, COL_BLOCKS):
-            top = jnp.maximum(top, scores[i, rows, :])
+    for at in range(0, ROWS, 256):
+        rows = pl.ds(at, 256)
+        top = None
+        for i in range(COL_BLOCKS // 2):
+            part = lax.dot_general(
+                emb_source[rows, :],
+                e_ref[i * 256 : (i + 1) * 256, :],
+                (((1,), (1,)), ((), ())),
+                preferred_element_type=jnp.float32,
+            )
+            part = 0.2 * part
+            scores[2 * i, rows, :] = part[:, :LANES]
+            scores[2 * i + 1, rows, :] = part[:, LANES:]
+            larger = jnp.maximum(part[:, :LANES], part[:, LANES:])
+            top = larger if top is None else jnp.maximum(top, larger)
         total = jnp.exp(scores[0, rows, :] - top)
         for i in range(1, COL_BLOCKS):
             total += jnp.exp(scores[i, rows, :] - top)
-        top, total = jnp.transpose(top), jnp.transpose(total)
-        larger = jnp.max(top, axis=0, keepdims=True)
-        total = jnp.sum(total * jnp.exp(top - larger), axis=0, keepdims=True)
-        for d in range(N_TGT):
-            send[d, b : b + 1, :] = larger
-            send[d, b + 4 : b + 5, :] = total
+        for half in range(2):
+            b = at // LANES + half
+            part_top = jnp.transpose(top[half * LANES : (half + 1) * LANES])
+            part_total = jnp.transpose(total[half * LANES : (half + 1) * LANES])
+            larger = jnp.max(part_top, axis=0, keepdims=True)
+            part_total = jnp.sum(part_total * jnp.exp(part_top - larger), axis=0, keepdims=True)
+            for d in range(N_TGT):
+                send[d, b : b + 1, :] = larger
+                send[d, b + 4 : b + 5, :] = part_total
 
 
 def column_kernel(scores, got, weights, tops, lse, potential, shift):
@@ -155,17 +161,25 @@
     for b in range(ROW_BLOCKS):
         shift[pl.ds(b * LANES, LANES), :] = spread(source[b : b + 1, :])
 
-    @pl.loop(0, COL_BLOCKS)
-    def _(i):
-        x = (scores[i] + shift[...]).reshape(ROWS // 8, 8, LANES)
-        top = jnp.max(x, axis=0)
-        e = jnp.exp(x - top[None])
-        weights[i] = e.reshape(ROWS, LANES)
-        total = jnp.sum(e, axis=0)
+    step = 64
+    for i in range(COL_BLOCKS):
+        top = None
+        for at in range(0, ROWS, step):
+            rows = pl.ds(at, step)
+            x = scores[i, rows, :] + shift[rows, :]
+            weights[i, rows, :] = x
+            larger = jnp.max(x.reshape(step // 8, 8, LANES), axis=0)
+            top = larger if top is None else jnp.maximum(top, larger)
+        total = jnp.zeros((8, LANES), jnp.float32)
+        for at in range(0, ROWS, step):
+            rows = pl.ds(at, step)
+            e = jnp.exp(weights[i, rows, :].reshape(step // 8, 8, LANES) - top[None])
+            weights[i, rows, :] = e.reshape(step, LANES)
+            total += jnp.sum(e, axis=0)
         tops[i] = top
         larger = jnp.max(top, axis=0, keepdims=True)
         total = jnp.sum(total * jnp.exp(top - larger), axis=0, keepdims=True)
-        lse[pl.ds(i, 1), :] = larger + jnp.log(total)
+        lse[i : i + 1, :] = larger + jnp.log(total)
 
 
 def row_kernel(weights, tops, got, send, potential, scale):
@@ -202,10 +216,14 @@
     for b in range(ROW_BLOCKS):
         factor[pl.ds(b * LANES, LANES), :] = spread(ratio[b : b + 1, :])
 
-    @pl.loop(0, COL_BLOCKS)
-    def _(i):
-        e = (weights[i] * factor[...]).reshape(ROWS // 8, 8, LANES)
-        sums[pl.ds(i, 1), :] = jnp.sum(jnp.sum(e, axis=0) * scale[i], axis=0, keepdims=True)
+    step = 64
+    for i in range(COL_BLOCKS):
+        total = jnp.zeros((8, LANES), jnp.float32)
+        for at in range(0, ROWS, step):
+            rows = pl.ds(at, step)
+            e = weights[i, rows, :] * factor[rows, :]
+            total += jnp.sum(e.reshape(step // 8, 8, LANES), axis=0)
+        sums[i : i + 1, :] = jnp.sum(total * scale[i], axis=0, keepdims=True)
 
 
 def call(kernel, outs, scratch, ins):
@@ -235,13 +253,22 @@
     weights = (near_first, self_first, near_second, self_second)
     me = lax.axis_index(("zh", "x", "c"))
 
-    held = pack(target_feats, target_tiles, target_links)
-    for axis, xor in (("zh", 1), ("zh", 3), ("x", 1), ("x", 3)):
+    held, packed = call(
+        pack_kernel,
+        [((1, PACK, LANES), bf16), ((N_TGT, PACK, LANES), bf16)],
+        [],
+        [SMEM()] * 2 + [VMEM()] * 4,
+    )(target_links, source_links, target_feats, target_tiles, source_feats, source_tiles)
+    for axis, xor in (("zh", 1), ("zh", 3), ("x", 1)):
         held = jnp.concatenate([held, swap(held, axis, 4, xor)], axis=0)
+    held, packed = lax.optimization_barrier((held, packed))
+    held = jnp.concatenate([held, swap(held, "x", 4, 3)], axis=0)
+    packed = exchange(packed, ("y", "zl"))
+    held, packed = lax.optimization_barrier((held, packed))
     other = swap(held, "c", 2, 1)
-
-    packed = pack(source_feats, source_tiles, source_links)
-    packed = exchange(jnp.broadcast_to(packed, (N_TGT, PACK, LANES)), ("y", "zl"))
+    own_links = held[:, 4 * PART, 0].astype(jnp.int32)
+    other_links = swap(own_links, "c", 2, 1)
+
     source_second = packed[:, 4 * PART, 0].astype(jnp.int32)
     (emb_source,) = call(
         source_kernel,
@@ -250,14 +277,12 @@
         [SMEM()] + [VMEM()] * 5,
     )(source_second, packed, *weights)
 
-    target_second = jnp.concatenate([held[:, 4 * PART, 0], other[:, 4 * PART, 0]]).astype(jnp.int32)
-    target_slots = jnp.concatenate([slot_of(target_second ^ me), me[None]])
     scores, send = call(
         target_kernel,
         [((COL_BLOCKS, ROWS, LANES), f32), ((N_TGT, 8, LANES), f32)],
         [pltpu.VMEM((COLS, D), bf16)] * 4,
-        [SMEM()] + [VMEM()] * 7,
-    )(target_slots, held, other, *weights, emb_source)
+        [SMEM()] * 3 + [VMEM()] * 7,
+    )(me[None], own_links, other_links, held, other, *weights, emb_source)
 
     got = exchange(send, ("y", "zl"))
     spread_weights, tops, lse, source_first = call(

time: 120 us -> 121 us (level)
  local copies, waits for them, and re-layouts: 11.8 us -> 5.63 us
  waiting for transfers between devices: 25 us -> 30.5 us
  starting transfers between devices: 32.1 us -> 37 us
  Pallas kernels: 15.6 us -> 13.7 us
    ppermute x7 -> x8, waiting for transfers between devices: 16.1 us -> 21.6 us  [swap(): return lax.ppermute(value, axis, [(i, i ^ xor) for i in range(size)])]
    ppermute x7 -> x8, starting transfers between devices: 18.9 us -> 21.4 us  [swap(): return lax.ppermute(value, axis, [(i, i ^ xor) for i in range(size)])]
    all_to_all x2, starting transfers between devices: 13.2 us -> 15.6 us  [exchange(): return lax.all_to_all(value, axes, 0, 0)]
    slice x4 -> x0, local copies, waits for them, and re-layouts: 2.34 us -> none  [the longest x2 1.17 us: pack(): link = jnp.broadcast_to(links[0, 0, 1].astype(jnp.bfloat16), (16, LANES))]
    unnamed x20, local copies, waits for them, and re-layouts: 5.89 us -> 4.36 us
    pallas_call x0 -> x1, Pallas kernels: none -> 1.43 us  [on_device(): call(pack_kernel, [((1, PACK, LANES), bf16), ((N_TGT, PACK, LANES), bf16)...]
    concatenate x3 -> x0, local copies, waits for them, and re-layouts: 1.38 us -> none  [the longest x2 1.31 us: pack(): return jnp.concatenate(pieces + [tiles[0], link], axis=0)[None]]
    another operation x2 -> x0, other arithmetic: 1.32 us -> none
  transfers between devices with their start and end apart: 9 -> 10, of which waited for: 5 -> 7; matrix products, arithmetic and copies ran while one was open for 6% -> 1% of each run, Pallas kernels for 2% -> 2%
where the time goes in v2:
time: 121 us; the launch traced here: 120 us
  starting transfers between devices  37 us (31%)
  blocking collectives  31 us (26%)
  waiting for transfers between devices  30.5 us (25%)
  Pallas kernels  13.7 us (11%)
  local copies, waits for them, and re-layouts  5.63 us (5%)
  other arithmetic  1.46 us (1%)
    all_to_all x3, blocking collectives, exchange(): return lax.all_to_all(value, axes, 0, 0)  31 us
    ppermute x8, waiting for transfers between devices, swap(): return lax.ppermute(value, axis, [(i, i ^ xor) for i in range(size)])  21.6 us
    ppermute x8, starting transfers between devices, swap(): return lax.ppermute(value, axis, [(i, i ^ xor) for i in range(size)])  21.4 us
    all_to_all x2, starting transfers between devices, exchange(): return lax.all_to_all(value, axes, 0, 0)  15.6 us
    all_to_all x2, waiting for transfers between devices, exchange(): return lax.all_to_all(value, axes, 0, 0)  8.83 us
    pallas_call x1, Pallas kernels, on_device(): call(target_kernel, [((COL_BLOCKS, ROWS, LANES), f32), ((N_TGT, 8, LANES)...  8.2 us
    unnamed x20, local copies, waits for them, and re-layouts  4.36 us
  transfers between devices with their start and end apart: 10, of which 7 were waited for; matrix products, arithmetic and copies ran while one was open for 1% of the time, Pallas kernels for 2%

profile of v2, /device:TPU:1, one launch (start us, length us, event | category | flops | bytes accessed | tf_op | source)
XLA Modules:
  0.0 120.1 jit_solution(2421592547988361779)
XLA Ops:
  0.6 0.8 copy-done.4
  1.4 0.8 copy-done.5
  2.2 0.7 copy-done.6
  3.0 0.7 copy-done.7
  3.7 0.7 copy-done.8
  4.3 0.7 copy-done.9
  5.0 1.4 %shard_map.113 = (bf16[1,272,128]{2,1,0:T(8,128)(2,1)S(1)}, bf16[8,272,128]{2,1,0:T(8,128)(2,1)}) custom-call(s32[1,1,2]{2,1,0:T(1,128)S(1)} %copy-done.8, s32[1,1,2]{2,1,0:T(1,128)S(1)} %copy-done.9, bf16[1,64,384]{2,1,0:T(8,128)(2,1)S(1)} %copy-done.4, bf16[1,64,128]{2,1,0:T(8,128)(2,1)S(1)} %copy-done.6, bf16[1,64,384]{2,1,0:T(8,128)(2,1)S(1)} %copy-done.5, ...), custom_call_target="tpu_custom_call" | custom-call | tf_op jit(solution)/shard_map/pallas_call | solution.py:256
  6.4 3.8 %collective-permute-start = (bf16[1,272,128]{2,1,0:T(8,128)(2,1)S(1)}, bf16[1,272,128]{2,1,0:T(8,128)(2,1)S(1)}, u32[]{:S(2)}, u32[]{:S(2)}) collective-permute-start(bf16[1,272,128]{2,1,0:T(8,128)(2,1)S(1)} %get-tuple-element.19), channel_id=1, source_target_pairs={{0,64},{64,0},{128,192},{192,128},{1,65},{65,1},{129,193},{193,129... | collective-permute-start | bytes 208904 | tf_op jit(solution)/shard_map/ppermute | solution.py:241
  10.2 1.7 %collective-permute-done = bf16[1,272,128]{2,1,0:T(8,128)(2,1)S(1)} collective-permute-done((bf16[1,272,128]{2,1,0:T(8,128)(2,1)S(1)}, bf16[1,272,128]{2,1,0:T(8,128)(2,1)S(1)}, u32[]{:S(2)}, u32[]{:S(2)}) %collective-permute-start) | collective-permute-done | bytes 69664 | tf_op jit(solution)/shard_map/ppermute | solution.py:241
  11.9 5.6 %collective-permute-start.1 = (bf16[2,272,128]{2,1,0:T(8,128)(2,1)S(1)}, bf16[2,272,128]{2,1,0:T(8,128)(2,1)S(1)}, u32[]{:S(2)}, u32[]{:S(2)}) collective-permute-start(bf16[2,272,128]{2,1,0:T(8,128)(2,1)S(1)} %pad_maximum_fusion.3), channel_id=1, source_target_pairs={{0,192},{64,128},{128,64},{192,0},{1,193},{65,129},{129,65},{193,1... | collective-permute-start | bytes 417800 | tf_op jit(solution)/shard_map/ppermute | solution.py:241
  17.5 2.8 %collective-permute-done.1 = bf16[2,272,128]{2,1,0:T(8,128)(2,1)S(1)} collective-permute-done((bf16[2,272,128]{2,1,0:T(8,128)(2,1)S(1)}, bf16[2,272,128]{2,1,0:T(8,128)(2,1)S(1)}, u32[]{:S(2)}, u32[]{:S(2)}) %collective-permute-start.1) | collective-permute-done | bytes 139296 | tf_op jit(solution)/shard_map/ppermute | solution.py:241
  20.4 1.3 %collective-permute-start.2 = (bf16[4,272,128]{2,1,0:T(8,128)(2,1)S(1)}, bf16[4,272,128]{2,1,0:T(8,128)(2,1)S(1)}, u32[]{:S(2)}, u32[]{:S(2)}) collective-permute-start(bf16[4,272,128]{2,1,0:T(8,128)(2,1)S(1)} %pad_maximum_fusion.2), channel_id=1, source_target_pairs={{0,16},{16,0},{32,48},{48,32},{1,17},{17,1},{33,49},{49,33},{2,18}... | collective-permute-start | bytes 835592 | tf_op jit(solution)/shard_map/ppermute | solution.py:241
  21.7 4.2 %collective-permute-done.2 = bf16[4,272,128]{2,1,0:T(8,128)(2,1)S(1)} collective-permute-done((bf16[4,272,128]{2,1,0:T(8,128)(2,1)S(1)}, bf16[4,272,128]{2,1,0:T(8,128)(2,1)S(1)}, u32[]{:S(2)}, u32[]{:S(2)}) %collective-permute-start.2) | collective-permute-done | bytes 278560 | tf_op jit(solution)/shard_map/ppermute | solution.py:241
  25.9 0.1 pad_maximum_fusion.1
  25.9 12.1 %all-to-all-start = ((bf16[8,272,128]{2,1,0:T(8,128)(2,1)}), bf16[8,272,128]{2,1,0:T(8,128)(2,1)S(1)}, u32[]{:S(2)}, u32[]{:S(2)}) async-start(bf16[8,272,128]{2,1,0:T(8,128)(2,1)} %get-tuple-element.22), calls=%async_computation | async-start | bytes 1114112 | tf_op jit(solution)/shard_map/all_to_all | solution.py:245
  38.0 0.0 copy-start.1
  38.0 0.0 copy-start.2
  38.0 0.0 copy-start.3
  38.0 2.6 %collective-permute-start.3 = (bf16[8,272,128]{2,1,0:T(8,128)(2,1)S(1)}, bf16[8,272,128]{2,1,0:T(8,128)(2,1)S(1)}, u32[]{:S(2)}, u32[]{:S(2)}) collective-permute-start(bf16[8,272,128]{2,1,0:T(8,128)(2,1)S(1)} %pad_maximum_fusion.1), channel_id=1, source_target_pairs={{0,48},{16,32},{32,16},{48,0},{1,49},{17,33},{33,17},{49,1},{2,50}... | collective-permute-start | bytes 1671176 | tf_op jit(solution)/shard_map/ppermute | solution.py:241
  40.6 11.2 %collective-permute-done.3 = bf16[8,272,128]{2,1,0:T(8,128)(2,1)S(1)} collective-permute-done((bf16[8,272,128]{2,1,0:T(8,128)(2,1)S(1)}, bf16[8,272,128]{2,1,0:T(8,128)(2,1)S(1)}, u32[]{:S(2)}, u32[]{:S(2)}) %collective-permute-start.3) | collective-permute-done | bytes 557088 | tf_op jit(solution)/shard_map/ppermute | solution.py:241
  51.8 0.1 pad_maximum_fusion.own
  51.9 0.0 all-to-all-done.packed
  52.0 2.6 %collective-permute-start.5 = (bf16[16,272,128]{2,1,0:T(8,128)(2,1)S(1)}, bf16[16,272,128]{2,1,0:T(8,128)(2,1)}, u32[]{:S(2)}, u32[]{:S(2)}) collective-permute-start(bf16[16,272,128]{2,1,0:T(8,128)(2,1)S(1)} %pad_maximum_fusion.own), channel_id=1, source_target_pairs={{0,8},{8,0},{1,9},{9,1},{2,10},{10,2},{3,11},{11,3},{4,12},{12,4},... | collective-permute-start | bytes 3342344 | tf_op jit(solution)/shard_map/ppermute | solution.py:241
  54.6 0.4 convert_reduce_fusion.own_links
  55.0 0.1 collective-permute-start.4
  55.1 0.2 convert_reduce_fusion.1.links
  55.3 0.0 copy-done.1
  55.3 0.0 copy-done.2
  55.3 0.0 copy-done.3
  55.3 2.1 %shard_map.114.emb_source = bf16[512,384]{1,0:T(8,128)(2,1)S(1)} custom-call(s32[8]{0:T(128)S(1)} %convert_reduce_fusion.1.links, bf16[8,272,128]{2,1,0:T(8,128)(2,1)S(1)} %all-to-all-done.packed, bf16[384,384]{1,0:T(8,128)(2,1)S(1)} %copy-done, bf16[384,384]{1,0:T(8,128)(2,1)S(1)} %copy-done.1, bf16[384,384]{1,0:T(8,128)(2,1)S(1)} %copy-done.2, ...), custom_call_target="tpu_custom_call" | custom-call | tf_op jit(solution)/shard_map/pallas_call | solution.py:273
  57.4 0.0 collective-permute-done.4.other_links
  57.4 0.0 collective-permute-done.5.other
  57.5 8.2 %shard_map.115 = (f32[16,512,128]{2,1,0:T(8,128)S(1)}, f32[8,8,128]{2,1,0:T(8,128)S(1)}) custom-call(s32[1]{0:T(128)} %bitcast.place, s32[16]{0:T(128)S(1)} %convert_reduce_fusion.own_links, s32[16]{0:T(128)S(1)} %collective-permute-done.4.other_links, bf16[16,272,128]{2,1,0:T(8,128)(2,1)S(1)} %pad_maximum_fusion.own, ...), custom_call_target="tpu_custom_call" | custom-call | tf_op jit(solution)/shard_map/pallas_call | solution.py:280
  65.7 10.0 %all_to_all.25.got = f32[8,8,128]{2,1,0:T(8,128)S(1)} all-to-all(f32[8,8,128]{2,1,0:T(8,128)S(1)} %get-tuple-element.26), channel_id=1, replica_groups=mesh['zh'=4,'x'=4,'c'=2,'y'=4,'zl'=2] {'y','zl'}, dimensions={0} | all-to-all | bytes 65536 | tf_op jit(solution)/shard_map/all_to_all | solution.py:245
  75.7 1.1 shard_map.116
  76.8 2.0 %collective-permute-start.6 = (f32[16,128]{1,0:T(8,128)S(1)}, f32[16,128]{1,0:T(8,128)S(1)}, u32[]{:S(2)}, u32[]{:S(2)}) collective-permute-start(f32[16,128]{1,0:T(8,128)S(1)} %get-tuple-element.29), channel_id=1, source_target_pairs={{0,8},{8,0},{1,9},{9,1},{2,10},{10,2},{3,11},{11,3},{4,12},{12,4},... | collective-permute-start | bytes 24584 | tf_op jit(solution)/shard_map/ppermute | solution.py:241
  78.8 0.8 collective-permute-done.6
  79.7 13.5 %all_to_all.26.got = f32[16,16,128]{2,1,0:T(8,128)S(1)} all-to-all(f32[16,16,128]{2,1,0:T(8,128)S(1)} %broadcast_in_dim.10), channel_id=1, replica_groups=mesh['zh'=4,'x'=4,'c'=2,'y'=4,'zl'=2] {'zh','x'}, dimensions={0} | all-to-all | bytes 262144 | tf_op jit(solution)/shard_map/all_to_all | solution.py:245
  93.2 0.4 shard_map.117
  93.7 7.5 %all_to_all.27.got = f32[8,8,128]{2,1,0:T(8,128)S(1)} all-to-all(f32[8,8,128]{2,1,0:T(8,128)S(1)} %get-tuple-element.31), channel_id=1, replica_groups=mesh['zh'=4,'x'=4,'c'=2,'y'=4,'zl'=2] {'y','zl'}, dimensions={0} | all-to-all | bytes 65536 | tf_op jit(solution)/shard_map/all_to_all | solution.py:245
  101.1 0.5 shard_map.118
  101.6 3.4 %collective-permute-start.7 = (f32[16,128]{1,0:T(8,128)S(1)}, f32[16,128]{1,0:T(8,128)S(1)}, u32[]{:S(2)}, u32[]{:S(2)}) collective-permute-start(f32[16,128]{1,0:T(8,128)S(1)} %get-tuple-element.35), channel_id=1, source_target_pairs={{0,8},{8,0},{1,9},{9,1},{2,10},{10,2},{3,11},{11,3},{4,12},{12,4},... | collective-permute-start | bytes 24584 | tf_op jit(solution)/shard_map/ppermute | solution.py:241
  105.0 0.8 collective-permute-done.7
  105.8 0.7 broadcast_in_dim.11
  106.5 3.5 %all-to-all-start.4 = ((f32[16,16,128]{2,1,0:T(8,128)}), f32[16,16,128]{2,1,0:T(8,128)S(1)}, u32[]{:S(2)}, u32[]{:S(2)}) async-start(f32[16,16,128]{2,1,0:T(8,128)} %broadcast_in_dim.11), calls=%async_computation.4 | async-start | bytes 262144 | tf_op jit(solution)/shard_map/all_to_all | solution.py:245
  110.0 0.6 slice_bitcast_fusion
  110.6 8.8 %all-to-all-done.4 = f32[16,16,128]{2,1,0:T(8,128)S(1)} async-done(((f32[16,16,128]{2,1,0:T(8,128)}), f32[16,16,128]{2,1,0:T(8,128)S(1)}, u32[]{:S(2)}, u32[]{:S(2)}) %all-to-all-start.4) | async-done | bytes 131104 | tf_op jit(solution)/shard_map/all_to_all | solution.py:245
  119.5 0.6 add_bitcast_fusion
  (14 shorter events, 0.1 us)
Async XLA Ops:
  0.6 0.8 copy-start.4
  1.4 0.8 copy-start.5
  2.2 0.7 copy-start.6
  2.9 0.7 copy-start.7
  3.7 0.7 copy-start.8
  4.3 0.7 copy-start.9
  6.4 5.5 %collective-permute-start = (bf16[1,272,128]{2,1,0:T(8,128)(2,1)S(1)}, bf16[1,272,128]{2,1,0:T(8,128)(2,1)S(1)}, u32[]{:S(2)}, u32[]{:S(2)}) collective-permute-start(bf16[1,272,128]{2,1,0:T(8,128)(2,1)S(1)} %get-tuple-element.19), channel_id=1, source_target_pairs={{0,64},{64,0},{128,192},{192,128},{1,65},{65,1},{129,193},{193,129... | collective-permute-start | bytes 208904 | tf_op jit(solution)/shard_map/ppermute | solution.py:241
  11.9 8.4 %collective-permute-start.1 = (bf16[2,272,128]{2,1,0:T(8,128)(2,1)S(1)}, bf16[2,272,128]{2,1,0:T(8,128)(2,1)S(1)}, u32[]{:S(2)}, u32[]{:S(2)}) collective-permute-start(bf16[2,272,128]{2,1,0:T(8,128)(2,1)S(1)} %pad_maximum_fusion.3), channel_id=1, source_target_pairs={{0,192},{64,128},{128,64},{192,0},{1,193},{65,129},{129,65},{193,1... | collective-permute-start | bytes 417800 | tf_op jit(solution)/shard_map/ppermute | solution.py:241
  20.4 5.5 %collective-permute-start.2 = (bf16[4,272,128]{2,1,0:T(8,128)(2,1)S(1)}, bf16[4,272,128]{2,1,0:T(8,128)(2,1)S(1)}, u32[]{:S(2)}, u32[]{:S(2)}) collective-permute-start(bf16[4,272,128]{2,1,0:T(8,128)(2,1)S(1)} %pad_maximum_fusion.2), channel_id=1, source_target_pairs={{0,16},{16,0},{32,48},{48,32},{1,17},{17,1},{33,49},{49,33},{2,18}... | collective-permute-start | bytes 835592 | tf_op jit(solution)/shard_map/ppermute | solution.py:241
  25.9 26.0 %all-to-all-start = ((bf16[8,272,128]{2,1,0:T(8,128)(2,1)}), bf16[8,272,128]{2,1,0:T(8,128)(2,1)S(1)}, u32[]{:S(2)}, u32[]{:S(2)}) async-start(bf16[8,272,128]{2,1,0:T(8,128)(2,1)} %get-tuple-element.22), calls=%async_computation | async-start | bytes 1114112 | tf_op jit(solution)/shard_map/all_to_all | solution.py:245
  38.0 17.3 %copy-start = (bf16[384,384]{1,0:T(8,128)(2,1)S(1)}, bf16[384,384]{1,0:T(8,128)(2,1)}, u32[]{:S(2)}) copy-start(bf16[384,384]{1,0:T(8,128)(2,1)} %near1.3) | copy-start | bytes 884740
  38.0 17.3 %copy-start.1 = (bf16[384,384]{1,0:T(8,128)(2,1)S(1)}, bf16[384,384]{1,0:T(8,128)(2,1)}, u32[]{:S(2)}) copy-start(bf16[384,384]{1,0:T(8,128)(2,1)} %self1.3) | copy-start | bytes 884740
  38.0 17.3 %copy-start.2 = (bf16[384,384]{1,0:T(8,128)(2,1)S(1)}, bf16[384,384]{1,0:T(8,128)(2,1)}, u32[]{:S(2)}) copy-start(bf16[384,384]{1,0:T(8,128)(2,1)} %near2.3) | copy-start | bytes 884740
  38.0 17.3 %copy-start.3 = (bf16[384,384]{1,0:T(8,128)(2,1)S(1)}, bf16[384,384]{1,0:T(8,128)(2,1)}, u32[]{:S(2)}) copy-start(bf16[384,384]{1,0:T(8,128)(2,1)} %self2.3) | copy-start | bytes 884740
  38.0 13.8 %collective-permute-start.3 = (bf16[8,272,128]{2,1,0:T(8,128)(2,1)S(1)}, bf16[8,272,128]{2,1,0:T(8,128)(2,1)S(1)}, u32[]{:S(2)}, u32[]{:S(2)}) collective-permute-start(bf16[8,272,128]{2,1,0:T(8,128)(2,1)S(1)} %pad_maximum_fusion.1), channel_id=1, source_target_pairs={{0,48},{16,32},{32,16},{48,0},{1,49},{17,33},{33,17},{49,1},{2,50}... | collective-permute-start | bytes 1671176 | tf_op jit(solution)/shard_map/ppermute | solution.py:241
  52.0 5.5 %collective-permute-start.5 = (bf16[16,272,128]{2,1,0:T(8,128)(2,1)S(1)}, bf16[16,272,128]{2,1,0:T(8,128)(2,1)}, u32[]{:S(2)}, u32[]{:S(2)}) collective-permute-start(bf16[16,272,128]{2,1,0:T(8,128)(2,1)S(1)} %pad_maximum_fusion.own), channel_id=1, source_target_pairs={{0,8},{8,0},{1,9},{9,1},{2,10},{10,2},{3,11},{11,3},{4,12},{12,4},... | collective-permute-start | bytes 3342344 | tf_op jit(solution)/shard_map/ppermute | solution.py:241
  55.0 2.5 %collective-permute-start.4 = (s32[16]{0:T(128)S(1)}, s32[16]{0:T(128)S(1)}, u32[]{:S(2)}, u32[]{:S(2)}) collective-permute-start(s32[16]{0:T(128)S(1)} %convert_reduce_fusion.own_links), channel_id=1, source_target_pairs={{0,8},{8,0},{1,9},{9,1},{2,10},{10,2},{3,11},{11,3},{4,12},{12,4},... | collective-permute-start | bytes 200 | tf_op jit(solution)/shard_map/ppermute | solution.py:241
  76.8 2.8 %collective-permute-start.6 = (f32[16,128]{1,0:T(8,128)S(1)}, f32[16,128]{1,0:T(8,128)S(1)}, u32[]{:S(2)}, u32[]{:S(2)}) collective-permute-start(f32[16,128]{1,0:T(8,128)S(1)} %get-tuple-element.29), channel_id=1, source_target_pairs={{0,8},{8,0},{1,9},{9,1},{2,10},{10,2},{3,11},{11,3},{4,12},{12,4},... | collective-permute-start | bytes 24584 | tf_op jit(solution)/shard_map/ppermute | solution.py:241
  101.6 4.2 %collective-permute-start.7 = (f32[16,128]{1,0:T(8,128)S(1)}, f32[16,128]{1,0:T(8,128)S(1)}, u32[]{:S(2)}, u32[]{:S(2)}) collective-permute-start(f32[16,128]{1,0:T(8,128)S(1)} %get-tuple-element.35), channel_id=1, source_target_pairs={{0,8},{8,0},{1,9},{9,1},{2,10},{10,2},{3,11},{11,3},{4,12},{12,4},... | collective-permute-start | bytes 24584 | tf_op jit(solution)/shard_map/ppermute | solution.py:241
  106.5 12.9 %all-to-all-start.4 = ((f32[16,16,128]{2,1,0:T(8,128)}), f32[16,16,128]{2,1,0:T(8,128)S(1)}, u32[]{:S(2)}, u32[]{:S(2)}) async-start(f32[16,16,128]{2,1,0:T(8,128)} %broadcast_in_dim.11), calls=%async_computation.4 | async-start | bytes 262144 | tf_op jit(solution)/shard_map/all_to_all | solution.py:245

commit v3 on v2

--- a/solution.py
+++ b/solution.py
@@ -21,21 +21,37 @@
 N_PEERS = 16
 LOG_N = math.log(16384.0)
 VMEM_LIMIT = 32 * 1024 * 1024
+PACK_LIMIT = 60 * 1024 * 1024
 
 VMEM = functools.partial(pl.BlockSpec, memory_space=pltpu.VMEM)
+HBM = functools.partial(pl.BlockSpec, memory_space=pltpu.HBM)
 SMEM = functools.partial(pl.BlockSpec, memory_space=pltpu.SMEM)
 
 
-def pack_kernel(t_links, s_links, t_feats, t_tiles, s_feats, s_tiles, held, packed):
-    def put(ref, at, feats, tiles, link):
+def pack_kernel(feats, tiles, links, out, feats_ref, tiles_ref, links_ref, sems):
+    pairs = ((feats, feats_ref), (tiles, tiles_ref), (links, links_ref))
+    copies = [pltpu.make_async_copy(src, dst, sems.at[i]) for i, (src, dst) in enumerate(pairs)]
+    for copy in copies:
+        copy.start()
+    for copy in copies:
+        copy.wait()
+    link = jnp.broadcast_to(links_ref[0, 0:1, 1:2].astype(jnp.float32), (16, LANES)).astype(jnp.bfloat16)
+    for d in range(out.shape[0]):
         for piece in range(D // LANES):
-            ref[at, piece * PART : (piece + 1) * PART, :] = feats[0, :, piece * LANES : (piece + 1) * LANES]
-        ref[at, 3 * PART : 4 * PART, :] = tiles[0]
-        ref[at, 4 * PART : PACK, :] = jnp.full((16, LANES), link.astype(jnp.float32)).astype(jnp.bfloat16)
-
-    put(held, 0, t_feats, t_tiles, t_links[0, 0, 1])
-    for d in range(N_TGT):
-        put(packed, d, s_feats, s_tiles, s_links[0, 0, 1])
+            out[d, piece * PART : (piece + 1) * PART, :] = feats_ref[0, :, piece * LANES : (piece + 1) * LANES]
+        out[d, 3 * PART : 4 * PART, :] = tiles_ref[0]
+        out[d, 4 * PART : PACK, :] = link
+
+
+def pack(feats, tiles, links, count):
+    (packed,) = call(
+        pack_kernel,
+        [((count, PACK, LANES), jnp.bfloat16)],
+        [pltpu.VMEM(v.shape, v.dtype) for v in (feats, tiles, links)] + [pltpu.SemaphoreType.DMA((3,))],
+        [HBM()] * 3,
+        limit=PACK_LIMIT,
+    )(feats, tiles, links)
+    return packed
 
 
 def graph_layers(packed, first, second, near1, self1, near2, self2, x_ref, s_ref, h_ref, emit):
@@ -83,16 +99,11 @@
 
 
 def slot_xor(k):
-    b0, b1, b2, b3, b4 = ((k >> bit) & 1 for bit in range(5))
-    return ((b0 ^ (3 * b1)) << 3) | ((b2 ^ (3 * b3)) << 1) | b4
-
-
-SLOT_OF = {slot_xor(k): k for k in range(32)}
+    return ((k & 3) << 3) | (((k >> 2) & 3) << 1) | (k >> 4)
 
 
 def slot_of(v):
-    z1, z0, x1, x0, c = ((v >> bit) & 1 for bit in (4, 3, 2, 1, 0))
-    return (z0 ^ z1) | (z1 << 1) | ((x0 ^ x1) << 2) | (x1 << 3) | (c << 4)
+    return (v >> 3) | (((v >> 1) & 3) << 2) | ((v & 1) << 4)
 
 
 def spread(row):
@@ -100,11 +111,14 @@
 
 
 def target_kernel(
-    place, own_links, other_links, own, other, near1, self1, near2, self2, emb_source,
+    place, own_links, other_links,
+    own0, own1, own2, own3, other0, other1, other2, other3,
+    near1, self1, near2, self2, emb_source,
     scores, send,
     x_ref, s_ref, h_ref, e_ref,
 ):
     me = place[0]
+    pieces = (own0, own1, own2, own3, other0, other1, other2, other3)
 
     def emit(at, value):
         for piece in range(value.shape[0] // PART):
@@ -112,8 +126,8 @@
             e_ref[pl.ds(pl.multiple_of(q * PART, PART), PART), :] = value[piece * PART : (piece + 1) * PART, :]
 
     graph_layers(
-        lambda k: (own, k) if k < 16 else (other, k - 16),
-        lambda k: k ^ SLOT_OF[31],
+        lambda k: (pieces[k // 4], k % 4),
+        lambda k: k ^ 31,
         lambda k: slot_of((own_links[k] if k < 16 else other_links[k - 16]) ^ me),
         near1, self1, near2, self2, x_ref, s_ref, h_ref, emit,
     )
@@ -226,14 +240,15 @@
         sums[i : i + 1, :] = jnp.sum(total * scale[i], axis=0, keepdims=True)
 
 
-def call(kernel, outs, scratch, ins):
+def call(kernel, outs, scratch, ins, cost=None, limit=VMEM_LIMIT):
     return pl.pallas_call(
         kernel,
         out_shape=[jax.ShapeDtypeStruct(shape, dtype) for shape, dtype in outs],
         in_specs=ins,
         out_specs=[VMEM() for _ in outs],
         scratch_shapes=scratch,
-        compiler_params=pltpu.CompilerParams(vmem_limit_bytes=VMEM_LIMIT),
+        cost_estimate=cost,
+        compiler_params=pltpu.CompilerParams(vmem_limit_bytes=limit),
     )
 
 
@@ -253,20 +268,15 @@
     weights = (near_first, self_first, near_second, self_second)
     me = lax.axis_index(("zh", "x", "c"))
 
-    held, packed = call(
-        pack_kernel,
-        [((1, PACK, LANES), bf16), ((N_TGT, PACK, LANES), bf16)],
-        [],
-        [SMEM()] * 2 + [VMEM()] * 4,
-    )(target_links, source_links, target_feats, target_tiles, source_feats, source_tiles)
-    for axis, xor in (("zh", 1), ("zh", 3), ("x", 1)):
-        held = jnp.concatenate([held, swap(held, axis, 4, xor)], axis=0)
-    held, packed = lax.optimization_barrier((held, packed))
-    held = jnp.concatenate([held, swap(held, "x", 4, 3)], axis=0)
+    held = pack(target_feats, target_tiles, target_links, 1)
+    packed = pack(source_feats, source_tiles, source_links, N_TGT)
+    near, far, beyond = (swap(held, "zh", 4, xor) for xor in (1, 2, 3))
+    near, packed = lax.optimization_barrier((near, packed))
     packed = exchange(packed, ("y", "zl"))
-    held, packed = lax.optimization_barrier((held, packed))
-    other = swap(held, "c", 2, 1)
-    own_links = held[:, 4 * PART, 0].astype(jnp.int32)
+    held = jnp.concatenate([held, near, far, beyond], axis=0)
+    own = [held] + [swap(held, "x", 4, xor) for xor in (1, 2, 3)]
+    other = [swap(piece, "c", 2, 1) for piece in own]
+    own_links = jnp.concatenate([piece[:, 4 * PART, 0] for piece in own]).astype(jnp.int32)
     other_links = swap(own_links, "c", 2, 1)
 
     source_second = packed[:, 4 * PART, 0].astype(jnp.int32)
@@ -275,14 +285,15 @@
         [((ROWS, D), bf16)],
         [pltpu.VMEM((ROWS, D), bf16)] * 3,
         [SMEM()] + [VMEM()] * 5,
+        pl.CostEstimate(flops=700_000_000, bytes_accessed=2_000_000, transcendentals=0),
     )(source_second, packed, *weights)
 
     scores, send = call(
         target_kernel,
         [((COL_BLOCKS, ROWS, LANES), f32), ((N_TGT, 8, LANES), f32)],
         [pltpu.VMEM((COLS, D), bf16)] * 4,
-        [SMEM()] * 3 + [VMEM()] * 7,
-    )(me[None], own_links, other_links, held, other, *weights, emb_source)
+        [SMEM()] * 3 + [VMEM()] * 13,
+    )(me[None], own_links, other_links, *own, *other, *weights, emb_source)
 
     got = exchange(send, ("y", "zl"))
     spread_weights, tops, lse, source_first = call(

time: 121 us -> 119 us (0.983)
  waiting for transfers between devices: 30.5 us -> 26 us
  blocking collectives: 31 us -> 33.4 us
  Pallas kernels: 13.7 us -> 15.1 us
  starting transfers between devices: 37 us -> 35.6 us
    all_to_all x2, starting transfers between devices: 15.6 us -> 9.95 us  [exchange(): return lax.all_to_all(value, axes, 0, 0)]
    ppermute x8 -> x13, waiting for transfers between devices: 21.6 us -> 17.1 us  [swap(): return lax.ppermute(value, axis, [(i, i ^ xor) for i in range(size)])]
    ppermute x8 -> x13, starting transfers between devices: 21.4 us -> 25.6 us  [swap(): return lax.ppermute(value, axis, [(i, i ^ xor) for i in range(size)])]
    all_to_all x3, blocking collectives: 31 us -> 33.4 us  [exchange(): return lax.all_to_all(value, axes, 0, 0)]
    pallas_call x1 -> x2, Pallas kernels: 1.43 us -> 3.31 us  [pack(): call(pack_kernel, [((count, PACK, LANES), jnp.bfloat16)], [pltpu.VMEM(v.s...]
    unnamed x20 -> x14, local copies, waits for them, and re-layouts: 4.36 us -> 3.87 us
  transfers between devices with their start and end apart: 10 -> 15, of which waited for: 7 -> 7; matrix products, arithmetic and copies ran while one was open for 1% -> 2% of each run, Pallas kernels for 2% -> 3%
where the time goes in v3:
time: 119 us; the launch traced here: 118 us
  starting transfers between devices  35.6 us (30%)
  blocking collectives  33.4 us (28%)
  waiting for transfers between devices  26 us (22%)
  Pallas kernels  15.1 us (13%)
  local copies, waits for them, and re-layouts  5.58 us (5%)
  other arithmetic  1.88 us (2%)
    all_to_all x3, blocking collectives, exchange(): return lax.all_to_all(value, axes, 0, 0)  33.4 us
    ppermute x13, starting transfers between devices, swap(): return lax.ppermute(value, axis, [(i, i ^ xor) for i in range(size)])  25.6 us
    ppermute x13, waiting for transfers between devices, swap(): return lax.ppermute(value, axis, [(i, i ^ xor) for i in range(size)])  17.1 us
    all_to_all x2, starting transfers between devices, exchange(): return lax.all_to_all(value, axes, 0, 0)  9.95 us
    all_to_all x2, waiting for transfers between devices, exchange(): return lax.all_to_all(value, axes, 0, 0)  8.83 us
    pallas_call x1, Pallas kernels, on_device(): call(target_kernel, [((COL_BLOCKS, ROWS, LANES), f32), ((N_TGT, 8, LANES)...  7.81 us
    unnamed x14, local copies, waits for them, and re-layouts  3.87 us
    pallas_call x2, Pallas kernels, pack(): call(pack_kernel, [((count, PACK, LANES), jnp.bfloat16)], [pltpu.VMEM(v.s...  3.31 us
  transfers between devices with their start and end apart: 15, of which 7 were waited for; matrix products, arithmetic and copies ran while one was open for 2% of the time, Pallas kernels for 3%

profile of v3, /device:TPU:1, one launch (start us, length us, event | category | flops | bytes accessed | tf_op | source)
XLA Modules:
  0.0 118.3 jit_solution(16934199165265673736)
XLA Ops:
  0.6 0.0 copy-start.5
  0.6 0.0 copy-start.3
  0.7 0.0 copy-start.1
  0.7 1.6 %shard_map.113 = bf16[1,272,128]{2,1,0:T(8,128)(2,1)} custom-call(bf16[1,64,384]{2,1,0:T(8,128)(2,1)} %feats.2, bf16[1,64,128]{2,1,0:T(8,128)(2,1)} %tiles.2, s32[1,1,2]{2,1,0:T(1,128)} %links.2), custom_call_target="tpu_custom_call" | custom-call | tf_op jit(solution)/shard_map/pallas_call | solution.py:47
  2.3 3.9 %collective-permute-start = (bf16[1,272,128]{2,1,0:T(8,128)(2,1)}, bf16[1,272,128]{2,1,0:T(8,128)(2,1)S(1)}, u32[]{:S(2)}, u32[]{:S(2)}) collective-permute-start(bf16[1,272,128]{2,1,0:T(8,128)(2,1)} %shard_map.113), channel_id=1, source_target_pairs={{0,64},{64,0},{128,192},{192,128},{1,65},{65,1},{129,193},{193,129... | collective-permute-start | bytes 208904 | tf_op jit(solution)/shard_map/ppermute | solution.py:256
  6.2 1.7 %shard_map.114 = bf16[8,272,128]{2,1,0:T(8,128)(2,1)} custom-call(bf16[1,64,384]{2,1,0:T(8,128)(2,1)} %feats.3, bf16[1,64,128]{2,1,0:T(8,128)(2,1)} %tiles.3, s32[1,1,2]{2,1,0:T(1,128)} %links.3), custom_call_target="tpu_custom_call" | custom-call | tf_op jit(solution)/shard_map/pallas_call | solution.py:47
  7.9 0.2 collective-permute-done
  8.1 6.4 %all-to-all-start = ((bf16[8,272,128]{2,1,0:T(8,128)(2,1)}), bf16[8,272,128]{2,1,0:T(8,128)(2,1)S(1)}, u32[]{:S(2)}, u32[]{:S(2)}) async-start(bf16[8,272,128]{2,1,0:T(8,128)(2,1)} %shard_map.114), calls=%async_computation | async-start | bytes 1114112 | tf_op jit(solution)/shard_map/all_to_all | solution.py:260
  14.5 5.6 %collective-permute-start.2 = (bf16[1,272,128]{2,1,0:T(8,128)(2,1)}, bf16[1,272,128]{2,1,0:T(8,128)(2,1)S(1)}, u32[]{:S(2)}, u32[]{:S(2)}) collective-permute-start(bf16[1,272,128]{2,1,0:T(8,128)(2,1)} %shard_map.113), channel_id=1, source_target_pairs={{0,192},{64,128},{128,64},{192,0},{1,193},{65,129},{129,65},{193,1... | collective-permute-start | bytes 208904 | tf_op jit(solution)/shard_map/ppermute | solution.py:256
  20.1 0.9 collective-permute-start.1
  21.0 6.5 %collective-permute-done.2 = bf16[1,272,128]{2,1,0:T(8,128)(2,1)S(1)} collective-permute-done((bf16[1,272,128]{2,1,0:T(8,128)(2,1)}, bf16[1,272,128]{2,1,0:T(8,128)(2,1)S(1)}, u32[]{:S(2)}, u32[]{:S(2)}) %collective-permute-start.2) | collective-permute-done | bytes 69664 | tf_op jit(solution)/shard_map/ppermute | solution.py:256
  27.5 1.7 %collective-permute-done.1 = bf16[1,272,128]{2,1,0:T(8,128)(2,1)S(1)} collective-permute-done((bf16[1,272,128]{2,1,0:T(8,128)(2,1)}, bf16[1,272,128]{2,1,0:T(8,128)(2,1)S(1)}, u32[]{:S(2)}, u32[]{:S(2)}) %collective-permute-start.1) | collective-permute-done | bytes 69664 | tf_op jit(solution)/shard_map/ppermute | solution.py:256
  29.1 0.9 pad_maximum_fusion.own0
  30.0 2.6 %collective-permute-start.5 = (bf16[4,272,128]{2,1,0:T(8,128)(2,1)S(1)}, bf16[4,272,128]{2,1,0:T(8,128)(2,1)S(1)}, u32[]{:S(2)}, u32[]{:S(2)}) collective-permute-start(bf16[4,272,128]{2,1,0:T(8,128)(2,1)S(1)} %pad_maximum_fusion.own0), channel_id=1, source_target_pairs={{0,48},{16,32},{32,16},{48,0},{1,49},{17,33},{33,17},{49,1},{2,50}... | collective-permute-start | bytes 835592 | tf_op jit(solution)/shard_map/ppermute | solution.py:256
  32.6 0.5 collective-permute-start.4
  33.1 0.3 collective-permute-start.3
  33.4 3.8 %collective-permute-start.7 = (bf16[4,272,128]{2,1,0:T(8,128)(2,1)S(1)}, bf16[4,272,128]{2,1,0:T(8,128)(2,1)S(1)}, u32[]{:S(2)}, u32[]{:S(2)}) collective-permute-start(bf16[4,272,128]{2,1,0:T(8,128)(2,1)S(1)} %pad_maximum_fusion.own0), channel_id=1, source_target_pairs={{0,8},{8,0},{1,9},{9,1},{2,10},{10,2},{3,11},{11,3},{4,12},{12,4},... | collective-permute-start | bytes 835592 | tf_op jit(solution)/shard_map/ppermute | solution.py:256
  37.2 0.1 slice_reduce_fusion.3
  37.3 7.1 %collective-permute-done.5.own3 = bf16[4,272,128]{2,1,0:T(8,128)(2,1)S(1)} collective-permute-done((bf16[4,272,128]{2,1,0:T(8,128)(2,1)S(1)}, bf16[4,272,128]{2,1,0:T(8,128)(2,1)S(1)}, u32[]{:S(2)}, u32[]{:S(2)}) %collective-permute-start.5) | collective-permute-done | bytes 278560 | tf_op jit(solution)/shard_map/ppermute | solution.py:256
  44.4 2.0 %collective-permute-start.10 = (bf16[4,272,128]{2,1,0:T(8,128)(2,1)S(1)}, bf16[4,272,128]{2,1,0:T(8,128)(2,1)S(1)}, u32[]{:S(2)}, u32[]{:S(2)}) collective-permute-start(bf16[4,272,128]{2,1,0:T(8,128)(2,1)S(1)} %collective-permute-done.5.own3), channel_id=1, source_target_pairs={{0,8},{8,0},{1,9},{9,1},{2,10},{10,2},{3,11},{11,3},{4,12},{12,4},... | collective-permute-start | bytes 835592 | tf_op jit(solution)/shard_map/ppermute | solution.py:256
  46.4 0.6 collective-permute-start.8
  47.0 0.1 slice_reduce_fusion
  47.1 0.1 slice_reduce_fusion.1
  47.2 0.1 slice_reduce_fusion.2
  47.4 0.1 maximum_convert_fusion.own_links
  47.4 0.2 collective-permute-start.6
  47.7 0.2 fusion.links
  47.9 1.0 copy-done
  48.9 1.0 copy-done.2
  49.8 1.0 copy-done.4
  50.8 1.0 copy-done.6
  51.8 2.1 %shard_map.115.emb_source = bf16[512,384]{1,0:T(8,128)(2,1)S(1)} custom-call(s32[8]{0:T(128)S(1)} %fusion.links, bf16[8,272,128]{2,1,0:T(8,128)(2,1)S(1)} %all-to-all-done.packed, bf16[384,384]{1,0:T(8,128)(2,1)S(1)} %copy-done, bf16[384,384]{1,0:T(8,128)(2,1)S(1)} %copy-done.2, bf16[384,384]{1,0:T(8,128)(2,1)S(1)} %copy-done.4, bf16[384,384]{1,0:T(8,128)(2,1)S(1)} %copy-done.6), custom_call_target="tpu_custom_call" | custom-call | flops 700000000 | bytes 2000000 | tf_op jit(solution)/shard_map/pallas_call | solution.py:283
  53.9 7.8 %shard_map.116 = (f32[16,512,128]{2,1,0:T(8,128)S(1)}, f32[8,8,128]{2,1,0:T(8,128)S(1)}) custom-call(s32[1]{0:T(128)} %bitcast.place, s32[16]{0:T(128)S(1)} %maximum_convert_fusion.own_links, s32[16]{0:T(128)S(1)} %collective-permute-done.6.other_links, bf16[4,272,128]{2,1,0:T(8,128)(2,1)S(1)} %pad_maximum_fusion.own0, ...), custom_call_target="tpu_custom_call" | custom-call | tf_op jit(solution)/shard_map/pallas_call | solution.py:291
  61.8 9.8 %all_to_all.25.got = f32[8,8,128]{2,1,0:T(8,128)S(1)} all-to-all(f32[8,8,128]{2,1,0:T(8,128)S(1)} %get-tuple-element.18), channel_id=1, replica_groups=mesh['zh'=4,'x'=4,'c'=2,'y'=4,'zl'=2] {'y','zl'}, dimensions={0} | all-to-all | bytes 65536 | tf_op jit(solution)/shard_map/all_to_all | solution.py:260
  71.6 1.0 shard_map.117
  72.6 2.0 %collective-permute-start.11 = (f32[16,128]{1,0:T(8,128)S(1)}, f32[16,128]{1,0:T(8,128)S(1)}, u32[]{:S(2)}, u32[]{:S(2)}) collective-permute-start(f32[16,128]{1,0:T(8,128)S(1)} %get-tuple-element.21), channel_id=1, source_target_pairs={{0,8},{8,0},{1,9},{9,1},{2,10},{10,2},{3,11},{11,3},{4,12},{12,4},... | collective-permute-start | bytes 24584 | tf_op jit(solution)/shard_map/ppermute | solution.py:256
  74.6 0.8 collective-permute-done.11
  75.5 16.1 %all_to_all.26.got = f32[16,16,128]{2,1,0:T(8,128)S(1)} all-to-all(f32[16,16,128]{2,1,0:T(8,128)S(1)} %broadcast_in_dim.10), channel_id=1, replica_groups=mesh['zh'=4,'x'=4,'c'=2,'y'=4,'zl'=2] {'zh','x'}, dimensions={0} | all-to-all | bytes 262144 | tf_op jit(solution)/shard_map/all_to_all | solution.py:260
  91.6 0.4 shard_map.118
  92.0 7.5 %all_to_all.27.got = f32[8,8,128]{2,1,0:T(8,128)S(1)} all-to-all(f32[8,8,128]{2,1,0:T(8,128)S(1)} %get-tuple-element.23), channel_id=1, replica_groups=mesh['zh'=4,'x'=4,'c'=2,'y'=4,'zl'=2] {'y','zl'}, dimensions={0} | all-to-all | bytes 65536 | tf_op jit(solution)/shard_map/all_to_all | solution.py:260
  99.5 0.5 shard_map.119
  99.9 3.4 %collective-permute-start.12 = (f32[16,128]{1,0:T(8,128)S(1)}, f32[16,128]{1,0:T(8,128)S(1)}, u32[]{:S(2)}, u32[]{:S(2)}) collective-permute-start(f32[16,128]{1,0:T(8,128)S(1)} %get-tuple-element.27), channel_id=1, source_target_pairs={{0,8},{8,0},{1,9},{9,1},{2,10},{10,2},{3,11},{11,3},{4,12},{12,4},... | collective-permute-start | bytes 24584 | tf_op jit(solution)/shard_map/ppermute | solution.py:256
  103.3 0.8 collective-permute-done.12
  104.1 0.7 broadcast_in_dim.11
  104.8 3.5 %all-to-all-start.4 = ((f32[16,16,128]{2,1,0:T(8,128)}), f32[16,16,128]{2,1,0:T(8,128)S(1)}, u32[]{:S(2)}, u32[]{:S(2)}) async-start(f32[16,16,128]{2,1,0:T(8,128)} %broadcast_in_dim.11), calls=%async_computation.4 | async-start | bytes 262144 | tf_op jit(solution)/shard_map/all_to_all | solution.py:260
  108.3 0.6 slice_bitcast_fusion
  108.9 8.8 %all-to-all-done.4 = f32[16,16,128]{2,1,0:T(8,128)S(1)} async-done(((f32[16,16,128]{2,1,0:T(8,128)}), f32[16,16,128]{2,1,0:T(8,128)S(1)}, u32[]{:S(2)}, u32[]{:S(2)}) %all-to-all-start.4) | async-done | bytes 131104 | tf_op jit(solution)/shard_map/all_to_all | solution.py:260
  117.7 0.6 add_bitcast_fusion
  (20 shorter events, 0.1 us)
Async XLA Ops:
  0.6 53.3 %copy-start.5 = (bf16[384,384]{1,0:T(8,128)(2,1)S(1)}, bf16[384,384]{1,0:T(8,128)(2,1)}, u32[]{:S(2)}) copy-start(bf16[384,384]{1,0:T(8,128)(2,1)} %near2.3) | copy-start | bytes 884740
  0.6 53.3 %copy-start.3 = (bf16[384,384]{1,0:T(8,128)(2,1)S(1)}, bf16[384,384]{1,0:T(8,128)(2,1)}, u32[]{:S(2)}) copy-start(bf16[384,384]{1,0:T(8,128)(2,1)} %self1.3) | copy-start | bytes 884740
  0.7 53.3 %copy-start.1 = (bf16[384,384]{1,0:T(8,128)(2,1)S(1)}, bf16[384,384]{1,0:T(8,128)(2,1)}, u32[]{:S(2)}) copy-start(bf16[384,384]{1,0:T(8,128)(2,1)} %near1.3) | copy-start | bytes 884740
  2.3 5.8 %collective-permute-start = (bf16[1,272,128]{2,1,0:T(8,128)(2,1)}, bf16[1,272,128]{2,1,0:T(8,128)(2,1)S(1)}, u32[]{:S(2)}, u32[]{:S(2)}) collective-permute-start(bf16[1,272,128]{2,1,0:T(8,128)(2,1)} %shard_map.113), channel_id=1, source_target_pairs={{0,64},{64,0},{128,192},{192,128},{1,65},{65,1},{129,193},{193,129... | collective-permute-start | bytes 208904 | tf_op jit(solution)/shard_map/ppermute | solution.py:256
  8.1 39.6 %all-to-all-start = ((bf16[8,272,128]{2,1,0:T(8,128)(2,1)}), bf16[8,272,128]{2,1,0:T(8,128)(2,1)S(1)}, u32[]{:S(2)}, u32[]{:S(2)}) async-start(bf16[8,272,128]{2,1,0:T(8,128)(2,1)} %shard_map.114), calls=%async_computation | async-start | bytes 1114112 | tf_op jit(solution)/shard_map/all_to_all | solution.py:260
  14.5 12.9 %collective-permute-start.2 = (bf16[1,272,128]{2,1,0:T(8,128)(2,1)}, bf16[1,272,128]{2,1,0:T(8,128)(2,1)S(1)}, u32[]{:S(2)}, u32[]{:S(2)}) collective-permute-start(bf16[1,272,128]{2,1,0:T(8,128)(2,1)} %shard_map.113), channel_id=1, source_target_pairs={{0,192},{64,128},{128,64},{192,0},{1,193},{65,129},{129,65},{193,1... | collective-permute-start | bytes 208904 | tf_op jit(solution)/shard_map/ppermute | solution.py:256
  20.1 9.0 %collective-permute-start.1 = (bf16[1,272,128]{2,1,0:T(8,128)(2,1)}, bf16[1,272,128]{2,1,0:T(8,128)(2,1)S(1)}, u32[]{:S(2)}, u32[]{:S(2)}) collective-permute-start(bf16[1,272,128]{2,1,0:T(8,128)(2,1)} %shard_map.113), channel_id=1, source_target_pairs={{0,128},{64,192},{128,0},{192,64},{1,129},{65,193},{129,1},{193,65... | collective-permute-start | bytes 208904 | tf_op jit(solution)/shard_map/ppermute | solution.py:256
  30.0 14.4 %collective-permute-start.5 = (bf16[4,272,128]{2,1,0:T(8,128)(2,1)S(1)}, bf16[4,272,128]{2,1,0:T(8,128)(2,1)S(1)}, u32[]{:S(2)}, u32[]{:S(2)}) collective-permute-start(bf16[4,272,128]{2,1,0:T(8,128)(2,1)S(1)} %pad_maximum_fusion.own0), channel_id=1, source_target_pairs={{0,48},{16,32},{32,16},{48,0},{1,49},{17,33},{33,17},{49,1},{2,50}... | collective-permute-start | bytes 835592 | tf_op jit(solution)/shard_map/ppermute | solution.py:256
  32.6 13.8 %collective-permute-start.4 = (bf16[4,272,128]{2,1,0:T(8,128)(2,1)S(1)}, bf16[4,272,128]{2,1,0:T(8,128)(2,1)S(1)}, u32[]{:S(2)}, u32[]{:S(2)}) collective-permute-start(bf16[4,272,128]{2,1,0:T(8,128)(2,1)S(1)} %pad_maximum_fusion.own0), channel_id=1, source_target_pairs={{0,32},{16,48},{32,0},{48,16},{1,33},{17,49},{33,1},{49,17},{2,34}... | collective-permute-start | bytes 835592 | tf_op jit(solution)/shard_map/ppermute | solution.py:256
  33.1 13.3 %collective-permute-start.3 = (bf16[4,272,128]{2,1,0:T(8,128)(2,1)S(1)}, bf16[4,272,128]{2,1,0:T(8,128)(2,1)S(1)}, u32[]{:S(2)}, u32[]{:S(2)}) collective-permute-start(bf16[4,272,128]{2,1,0:T(8,128)(2,1)S(1)} %pad_maximum_fusion.own0), channel_id=1, source_target_pairs={{0,16},{16,0},{32,48},{48,32},{1,17},{17,1},{33,49},{49,33},{2,18}... | collective-permute-start | bytes 835592 | tf_op jit(solution)/shard_map/ppermute | solution.py:256
  33.4 20.5 %collective-permute-start.7 = (bf16[4,272,128]{2,1,0:T(8,128)(2,1)S(1)}, bf16[4,272,128]{2,1,0:T(8,128)(2,1)S(1)}, u32[]{:S(2)}, u32[]{:S(2)}) collective-permute-start(bf16[4,272,128]{2,1,0:T(8,128)(2,1)S(1)} %pad_maximum_fusion.own0), channel_id=1, source_target_pairs={{0,8},{8,0},{1,9},{9,1},{2,10},{10,2},{3,11},{11,3},{4,12},{12,4},... | collective-permute-start | bytes 835592 | tf_op jit(solution)/shard_map/ppermute | solution.py:256
  44.4 9.5 %collective-permute-start.10 = (bf16[4,272,128]{2,1,0:T(8,128)(2,1)S(1)}, bf16[4,272,128]{2,1,0:T(8,128)(2,1)S(1)}, u32[]{:S(2)}, u32[]{:S(2)}) collective-permute-start(bf16[4,272,128]{2,1,0:T(8,128)(2,1)S(1)} %collective-permute-done.5.own3), channel_id=1, source_target_pairs={{0,8},{8,0},{1,9},{9,1},{2,10},{10,2},{3,11},{11,3},{4,12},{12,4},... | collective-permute-start | bytes 835592 | tf_op jit(solution)/shard_map/ppermute | solution.py:256
  46.4 7.5 %collective-permute-start.9 = (bf16[4,272,128]{2,1,0:T(8,128)(2,1)S(1)}, bf16[4,272,128]{2,1,0:T(8,128)(2,1)S(1)}, u32[]{:S(2)}, u32[]{:S(2)}) collective-permute-start(bf16[4,272,128]{2,1,0:T(8,128)(2,1)S(1)} %collective-permute-done.4.own2), channel_id=1, source_target_pairs={{0,8},{8,0},{1,9},{9,1},{2,10},{10,2},{3,11},{11,3},{4,12},{12,4},... | collective-permute-start | bytes 835592 | tf_op jit(solution)/shard_map/ppermute | solution.py:256
  46.4 7.5 %collective-permute-start.8 = (bf16[4,272,128]{2,1,0:T(8,128)(2,1)S(1)}, bf16[4,272,128]{2,1,0:T(8,128)(2,1)}, u32[]{:S(2)}, u32[]{:S(2)}) collective-permute-start(bf16[4,272,128]{2,1,0:T(8,128)(2,1)S(1)} %collective-permute-done.3.own1), channel_id=1, source_target_pairs={{0,8},{8,0},{1,9},{9,1},{2,10},{10,2},{3,11},{11,3},{4,12},{12,4},... | collective-permute-start | bytes 835592 | tf_op jit(solution)/shard_map/ppermute | solution.py:256
  47.4 6.4 %collective-permute-start.6 = (s32[16]{0:T(128)S(1)}, s32[16]{0:T(128)S(1)}, u32[]{:S(2)}, u32[]{:S(2)}) collective-permute-start(s32[16]{0:T(128)S(1)} %maximum_convert_fusion.own_links), channel_id=1, source_target_pairs={{0,8},{8,0},{1,9},{9,1},{2,10},{10,2},{3,11},{11,3},{4,12},{12,4},... | collective-permute-start | bytes 200 | tf_op jit(solution)/shard_map/ppermute | solution.py:256
  47.9 1.0 copy-start
  48.9 1.0 copy-start.2
  49.8 1.0 copy-start.4
  50.8 1.0 copy-start.6
  72.6 2.8 %collective-permute-start.11 = (f32[16,128]{1,0:T(8,128)S(1)}, f32[16,128]{1,0:T(8,128)S(1)}, u32[]{:S(2)}, u32[]{:S(2)}) collective-permute-start(f32[16,128]{1,0:T(8,128)S(1)} %get-tuple-element.21), channel_id=1, source_target_pairs={{0,8},{8,0},{1,9},{9,1},{2,10},{10,2},{3,11},{11,3},{4,12},{12,4},... | collective-permute-start | bytes 24584 | tf_op jit(solution)/shard_map/ppermute | solution.py:256
  99.9 4.2 %collective-permute-start.12 = (f32[16,128]{1,0:T(8,128)S(1)}, f32[16,128]{1,0:T(8,128)S(1)}, u32[]{:S(2)}, u32[]{:S(2)}) collective-permute-start(f32[16,128]{1,0:T(8,128)S(1)} %get-tuple-element.27), channel_id=1, source_target_pairs={{0,8},{8,0},{1,9},{9,1},{2,10},{10,2},{3,11},{11,3},{4,12},{12,4},... | collective-permute-start | bytes 24584 | tf_op jit(solution)/shard_map/ppermute | solution.py:256
  104.8 12.9 %all-to-all-start.4 = ((f32[16,16,128]{2,1,0:T(8,128)}), f32[16,16,128]{2,1,0:T(8,128)S(1)}, u32[]{:S(2)}, u32[]{:S(2)}) async-start(f32[16,16,128]{2,1,0:T(8,128)} %broadcast_in_dim.11), calls=%async_computation.4 | async-start | bytes 262144 | tf_op jit(solution)/shard_map/all_to_all | solution.py:260

commit v4 on v3

--- a/solution.py
+++ b/solution.py
@@ -35,18 +35,17 @@
         copy.start()
     for copy in copies:
         copy.wait()
-    link = jnp.broadcast_to(links_ref[0, 0:1, 1:2].astype(jnp.float32), (16, LANES)).astype(jnp.bfloat16)
-    for d in range(out.shape[0]):
-        for piece in range(D // LANES):
-            out[d, piece * PART : (piece + 1) * PART, :] = feats_ref[0, :, piece * LANES : (piece + 1) * LANES]
-        out[d, 3 * PART : 4 * PART, :] = tiles_ref[0]
-        out[d, 4 * PART : PACK, :] = link
-
-
-def pack(feats, tiles, links, count):
+    for piece in range(D // LANES):
+        out[0, piece * PART : (piece + 1) * PART, :] = feats_ref[0, :, piece * LANES : (piece + 1) * LANES]
+    out[0, 3 * PART : 4 * PART, :] = tiles_ref[0]
+    link = jnp.broadcast_to(links_ref[0, 0:1, 1:2].astype(jnp.float32), (16, LANES))
+    out[0, 4 * PART : PACK, :] = link.astype(jnp.bfloat16)
+
+
+def pack(feats, tiles, links):
     (packed,) = call(
         pack_kernel,
-        [((count, PACK, LANES), jnp.bfloat16)],
+        [((1, PACK, LANES), jnp.bfloat16)],
         [pltpu.VMEM(v.shape, v.dtype) for v in (feats, tiles, links)] + [pltpu.SemaphoreType.DMA((3,))],
         [HBM()] * 3,
         limit=PACK_LIMIT,
@@ -54,7 +53,7 @@
     return packed
 
 
-def graph_layers(packed, first, second, near1, self1, near2, self2, x_ref, s_ref, h_ref, emit):
+def graph_layers(packed, first, second, weights, x_ref, s_ref, h_ref, emit):
     count = x_ref.shape[0] // PART
     for k in range(count):
         ref, at = packed(k)
@@ -73,28 +72,33 @@
             total = jnp.dot(panel, both, preferred_element_type=jnp.float32)
             s_ref[k * PART : (k + 1) * PART, :] = total.astype(jnp.bfloat16)
 
-    def mix(src, at, near, own):
+    def mix(src, at, layer):
         left = jnp.concatenate([s_ref[at : at + STEP, :], src[at : at + STEP, :]], axis=1)
-        right = jnp.concatenate([near[...], own[...]], axis=0)
+        right = weights[layer * 2 * D : (layer + 1) * 2 * D, :]
         return jnp.dot(left, right, preferred_element_type=jnp.float32)
 
     neighbour_sums(x_ref)
     for at in range(0, count * PART, STEP):
-        h_ref[at : at + STEP, :] = jnp.maximum(mix(x_ref, at, near1, self1), 0.0).astype(jnp.bfloat16)
+        h_ref[at : at + STEP, :] = jnp.maximum(mix(x_ref, at, 0), 0.0).astype(jnp.bfloat16)
     neighbour_sums(h_ref)
     for at in range(0, count * PART, STEP):
-        emit(at, mix(h_ref, at, near2, self2).astype(jnp.bfloat16))
-
-
-def source_kernel(links, packed, near1, self1, near2, self2, out, x_ref, s_ref, h_ref):
+        emit(at, mix(h_ref, at, 1).astype(jnp.bfloat16))
+
+
+def source_kernel(place, links, own0, own1, own2, own3, weights, out, x_ref, s_ref, h_ref):
+    me = place[0]
+    pieces = (own0, own1, own2, own3)
+
     def emit(at, value):
-        out[at : at + value.shape[0], :] = value
+        for k in range(value.shape[0] // PART):
+            q = me ^ (at // PART + k)
+            out[pl.ds(pl.multiple_of(q * PART, PART), PART), :] = value[k * PART : (k + 1) * PART, :]
 
     graph_layers(
-        lambda k: (packed, k),
-        lambda k: 7 - k,
-        lambda k: links[k],
-        near1, self1, near2, self2, x_ref, s_ref, h_ref, emit,
+        lambda k: (pieces[k // 2], k % 2),
+        lambda k: k ^ 7,
+        lambda k: links[k] ^ me,
+        weights, x_ref, s_ref, h_ref, emit,
     )
 
 
@@ -113,7 +117,7 @@
 def target_kernel(
     place, own_links, other_links,
     own0, own1, own2, own3, other0, other1, other2, other3,
-    near1, self1, near2, self2, emb_source,
+    weights, emb_source,
     scores, send,
     x_ref, s_ref, h_ref, e_ref,
 ):
@@ -129,7 +133,7 @@
         lambda k: (pieces[k // 4], k % 4),
         lambda k: k ^ 31,
         lambda k: slot_of((own_links[k] if k < 16 else other_links[k - 16]) ^ me),
-        near1, self1, near2, self2, x_ref, s_ref, h_ref, emit,
+        weights, x_ref, s_ref, h_ref, emit,
     )
 
     for at in range(0, ROWS, 256):
@@ -237,7 +241,9 @@
             rows = pl.ds(at, step)
             e = weights[i, rows, :] * factor[rows, :]
             total += jnp.sum(e.reshape(step // 8, 8, LANES), axis=0)
-        sums[i : i + 1, :] = jnp.sum(total * scale[i], axis=0, keepdims=True)
+        total = jnp.sum(total * scale[i], axis=0, keepdims=True)
+        for d in range(N_PEERS):
+            sums[d, i : i + 1, :] = total
 
 
 def call(kernel, outs, scratch, ins, cost=None, limit=VMEM_LIMIT):
@@ -265,35 +271,43 @@
     near_first, self_first, near_second, self_second,
 ):
     f32, bf16 = jnp.float32, jnp.bfloat16
-    weights = (near_first, self_first, near_second, self_second)
     me = lax.axis_index(("zh", "x", "c"))
-
-    held = pack(target_feats, target_tiles, target_links, 1)
-    packed = pack(source_feats, source_tiles, source_links, N_TGT)
-    near, far, beyond = (swap(held, "zh", 4, xor) for xor in (1, 2, 3))
-    near, packed = lax.optimization_barrier((near, packed))
-    packed = exchange(packed, ("y", "zl"))
-    held = jnp.concatenate([held, near, far, beyond], axis=0)
+    me_source = lax.axis_index(("y", "zl"))
+
+    held = pack(target_feats, target_tiles, target_links)
+    source = pack(source_feats, source_tiles, source_links)
+    held, source, *weights = lax.optimization_barrier(
+        (held, source, near_first, self_first, near_second, self_second)
+    )
+    weights = jnp.concatenate(weights, axis=0)
+    held = jnp.concatenate([held] + [swap(held, "zh", 4, xor) for xor in (1, 2, 3)], axis=0)
+    source = jnp.concatenate([source, swap(source, "zl", 2, 1)], axis=0)
+    held, source, weights = lax.optimization_barrier((held, source, weights))
     own = [held] + [swap(held, "x", 4, xor) for xor in (1, 2, 3)]
+    source = [source] + [swap(source, "y", 4, xor) for xor in (1, 2, 3)]
     other = [swap(piece, "c", 2, 1) for piece in own]
     own_links = jnp.concatenate([piece[:, 4 * PART, 0] for piece in own]).astype(jnp.int32)
     other_links = swap(own_links, "c", 2, 1)
 
-    source_second = packed[:, 4 * PART, 0].astype(jnp.int32)
     (emb_source,) = call(
         source_kernel,
         [((ROWS, D), bf16)],
         [pltpu.VMEM((ROWS, D), bf16)] * 3,
-        [SMEM()] + [VMEM()] * 5,
+        [SMEM()] * 2 + [VMEM()] * 5,
         pl.CostEstimate(flops=700_000_000, bytes_accessed=2_000_000, transcendentals=0),
-    )(source_second, packed, *weights)
+    )(
+        me_source[None],
+        jnp.concatenate([piece[:, 4 * PART, 0] for piece in source]).astype(jnp.int32),
+        *source,
+        weights,
+    )
 
     scores, send = call(
         target_kernel,
         [((COL_BLOCKS, ROWS, LANES), f32), ((N_TGT, 8, LANES), f32)],
         [pltpu.VMEM((COLS, D), bf16)] * 4,
-        [SMEM()] * 3 + [VMEM()] * 13,
-    )(me[None], own_links, other_links, *own, *other, *weights, emb_source)
+        [SMEM()] * 3 + [VMEM()] * 10,
+    )(me[None], own_links, other_links, *own, *other, weights, emb_source)
 
     got = exchange(send, ("y", "zl"))
     spread_weights, tops, lse, source_first = call(
@@ -320,14 +334,14 @@
     got = exchange(send, ("y", "zl"))
     sums, source_potential = call(
         last_kernel,
-        [((COL_BLOCKS, LANES), f32), ((8, LANES), f32)],
+        [((N_PEERS, COL_BLOCKS, LANES), f32), ((8, LANES), f32)],
         [pltpu.VMEM((ROWS, LANES), f32)],
         [VMEM()] * 4,
     )(spread_weights, scale, got, source_first)
 
-    sums = sums + swap(sums, "c", 2, 1)
-    got = exchange(jnp.broadcast_to(sums, (N_PEERS, COL_BLOCKS, LANES)), ("zh", "x"))
-    target_potential = target_first + (LOG_N - jnp.log(jnp.sum(got, axis=0)))
+    total = jnp.sum(exchange(sums, ("zh", "x")), axis=0)
+    total = total + swap(total, "c", 2, 1)
+    target_potential = target_first + (LOG_N - jnp.log(total))
     return source_potential[0:4].reshape(ROWS), target_potential.reshape(COLS)
 
 

time: 119 us -> 111 us (0.933)
  blocking collectives: 33.4 us -> 47.9 us
  waiting for transfers between devices: 26 us -> 16 us
  starting transfers between devices: 35.6 us -> 28.2 us
  local copies, waits for them, and re-layouts: 5.58 us -> 1.47 us
    all_to_all x3 -> x4, blocking collectives: 33.4 us -> 47.9 us  [exchange(): return lax.all_to_all(value, axes, 0, 0)]
    all_to_all x2 -> x0, starting transfers between devices: 9.95 us -> none  [exchange(): return lax.all_to_all(value, axes, 0, 0)]
    all_to_all x2 -> x0, waiting for transfers between devices: 8.83 us -> none  [exchange(): return lax.all_to_all(value, axes, 0, 0)]
    unnamed x14 -> x4, local copies, waits for them, and re-layouts: 3.87 us -> 0.01 us
    ppermute x13 -> x17, starting transfers between devices: 25.6 us -> 28.2 us  [swap(): return lax.ppermute(value, axis, [(i, i ^ xor) for i in range(size)])]
    ppermute x13 -> x17, waiting for transfers between devices: 17.1 us -> 16 us  [swap(): return lax.ppermute(value, axis, [(i, i ^ xor) for i in range(size)])]
  transfers between devices with their start and end apart: 15 -> 17, of which waited for: 7 -> 6; matrix products, arithmetic and copies ran while one was open for 2% -> 3% of each run, Pallas kernels for 3% -> 2%
where the time goes in v4:
time: 111 us
  blocking collectives  47.9 us (43%)
  starting transfers between devices  28.2 us (25%)
  waiting for transfers between devices  16 us (14%)
  Pallas kernels  14.5 us (13%)
  other arithmetic  2.21 us (2%)
  local copies, waits for them, and re-layouts  1.47 us (1%)
    all_to_all x4, blocking collectives, exchange(): return lax.all_to_all(value, axes, 0, 0)  47.9 us
    ppermute x17, starting transfers between devices, swap(): return lax.ppermute(value, axis, [(i, i ^ xor) for i in range(size)])  28.2 us
    ppermute x17, waiting for transfers between devices, swap(): return lax.ppermute(value, axis, [(i, i ^ xor) for i in range(size)])  16 us
    pallas_call x1, Pallas kernels, on_device(): call(target_kernel, [((COL_BLOCKS, ROWS, LANES), f32), ((N_TGT, 8, LANES)...  7.44 us
    pallas_call x2, Pallas kernels, pack(): call(pack_kernel, [((1, PACK, LANES), jnp.bfloat16)], [pltpu.VMEM(v.shape...  3.07 us
  transfers between devices with their start and end apart: 17, of which 6 were waited for; matrix products, arithmetic and copies ran while one was open for 3% of the time, Pallas kernels for 2%

profile of v4, /device:TPU:1, one launch (start us, length us, event | category | flops | bytes accessed | tf_op | source)
XLA Modules:
  0.0 111.1 jit_solution(3066568136611616866)
XLA Ops:
  0.6 1.5 %shard_map.114 = bf16[1,272,128]{2,1,0:T(8,128)(2,1)} custom-call(bf16[1,64,384]{2,1,0:T(8,128)(2,1)} %feats.3, bf16[1,64,128]{2,1,0:T(8,128)(2,1)} %tiles.3, s32[1,1,2]{2,1,0:T(1,128)} %links.3), custom_call_target="tpu_custom_call" | custom-call | tf_op jit(solution)/shard_map/pallas_call | solution.py:46
  2.2 1.6 %shard_map.113 = bf16[1,272,128]{2,1,0:T(8,128)(2,1)} custom-call(bf16[1,64,384]{2,1,0:T(8,128)(2,1)} %feats.2, bf16[1,64,128]{2,1,0:T(8,128)(2,1)} %tiles.2, s32[1,1,2]{2,1,0:T(1,128)} %links.2), custom_call_target="tpu_custom_call" | custom-call | tf_op jit(solution)/shard_map/pallas_call | solution.py:46
  3.7 6.9 %collective-permute-start.2 = (bf16[1,272,128]{2,1,0:T(8,128)(2,1)}, bf16[1,272,128]{2,1,0:T(8,128)(2,1)S(1)}, u32[]{:S(2)}, u32[]{:S(2)}) collective-permute-start(bf16[1,272,128]{2,1,0:T(8,128)(2,1)} %shard_map.113), channel_id=1, source_target_pairs={{0,192},{64,128},{128,64},{192,0},{1,193},{65,129},{129,65},{193,1... | collective-permute-start | bytes 208904 | tf_op jit(solution)/shard_map/ppermute | solution.py:262
  10.7 1.0 collective-permute-start.1
  11.7 1.2 %collective-permute-start = (bf16[1,272,128]{2,1,0:T(8,128)(2,1)}, bf16[1,272,128]{2,1,0:T(8,128)(2,1)S(1)}, u32[]{:S(2)}, u32[]{:S(2)}) collective-permute-start(bf16[1,272,128]{2,1,0:T(8,128)(2,1)} %shard_map.113), channel_id=1, source_target_pairs={{0,64},{64,0},{128,192},{192,128},{1,65},{65,1},{129,193},{193,129... | collective-permute-start | bytes 208904 | tf_op jit(solution)/shard_map/ppermute | solution.py:262
  12.9 0.7 collective-permute-start.3
  13.6 1.3 %pad_maximum_fusion.weights = bf16[1536,384]{1,0:T(8,128)(2,1)S(1)} fusion(bf16[384,384]{1,0:T(8,128)(2,1)} %param.19, bf16[384,384]{1,0:T(8,128)(2,1)} %param.18, bf16[384,384]{1,0:T(8,128)(2,1)} %param.17, bf16[384,384]{1,0:T(8,128)(2,1)} %param.16), kind=kLoop, calls=%fused_computation | loop fusion | flops 4718592 | bytes 2359296 | tf_op jit(solution)/shard_map/concatenate | solution.py:282
  15.0 4.6 %collective-permute-done.3 = bf16[1,272,128]{2,1,0:T(8,128)(2,1)S(1)} collective-permute-done((bf16[1,272,128]{2,1,0:T(8,128)(2,1)}, bf16[1,272,128]{2,1,0:T(8,128)(2,1)S(1)}, u32[]{:S(2)}, u32[]{:S(2)}) %collective-permute-start.3) | collective-permute-done | bytes 69664 | tf_op jit(solution)/shard_map/ppermute | solution.py:262
  19.6 0.0 collective-permute-done.1
  19.6 0.4 collective-permute-done
  20.1 2.8 %collective-permute-start.14 = (bf16[2,272,128]{2,1,0:T(8,128)(2,1)S(1)}, bf16[2,272,128]{2,1,0:T(8,128)(2,1)S(1)}, u32[]{:S(2)}, u32[]{:S(2)}) collective-permute-start(bf16[2,272,128]{2,1,0:T(8,128)(2,1)S(1)} %pad_maximum_fusion.2.own0), channel_id=1, source_target_pairs={{0,6},{2,4},{4,2},{6,0},{1,7},{3,5},{5,3},{7,1},{8,14},{10,12},{12... | collective-permute-start | bytes 417800 | tf_op jit(solution)/shard_map/ppermute | solution.py:262
  22.9 0.3 collective-permute-start.13
  23.3 0.1 slice_reduce_fusion.3
  23.4 0.1 slice_reduce_fusion.7
  23.5 0.3 collective-permute-start.12
  23.8 2.5 %collective-permute-start.8 = (bf16[4,272,128]{2,1,0:T(8,128)(2,1)S(1)}, bf16[4,272,128]{2,1,0:T(8,128)(2,1)S(1)}, u32[]{:S(2)}, u32[]{:S(2)}) collective-permute-start(bf16[4,272,128]{2,1,0:T(8,128)(2,1)S(1)} %pad_maximum_fusion.1.own0), channel_id=1, source_target_pairs={{0,8},{8,0},{1,9},{9,1},{2,10},{10,2},{3,11},{11,3},{4,12},{12,4},... | collective-permute-start | bytes 835592 | tf_op jit(solution)/shard_map/ppermute | solution.py:262
  26.3 2.5 %collective-permute-start.6 = (bf16[4,272,128]{2,1,0:T(8,128)(2,1)S(1)}, bf16[4,272,128]{2,1,0:T(8,128)(2,1)S(1)}, u32[]{:S(2)}, u32[]{:S(2)}) collective-permute-start(bf16[4,272,128]{2,1,0:T(8,128)(2,1)S(1)} %pad_maximum_fusion.1.own0), channel_id=1, source_target_pairs={{0,48},{16,32},{32,16},{48,0},{1,49},{17,33},{33,17},{49,1},{2,50}... | collective-permute-start | bytes 835592 | tf_op jit(solution)/shard_map/ppermute | solution.py:262
  28.8 1.4 %collective-permute-start.5 = (bf16[4,272,128]{2,1,0:T(8,128)(2,1)S(1)}, bf16[4,272,128]{2,1,0:T(8,128)(2,1)S(1)}, u32[]{:S(2)}, u32[]{:S(2)}) collective-permute-start(bf16[4,272,128]{2,1,0:T(8,128)(2,1)S(1)} %pad_maximum_fusion.1.own0), channel_id=1, source_target_pairs={{0,32},{16,48},{32,0},{48,16},{1,33},{17,49},{33,1},{49,17},{2,34}... | collective-permute-start | bytes 835592 | tf_op jit(solution)/shard_map/ppermute | solution.py:262
  30.2 0.1 slice_reduce_fusion.4
  30.3 0.4 collective-permute-start.4
  30.7 0.1 slice_reduce_fusion.5
  30.8 0.1 slice_reduce_fusion.6
  30.9 0.1 maximum_convert_fusion.1.links
  30.9 2.1 %shard_map.115.emb_source = bf16[512,384]{1,0:T(8,128)(2,1)S(1)} custom-call(s32[1]{0:T(128)} %bitcast.1.place, s32[8]{0:T(128)S(1)} %maximum_convert_fusion.1.links, bf16[2,272,128]{2,1,0:T(8,128)(2,1)S(1)} %pad_maximum_fusion.2.own0, bf16[2,272,128]{2,1,0:T(8,128)(2,1)S(1)} %collective-permute-done.12.own1, ...), custom_call_target="tpu_custom_call" | custom-call | flops 700000000 | bytes 2000000 | tf_op jit(solution)/shard_map/pallas_call | solution.py:292
  33.0 8.7 %collective-permute-done.6.own3 = bf16[4,272,128]{2,1,0:T(8,128)(2,1)S(1)} collective-permute-done((bf16[4,272,128]{2,1,0:T(8,128)(2,1)S(1)}, bf16[4,272,128]{2,1,0:T(8,128)(2,1)S(1)}, u32[]{:S(2)}, u32[]{:S(2)}) %collective-permute-start.6) | collective-permute-done | bytes 278560 | tf_op jit(solution)/shard_map/ppermute | solution.py:262
  41.7 0.8 collective-permute-start.11
  42.5 0.0 collective-permute-start.10
  42.5 0.1 slice_reduce_fusion
  42.7 1.5 %collective-permute-start.9 = (bf16[4,272,128]{2,1,0:T(8,128)(2,1)S(1)}, bf16[4,272,128]{2,1,0:T(8,128)(2,1)S(1)}, u32[]{:S(2)}, u32[]{:S(2)}) collective-permute-start(bf16[4,272,128]{2,1,0:T(8,128)(2,1)S(1)} %collective-permute-done.4.own1), channel_id=1, source_target_pairs={{0,8},{8,0},{1,9},{9,1},{2,10},{10,2},{3,11},{11,3},{4,12},{12,4},... | collective-permute-start | bytes 835592 | tf_op jit(solution)/shard_map/ppermute | solution.py:262
  44.1 0.1 slice_reduce_fusion.1
  44.2 0.1 slice_reduce_fusion.2
  44.4 0.1 maximum_convert_fusion.own_links
  44.4 0.2 collective-permute-start.7
  44.7 1.1 collective-permute-done.7.other_links
  45.8 7.4 %shard_map.116 = (f32[16,512,128]{2,1,0:T(8,128)S(1)}, f32[8,8,128]{2,1,0:T(8,128)S(1)}) custom-call(s32[1]{0:T(128)} %bitcast.place, s32[16]{0:T(128)S(1)} %maximum_convert_fusion.own_links, s32[16]{0:T(128)S(1)} %collective-permute-done.7.other_links, bf16[4,272,128]{2,1,0:T(8,128)(2,1)S(1)} %pad_maximum_fusion.1.own0, ...), custom_call_target="tpu_custom_call" | custom-call | tf_op jit(solution)/shard_map/pallas_call | solution.py:305
  53.2 10.7 %all_to_all.20.got = f32[8,8,128]{2,1,0:T(8,128)S(1)} all-to-all(f32[8,8,128]{2,1,0:T(8,128)S(1)} %get-tuple-element.32), channel_id=1, replica_groups=mesh['zh'=4,'x'=4,'c'=2,'y'=4,'zl'=2] {'y','zl'}, dimensions={0} | all-to-all | bytes 65536 | tf_op jit(solution)/shard_map/all_to_all | solution.py:266
  64.0 1.0 shard_map.117
  65.0 1.7 %collective-permute-start.15 = (f32[16,128]{1,0:T(8,128)S(1)}, f32[16,128]{1,0:T(8,128)S(1)}, u32[]{:S(2)}, u32[]{:S(2)}) collective-permute-start(f32[16,128]{1,0:T(8,128)S(1)} %get-tuple-element.35), channel_id=1, source_target_pairs={{0,8},{8,0},{1,9},{9,1},{2,10},{10,2},{3,11},{11,3},{4,12},{12,4},... | collective-permute-start | bytes 24584 | tf_op jit(solution)/shard_map/ppermute | solution.py:262
  66.7 0.8 collective-permute-done.15
  67.6 16.6 %all_to_all.21.got = f32[16,16,128]{2,1,0:T(8,128)S(1)} all-to-all(f32[16,16,128]{2,1,0:T(8,128)S(1)} %broadcast_in_dim.11), channel_id=1, replica_groups=mesh['zh'=4,'x'=4,'c'=2,'y'=4,'zl'=2] {'zh','x'}, dimensions={0} | all-to-all | bytes 262144 | tf_op jit(solution)/shard_map/all_to_all | solution.py:266
  84.2 0.4 shard_map.118
  84.6 7.5 %all_to_all.22.got = f32[8,8,128]{2,1,0:T(8,128)S(1)} all-to-all(f32[8,8,128]{2,1,0:T(8,128)S(1)} %get-tuple-element.37), channel_id=1, replica_groups=mesh['zh'=4,'x'=4,'c'=2,'y'=4,'zl'=2] {'y','zl'}, dimensions={0} | all-to-all | bytes 65536 | tf_op jit(solution)/shard_map/all_to_all | solution.py:266
  92.1 0.5 shard_map.119
  92.6 13.1 %all_to_all.23 = f32[16,16,128]{2,1,0:T(8,128)S(1)} all-to-all(f32[16,16,128]{2,1,0:T(8,128)S(1)} %get-tuple-element.41), channel_id=1, replica_groups=mesh['zh'=4,'x'=4,'c'=2,'y'=4,'zl'=2] {'zh','x'}, dimensions={0} | all-to-all | bytes 262144 | tf_op jit(solution)/shard_map/all_to_all | solution.py:266
  105.7 4.0 %collective-permute-start.16 = (f32[16,128]{1,0:T(8,128)S(1)}, f32[16,128]{1,0:T(8,128)S(1)}, u32[]{:S(2)}, u32[]{:S(2)}) collective-permute-start(f32[16,128]{1,0:T(8,128)S(1)} %reduce_sum.9), channel_id=1, source_target_pairs={{0,8},{8,0},{1,9},{9,1},{2,10},{10,2},{3,11},{11,3},{4,12},{12,4},... | collective-permute-start | bytes 24584 | tf_op jit(solution)/shard_map/ppermute | solution.py:262
  109.7 0.6 slice_bitcast_fusion
  110.2 0.2 collective-permute-done.16
  110.5 0.6 add_bitcast_fusion
  (19 shorter events, 0.1 us)
Async XLA Ops:
  2.2 17.4 %copy-start.1 = (bf16[1,272,128]{2,1,0:T(8,128)(2,1)S(1)}, bf16[1,272,128]{2,1,0:T(8,128)(2,1)}, u32[]{:S(2)}) copy-start(bf16[1,272,128]{2,1,0:T(8,128)(2,1)} %shard_map.114) | copy-start | bytes 208900
  3.7 16.3 %copy-start = (bf16[1,272,128]{2,1,0:T(8,128)(2,1)S(1)}, bf16[1,272,128]{2,1,0:T(8,128)(2,1)}, u32[]{:S(2)}) copy-start(bf16[1,272,128]{2,1,0:T(8,128)(2,1)} %shard_map.113) | copy-start | bytes 208900
  3.7 15.9 %collective-permute-start.2 = (bf16[1,272,128]{2,1,0:T(8,128)(2,1)}, bf16[1,272,128]{2,1,0:T(8,128)(2,1)S(1)}, u32[]{:S(2)}, u32[]{:S(2)}) collective-permute-start(bf16[1,272,128]{2,1,0:T(8,128)(2,1)} %shard_map.113), channel_id=1, source_target_pairs={{0,192},{64,128},{128,64},{192,0},{1,193},{65,129},{129,65},{193,1... | collective-permute-start | bytes 208904 | tf_op jit(solution)/shard_map/ppermute | solution.py:262
  10.7 8.9 %collective-permute-start.1 = (bf16[1,272,128]{2,1,0:T(8,128)(2,1)}, bf16[1,272,128]{2,1,0:T(8,128)(2,1)S(1)}, u32[]{:S(2)}, u32[]{:S(2)}) collective-permute-start(bf16[1,272,128]{2,1,0:T(8,128)(2,1)} %shard_map.113), channel_id=1, source_target_pairs={{0,128},{64,192},{128,0},{192,64},{1,129},{65,193},{129,1},{193,65... | collective-permute-start | bytes 208904 | tf_op jit(solution)/shard_map/ppermute | solution.py:262
  11.7 8.4 %collective-permute-start = (bf16[1,272,128]{2,1,0:T(8,128)(2,1)}, bf16[1,272,128]{2,1,0:T(8,128)(2,1)S(1)}, u32[]{:S(2)}, u32[]{:S(2)}) collective-permute-start(bf16[1,272,128]{2,1,0:T(8,128)(2,1)} %shard_map.113), channel_id=1, source_target_pairs={{0,64},{64,0},{128,192},{192,128},{1,65},{65,1},{129,193},{193,129... | collective-permute-start | bytes 208904 | tf_op jit(solution)/shard_map/ppermute | solution.py:262
  12.9 6.7 %collective-permute-start.3 = (bf16[1,272,128]{2,1,0:T(8,128)(2,1)}, bf16[1,272,128]{2,1,0:T(8,128)(2,1)S(1)}, u32[]{:S(2)}, u32[]{:S(2)}) collective-permute-start(bf16[1,272,128]{2,1,0:T(8,128)(2,1)} %shard_map.114), channel_id=1, source_target_pairs={{0,1},{1,0},{2,3},{3,2},{4,5},{5,4},{6,7},{7,6},{8,9},{9,8},{10,11... | collective-permute-start | bytes 208904 | tf_op jit(solution)/shard_map/ppermute | solution.py:262
  20.1 8.7 %collective-permute-start.14 = (bf16[2,272,128]{2,1,0:T(8,128)(2,1)S(1)}, bf16[2,272,128]{2,1,0:T(8,128)(2,1)S(1)}, u32[]{:S(2)}, u32[]{:S(2)}) collective-permute-start(bf16[2,272,128]{2,1,0:T(8,128)(2,1)S(1)} %pad_maximum_fusion.2.own0), channel_id=1, source_target_pairs={{0,6},{2,4},{4,2},{6,0},{1,7},{3,5},{5,3},{7,1},{8,14},{10,12},{12... | collective-permute-start | bytes 417800 | tf_op jit(solution)/shard_map/ppermute | solution.py:262
  22.9 7.4 %collective-permute-start.13 = (bf16[2,272,128]{2,1,0:T(8,128)(2,1)S(1)}, bf16[2,272,128]{2,1,0:T(8,128)(2,1)S(1)}, u32[]{:S(2)}, u32[]{:S(2)}) collective-permute-start(bf16[2,272,128]{2,1,0:T(8,128)(2,1)S(1)} %pad_maximum_fusion.2.own0), channel_id=1, source_target_pairs={{0,4},{2,6},{4,0},{6,2},{1,5},{3,7},{5,1},{7,3},{8,12},{10,14},{12... | collective-permute-start | bytes 417800 | tf_op jit(solution)/shard_map/ppermute | solution.py:262
  23.5 7.3 %collective-permute-start.12 = (bf16[2,272,128]{2,1,0:T(8,128)(2,1)S(1)}, bf16[2,272,128]{2,1,0:T(8,128)(2,1)S(1)}, u32[]{:S(2)}, u32[]{:S(2)}) collective-permute-start(bf16[2,272,128]{2,1,0:T(8,128)(2,1)S(1)} %pad_maximum_fusion.2.own0), channel_id=1, source_target_pairs={{0,2},{2,0},{4,6},{6,4},{1,3},{3,1},{5,7},{7,5},{8,10},{10,8},{12,... | collective-permute-start | bytes 417800 | tf_op jit(solution)/shard_map/ppermute | solution.py:262
  23.8 20.8 %collective-permute-start.8 = (bf16[4,272,128]{2,1,0:T(8,128)(2,1)S(1)}, bf16[4,272,128]{2,1,0:T(8,128)(2,1)S(1)}, u32[]{:S(2)}, u32[]{:S(2)}) collective-permute-start(bf16[4,272,128]{2,1,0:T(8,128)(2,1)S(1)} %pad_maximum_fusion.1.own0), channel_id=1, source_target_pairs={{0,8},{8,0},{1,9},{9,1},{2,10},{10,2},{3,11},{11,3},{4,12},{12,4},... | collective-permute-start | bytes 835592 | tf_op jit(solution)/shard_map/ppermute | solution.py:262
  26.3 15.5 %collective-permute-start.6 = (bf16[4,272,128]{2,1,0:T(8,128)(2,1)S(1)}, bf16[4,272,128]{2,1,0:T(8,128)(2,1)S(1)}, u32[]{:S(2)}, u32[]{:S(2)}) collective-permute-start(bf16[4,272,128]{2,1,0:T(8,128)(2,1)S(1)} %pad_maximum_fusion.1.own0), channel_id=1, source_target_pairs={{0,48},{16,32},{32,16},{48,0},{1,49},{17,33},{33,17},{49,1},{2,50}... | collective-permute-start | bytes 835592 | tf_op jit(solution)/shard_map/ppermute | solution.py:262
  28.8 13.8 %collective-permute-start.5 = (bf16[4,272,128]{2,1,0:T(8,128)(2,1)S(1)}, bf16[4,272,128]{2,1,0:T(8,128)(2,1)S(1)}, u32[]{:S(2)}, u32[]{:S(2)}) collective-permute-start(bf16[4,272,128]{2,1,0:T(8,128)(2,1)S(1)} %pad_maximum_fusion.1.own0), channel_id=1, source_target_pairs={{0,32},{16,48},{32,0},{48,16},{1,33},{17,49},{33,1},{49,17},{2,34}... | collective-permute-start | bytes 835592 | tf_op jit(solution)/shard_map/ppermute | solution.py:262
  30.3 12.4 %collective-permute-start.4 = (bf16[4,272,128]{2,1,0:T(8,128)(2,1)S(1)}, bf16[4,272,128]{2,1,0:T(8,128)(2,1)S(1)}, u32[]{:S(2)}, u32[]{:S(2)}) collective-permute-start(bf16[4,272,128]{2,1,0:T(8,128)(2,1)S(1)} %pad_maximum_fusion.1.own0), channel_id=1, source_target_pairs={{0,16},{16,0},{32,48},{48,32},{1,17},{17,1},{33,49},{49,33},{2,18}... | collective-permute-start | bytes 835592 | tf_op jit(solution)/shard_map/ppermute | solution.py:262
  41.7 4.0 %collective-permute-start.11 = (bf16[4,272,128]{2,1,0:T(8,128)(2,1)S(1)}, bf16[4,272,128]{2,1,0:T(8,128)(2,1)S(1)}, u32[]{:S(2)}, u32[]{:S(2)}) collective-permute-start(bf16[4,272,128]{2,1,0:T(8,128)(2,1)S(1)} %collective-permute-done.6.own3), channel_id=1, source_target_pairs={{0,8},{8,0},{1,9},{9,1},{2,10},{10,2},{3,11},{11,3},{4,12},{12,4},... | collective-permute-start | bytes 835592 | tf_op jit(solution)/shard_map/ppermute | solution.py:262
  42.5 3.2 %collective-permute-start.10 = (bf16[4,272,128]{2,1,0:T(8,128)(2,1)S(1)}, bf16[4,272,128]{2,1,0:T(8,128)(2,1)S(1)}, u32[]{:S(2)}, u32[]{:S(2)}) collective-permute-start(bf16[4,272,128]{2,1,0:T(8,128)(2,1)S(1)} %collective-permute-done.5.own2), channel_id=1, source_target_pairs={{0,8},{8,0},{1,9},{9,1},{2,10},{10,2},{3,11},{11,3},{4,12},{12,4},... | collective-permute-start | bytes 835592 | tf_op jit(solution)/shard_map/ppermute | solution.py:262
  42.7 3.1 %collective-permute-start.9 = (bf16[4,272,128]{2,1,0:T(8,128)(2,1)S(1)}, bf16[4,272,128]{2,1,0:T(8,128)(2,1)S(1)}, u32[]{:S(2)}, u32[]{:S(2)}) collective-permute-start(bf16[4,272,128]{2,1,0:T(8,128)(2,1)S(1)} %collective-permute-done.4.own1), channel_id=1, source_target_pairs={{0,8},{8,0},{1,9},{9,1},{2,10},{10,2},{3,11},{11,3},{4,12},{12,4},... | collective-permute-start | bytes 835592 | tf_op jit(solution)/shard_map/ppermute | solution.py:262
  44.4 1.3 %collective-permute-start.7 = (s32[16]{0:T(128)S(1)}, s32[16]{0:T(128)S(1)}, u32[]{:S(2)}, u32[]{:S(2)}) collective-permute-start(s32[16]{0:T(128)S(1)} %maximum_convert_fusion.own_links), channel_id=1, source_target_pairs={{0,8},{8,0},{1,9},{9,1},{2,10},{10,2},{3,11},{11,3},{4,12},{12,4},... | collective-permute-start | bytes 200 | tf_op jit(solution)/shard_map/ppermute | solution.py:262
  65.0 2.5 %collective-permute-start.15 = (f32[16,128]{1,0:T(8,128)S(1)}, f32[16,128]{1,0:T(8,128)S(1)}, u32[]{:S(2)}, u32[]{:S(2)}) collective-permute-start(f32[16,128]{1,0:T(8,128)S(1)} %get-tuple-element.35), channel_id=1, source_target_pairs={{0,8},{8,0},{1,9},{9,1},{2,10},{10,2},{3,11},{11,3},{4,12},{12,4},... | collective-permute-start | bytes 24584 | tf_op jit(solution)/shard_map/ppermute | solution.py:262
  105.7 4.8 %collective-permute-start.16 = (f32[16,128]{1,0:T(8,128)S(1)}, f32[16,128]{1,0:T(8,128)S(1)}, u32[]{:S(2)}, u32[]{:S(2)}) collective-permute-start(f32[16,128]{1,0:T(8,128)S(1)} %reduce_sum.9), channel_id=1, source_target_pairs={{0,8},{8,0},{1,9},{9,1},{2,10},{10,2},{3,11},{11,3},{4,12},{12,4},... | collective-permute-start | bytes 24584 | tf_op jit(solution)/shard_map/ppermute | solution.py:262

commit v5 on v4

--- a/solution.py
+++ b/solution.py
@@ -28,29 +28,30 @@
 SMEM = functools.partial(pl.BlockSpec, memory_space=pltpu.SMEM)
 
 
-def pack_kernel(feats, tiles, links, out, feats_ref, tiles_ref, links_ref, sems):
-    pairs = ((feats, feats_ref), (tiles, tiles_ref), (links, links_ref))
-    copies = [pltpu.make_async_copy(src, dst, sems.at[i]) for i, (src, dst) in enumerate(pairs)]
+def pack_kernel(*refs):
+    sources, outs, held, sems = refs[:6], refs[6:8], refs[8:14], refs[14]
+    copies = [pltpu.make_async_copy(src, dst, sems.at[i]) for i, (src, dst) in enumerate(zip(sources, held))]
     for copy in copies:
         copy.start()
-    for copy in copies:
-        copy.wait()
-    for piece in range(D // LANES):
-        out[0, piece * PART : (piece + 1) * PART, :] = feats_ref[0, :, piece * LANES : (piece + 1) * LANES]
-    out[0, 3 * PART : 4 * PART, :] = tiles_ref[0]
-    link = jnp.broadcast_to(links_ref[0, 0:1, 1:2].astype(jnp.float32), (16, LANES))
-    out[0, 4 * PART : PACK, :] = link.astype(jnp.bfloat16)
-
-
-def pack(feats, tiles, links):
-    (packed,) = call(
+    for graph, out in enumerate(outs):
+        for copy in copies[3 * graph : 3 * graph + 3]:
+            copy.wait()
+        feats, tiles, links = held[3 * graph : 3 * graph + 3]
+        for piece in range(D // LANES):
+            out[0, piece * PART : (piece + 1) * PART, :] = feats[0, :, piece * LANES : (piece + 1) * LANES]
+        out[0, 3 * PART : 4 * PART, :] = tiles[0]
+        link = jnp.broadcast_to(links[0, 0:1, 1:2].astype(jnp.float32), (16, LANES))
+        out[0, 4 * PART : PACK, :] = link.astype(jnp.bfloat16)
+
+
+def pack(*arrays):
+    return call(
         pack_kernel,
-        [((1, PACK, LANES), jnp.bfloat16)],
-        [pltpu.VMEM(v.shape, v.dtype) for v in (feats, tiles, links)] + [pltpu.SemaphoreType.DMA((3,))],
-        [HBM()] * 3,
+        [((1, PACK, LANES), jnp.bfloat16)] * 2,
+        [pltpu.VMEM(v.shape, v.dtype) for v in arrays] + [pltpu.SemaphoreType.DMA((6,))],
+        [HBM()] * 6,
         limit=PACK_LIMIT,
-    )(feats, tiles, links)
-    return packed
+    )(*arrays)
 
 
 def graph_layers(packed, first, second, weights, x_ref, s_ref, h_ref, emit):
@@ -85,29 +86,34 @@
         emit(at, mix(h_ref, at, 1).astype(jnp.bfloat16))
 
 
+def turn(v):
+    return ((v & 1) << 1) | (v >> 1)
+
+
+def slot_xor(k):
+    return (turn(k & 3) << 3) | (turn((k >> 2) & 3) << 1) | (k >> 4)
+
+
+def slot_of(v):
+    return turn(v >> 3) | (turn((v >> 1) & 3) << 2) | ((v & 1) << 4)
+
+
 def source_kernel(place, links, own0, own1, own2, own3, weights, out, x_ref, s_ref, h_ref):
     me = place[0]
     pieces = (own0, own1, own2, own3)
 
     def emit(at, value):
         for k in range(value.shape[0] // PART):
-            q = me ^ (at // PART + k)
+            slot = at // PART + k
+            q = me ^ ((turn(slot >> 1) << 1) | (slot & 1))
             out[pl.ds(pl.multiple_of(q * PART, PART), PART), :] = value[k * PART : (k + 1) * PART, :]
 
     graph_layers(
         lambda k: (pieces[k // 2], k % 2),
         lambda k: k ^ 7,
-        lambda k: links[k] ^ me,
+        lambda k: (turn((links[k] ^ me) >> 1) << 1) | ((links[k] ^ me) & 1),
         weights, x_ref, s_ref, h_ref, emit,
     )
-
-
-def slot_xor(k):
-    return ((k & 3) << 3) | (((k >> 2) & 3) << 1) | (k >> 4)
-
-
-def slot_of(v):
-    return (v >> 3) | (((v >> 1) & 3) << 2) | ((v & 1) << 4)
 
 
 def spread(row):
@@ -262,6 +268,11 @@
     return lax.ppermute(value, axis, [(i, i ^ xor) for i in range(size)])
 
 
+def direct(value, axis):
+    far, near, beyond = (swap(value, axis, 4, xor) for xor in (2, 1, 3))
+    return [value, far, near, beyond]
+
+
 def exchange(value, axes):
     return lax.all_to_all(value, axes, 0, 0)
 
@@ -274,17 +285,17 @@
     me = lax.axis_index(("zh", "x", "c"))
     me_source = lax.axis_index(("y", "zl"))
 
-    held = pack(target_feats, target_tiles, target_links)
-    source = pack(source_feats, source_tiles, source_links)
+    held, source = pack(target_feats, target_tiles, target_links, source_feats, source_tiles, source_links)
     held, source, *weights = lax.optimization_barrier(
         (held, source, near_first, self_first, near_second, self_second)
     )
     weights = jnp.concatenate(weights, axis=0)
-    held = jnp.concatenate([held] + [swap(held, "zh", 4, xor) for xor in (1, 2, 3)], axis=0)
     source = jnp.concatenate([source, swap(source, "zl", 2, 1)], axis=0)
+    held = jnp.concatenate(direct(held, "zh"), axis=0)
     held, source, weights = lax.optimization_barrier((held, source, weights))
-    own = [held] + [swap(held, "x", 4, xor) for xor in (1, 2, 3)]
-    source = [source] + [swap(source, "y", 4, xor) for xor in (1, 2, 3)]
+    source = direct(source, "y")
+    own = direct(held, "x")
+    own[1:], source = lax.optimization_barrier((own[1:], source))
     other = [swap(piece, "c", 2, 1) for piece in own]
     own_links = jnp.concatenate([piece[:, 4 * PART, 0] for piece in own]).astype(jnp.int32)
     other_links = swap(own_links, "c", 2, 1)

time: 111 us -> 104 us (0.937)
  waiting for transfers between devices: 16 us -> 10.1 us
  starting transfers between devices: 28.2 us -> 32.8 us
  blocking collectives: 47.9 us -> 43.4 us
  Pallas kernels: 14.5 us -> 13.3 us
    ppermute x17, waiting for transfers between devices: 16 us -> 10.1 us  [swap(): return lax.ppermute(value, axis, [(i, i ^ xor) for i in range(size)])]
    ppermute x17, starting transfers between devices: 28.2 us -> 32.8 us  [swap(): return lax.ppermute(value, axis, [(i, i ^ xor) for i in range(size)])]
    all_to_all x4, blocking collectives: 47.9 us -> 43.4 us  [exchange(): return lax.all_to_all(value, axes, 0, 0)]
    pallas_call x2 -> x1, Pallas kernels: 3.07 us -> 1.64 us  [pack(): call(pack_kernel, [((1, PACK, LANES), jnp.bfloat16)] * 2, [pltpu.VMEM(v.s...]
where the time goes in v5:
time: 104 us
  blocking collectives  43.4 us (42%)
  starting transfers between devices  32.8 us (32%)
  Pallas kernels  13.3 us (13%)
  waiting for transfers between devices  10.1 us (10%)
  other arithmetic  2.2 us (2%)
  local copies, waits for them, and re-layouts  1.15 us (1%)
    all_to_all x4, blocking collectives, exchange(): return lax.all_to_all(value, axes, 0, 0)  43.4 us
    ppermute x17, starting transfers between devices, swap(): return lax.ppermute(value, axis, [(i, i ^ xor) for i in range(size)])  32.8 us
    ppermute x17, waiting for transfers between devices, swap(): return lax.ppermute(value, axis, [(i, i ^ xor) for i in range(size)])  10.1 us
    pallas_call x1, Pallas kernels, on_device(): call(target_kernel, [((COL_BLOCKS, ROWS, LANES), f32), ((N_TGT, 8, LANES)...  7.48 us
    pallas_call x1, Pallas kernels, on_device(): call(source_kernel, [((ROWS, D), bf16)], [pltpu.VMEM((ROWS, D), bf16)] *...  2.08 us
  transfers between devices with their start and end apart: 17, of which 6 were waited for; matrix products, arithmetic and copies ran while one was open for 3% of the time, Pallas kernels for 2%

profile of v5, /device:TPU:1, one launch (start us, length us, event | category | flops | bytes accessed | tf_op | source)
XLA Modules:
  0.0 103.7 jit_solution(4297045498329078910)
XLA Ops:
  0.6 1.6 %shard_map.113 = (bf16[1,272,128]{2,1,0:T(8,128)(2,1)}, bf16[1,272,128]{2,1,0:T(8,128)(2,1)}) custom-call(bf16[1,64,384]{2,1,0:T(8,128)(2,1)} %refs_0_.1, bf16[1,64,128]{2,1,0:T(8,128)(2,1)} %refs_1_.1, s32[1,1,2]{2,1,0:T(1,128)} %refs_2_.1, bf16[1,64,384]{2,1,0:T(8,128)(2,1)} %refs_3_.1, bf16[1,64,128]{2,1,0:T(8,128)(2,1)} %refs_4_.1, s32[1,1,2]{2,1,0:T(1,128)} %refs_5_.1), custom_call_target="tpu_custom_call" | custom-call | tf_op jit(solution)/shard_map/pallas_call | solution.py:48
  2.3 6.9 %collective-permute-start.2 = (bf16[1,272,128]{2,1,0:T(8,128)(2,1)}, bf16[1,272,128]{2,1,0:T(8,128)(2,1)S(1)}, u32[]{:S(2)}, u32[]{:S(2)}) collective-permute-start(bf16[1,272,128]{2,1,0:T(8,128)(2,1)} %get-tuple-element.33), channel_id=1, source_target_pairs={{0,192},{64,128},{128,64},{192,0},{1,193},{65,129},{129,65},{193,1... | collective-permute-start | bytes 208904 | tf_op jit(solution)/shard_map/ppermute | solution.py:268
  9.2 1.2 %collective-permute-start.1 = (bf16[1,272,128]{2,1,0:T(8,128)(2,1)}, bf16[1,272,128]{2,1,0:T(8,128)(2,1)S(1)}, u32[]{:S(2)}, u32[]{:S(2)}) collective-permute-start(bf16[1,272,128]{2,1,0:T(8,128)(2,1)} %get-tuple-element.33), channel_id=1, source_target_pairs={{0,64},{64,0},{128,192},{192,128},{1,65},{65,1},{129,193},{193,129... | collective-permute-start | bytes 208904 | tf_op jit(solution)/shard_map/ppermute | solution.py:268
  10.4 1.0 collective-permute-start
  11.4 0.7 collective-permute-start.3
  12.2 1.3 %pad_maximum_fusion.weights = bf16[1536,384]{1,0:T(8,128)(2,1)S(1)} fusion(bf16[384,384]{1,0:T(8,128)(2,1)} %param.19, bf16[384,384]{1,0:T(8,128)(2,1)} %param.18, bf16[384,384]{1,0:T(8,128)(2,1)} %param.17, bf16[384,384]{1,0:T(8,128)(2,1)} %param.16), kind=kLoop, calls=%fused_computation | loop fusion | flops 4718592 | bytes 2359296 | tf_op jit(solution)/shard_map/concatenate | solution.py:292
  13.5 5.0 %collective-permute-done.3 = bf16[1,272,128]{2,1,0:T(8,128)(2,1)S(1)} collective-permute-done((bf16[1,272,128]{2,1,0:T(8,128)(2,1)}, bf16[1,272,128]{2,1,0:T(8,128)(2,1)S(1)}, u32[]{:S(2)}, u32[]{:S(2)}) %collective-permute-start.3) | collective-permute-done | bytes 69664 | tf_op jit(solution)/shard_map/ppermute | solution.py:268
  18.6 0.0 collective-permute-done.2
  18.6 0.2 collective-permute-done
  18.8 2.8 %collective-permute-start.9 = (bf16[2,272,128]{2,1,0:T(8,128)(2,1)S(1)}, bf16[2,272,128]{2,1,0:T(8,128)(2,1)S(1)}, u32[]{:S(2)}, u32[]{:S(2)}) collective-permute-start(bf16[2,272,128]{2,1,0:T(8,128)(2,1)S(1)} %pad_maximum_fusion.2.own0), channel_id=1, source_target_pairs={{0,6},{2,4},{4,2},{6,0},{1,7},{3,5},{5,3},{7,1},{8,14},{10,12},{12... | collective-permute-start | bytes 417800 | tf_op jit(solution)/shard_map/ppermute | solution.py:268
  21.6 2.5 %collective-permute-start.6 = (bf16[4,272,128]{2,1,0:T(8,128)(2,1)S(1)}, bf16[4,272,128]{2,1,0:T(8,128)(2,1)S(1)}, u32[]{:S(2)}, u32[]{:S(2)}) collective-permute-start(bf16[4,272,128]{2,1,0:T(8,128)(2,1)S(1)} %pad_maximum_fusion.1.own0), channel_id=1, source_target_pairs={{0,48},{16,32},{32,16},{48,0},{1,49},{17,33},{33,17},{49,1},{2,50}... | collective-permute-start | bytes 835592 | tf_op jit(solution)/shard_map/ppermute | solution.py:268
  24.1 1.4 %collective-permute-start.4 = (bf16[4,272,128]{2,1,0:T(8,128)(2,1)S(1)}, bf16[4,272,128]{2,1,0:T(8,128)(2,1)S(1)}, u32[]{:S(2)}, u32[]{:S(2)}) collective-permute-start(bf16[4,272,128]{2,1,0:T(8,128)(2,1)S(1)} %pad_maximum_fusion.1.own0), channel_id=1, source_target_pairs={{0,32},{16,48},{32,0},{48,16},{1,33},{17,49},{33,1},{49,17},{2,34}... | collective-permute-start | bytes 835592 | tf_op jit(solution)/shard_map/ppermute | solution.py:268
  25.5 0.0 collective-permute-start.8
  25.5 0.0 collective-permute-done.9.own3
  25.5 1.3 %collective-permute-start.7 = (bf16[2,272,128]{2,1,0:T(8,128)(2,1)S(1)}, bf16[2,272,128]{2,1,0:T(8,128)(2,1)S(1)}, u32[]{:S(2)}, u32[]{:S(2)}) collective-permute-start(bf16[2,272,128]{2,1,0:T(8,128)(2,1)S(1)} %pad_maximum_fusion.2.own0), channel_id=1, source_target_pairs={{0,4},{2,6},{4,0},{6,2},{1,5},{3,7},{5,1},{7,3},{8,12},{10,14},{12... | collective-permute-start | bytes 417800 | tf_op jit(solution)/shard_map/ppermute | solution.py:268
  26.8 0.1 slice_reduce_fusion.3
  26.9 2.8 %collective-permute-done.8.own2 = bf16[2,272,128]{2,1,0:T(8,128)(2,1)S(1)} collective-permute-done((bf16[2,272,128]{2,1,0:T(8,128)(2,1)S(1)}, bf16[2,272,128]{2,1,0:T(8,128)(2,1)S(1)}, u32[]{:S(2)}, u32[]{:S(2)}) %collective-permute-start.8) | collective-permute-done | bytes 139296 | tf_op jit(solution)/shard_map/ppermute | solution.py:268
  29.7 4.4 %collective-permute-start.11 = (bf16[4,272,128]{2,1,0:T(8,128)(2,1)S(1)}, bf16[4,272,128]{2,1,0:T(8,128)(2,1)S(1)}, u32[]{:S(2)}, u32[]{:S(2)}) collective-permute-start(bf16[4,272,128]{2,1,0:T(8,128)(2,1)S(1)} %pad_maximum_fusion.1.own0), channel_id=1, source_target_pairs={{0,8},{8,0},{1,9},{9,1},{2,10},{10,2},{3,11},{11,3},{4,12},{12,4},... | collective-permute-start | bytes 835592 | tf_op jit(solution)/shard_map/ppermute | solution.py:268
  34.1 0.0 collective-permute-done.7.own1
  34.1 0.0 collective-permute-done.6.own3
  34.1 0.0 collective-permute-done.5.own2
  34.1 1.0 collective-permute-done.4.own1
  35.1 0.1 slice_reduce_fusion.2
  35.2 4.0 %collective-permute-start.12 = (bf16[4,272,128]{2,1,0:T(8,128)(2,1)S(1)}, bf16[4,272,128]{2,1,0:T(8,128)(2,1)S(1)}, u32[]{:S(2)}, u32[]{:S(2)}) collective-permute-start(bf16[4,272,128]{2,1,0:T(8,128)(2,1)S(1)} %collective-permute-done.4.own1), channel_id=1, source_target_pairs={{0,8},{8,0},{1,9},{9,1},{2,10},{10,2},{3,11},{11,3},{4,12},{12,4},... | collective-permute-start | bytes 835592 | tf_op jit(solution)/shard_map/ppermute | solution.py:268
  39.2 0.1 collective-permute-start.13
  39.3 0.1 slice_reduce_fusion
  39.4 0.5 collective-permute-start.14
  39.9 0.1 maximum_convert_fusion.own_links
  40.0 0.3 collective-permute-start.10
  40.3 0.1 slice_reduce_fusion.6
  40.4 0.1 slice_reduce_fusion.4
  40.5 0.1 maximum_convert_fusion.1.links
  40.6 2.1 %shard_map.114.emb_source = bf16[512,384]{1,0:T(8,128)(2,1)S(1)} custom-call(s32[1]{0:T(128)} %bitcast.1.place, s32[8]{0:T(128)S(1)} %maximum_convert_fusion.1.links, bf16[2,272,128]{2,1,0:T(8,128)(2,1)S(1)} %pad_maximum_fusion.2.own0, bf16[2,272,128]{2,1,0:T(8,128)(2,1)S(1)} %collective-permute-done.7.own1, ...), custom_call_target="tpu_custom_call" | custom-call | flops 700000000 | bytes 2000000 | tf_op jit(solution)/shard_map/pallas_call | solution.py:303
  42.7 0.0 collective-permute-done.11.other0
  42.8 7.5 %shard_map.115 = (f32[16,512,128]{2,1,0:T(8,128)S(1)}, f32[8,8,128]{2,1,0:T(8,128)S(1)}) custom-call(s32[1]{0:T(128)} %bitcast.place, s32[16]{0:T(128)S(1)} %maximum_convert_fusion.own_links, s32[16]{0:T(128)S(1)} %collective-permute-done.10.other_links, bf16[4,272,128]{2,1,0:T(8,128)(2,1)S(1)} %pad_maximum_fusion.1.own0, ...), custom_call_target="tpu_custom_call" | custom-call | tf_op jit(solution)/shard_map/pallas_call | solution.py:316
  50.2 7.5 %all_to_all.20.got = f32[8,8,128]{2,1,0:T(8,128)S(1)} all-to-all(f32[8,8,128]{2,1,0:T(8,128)S(1)} %get-tuple-element.50), channel_id=1, replica_groups=mesh['zh'=4,'x'=4,'c'=2,'y'=4,'zl'=2] {'y','zl'}, dimensions={0} | all-to-all | bytes 65536 | tf_op jit(solution)/shard_map/all_to_all | solution.py:277
  57.7 1.1 %shard_map.116 = (f32[16,512,128]{2,1,0:T(8,128)S(1)}, f32[16,8,128]{2,1,0:T(8,128)S(1)}, f32[16,128]{1,0:T(8,128)S(1)}, f32[8,128]{1,0:T(8,128)S(1)}) custom-call(f32[16,512,128]{2,1,0:T(8,128)S(1)} %get-tuple-element.49.scores, f32[8,8,128]{2,1,0:T(8,128)S(1)} %all_to_all.20.got), custom_call_target="tpu_custom_call" | custom-call | tf_op jit(solution)/shard_map/pallas_call | solution.py:324
  58.9 1.6 %collective-permute-start.15 = (f32[16,128]{1,0:T(8,128)S(1)}, f32[16,128]{1,0:T(8,128)S(1)}, u32[]{:S(2)}, u32[]{:S(2)}) collective-permute-start(f32[16,128]{1,0:T(8,128)S(1)} %get-tuple-element.53), channel_id=1, source_target_pairs={{0,8},{8,0},{1,9},{9,1},{2,10},{10,2},{3,11},{11,3},{4,12},{12,4},... | collective-permute-start | bytes 24584 | tf_op jit(solution)/shard_map/ppermute | solution.py:268
  60.5 0.8 collective-permute-done.15
  61.4 15.4 %all_to_all.21.got = f32[16,16,128]{2,1,0:T(8,128)S(1)} all-to-all(f32[16,16,128]{2,1,0:T(8,128)S(1)} %broadcast_in_dim.11), channel_id=1, replica_groups=mesh['zh'=4,'x'=4,'c'=2,'y'=4,'zl'=2] {'zh','x'}, dimensions={0} | all-to-all | bytes 262144 | tf_op jit(solution)/shard_map/all_to_all | solution.py:277
  76.8 0.4 shard_map.117
  77.2 7.5 %all_to_all.22.got = f32[8,8,128]{2,1,0:T(8,128)S(1)} all-to-all(f32[8,8,128]{2,1,0:T(8,128)S(1)} %get-tuple-element.55), channel_id=1, replica_groups=mesh['zh'=4,'x'=4,'c'=2,'y'=4,'zl'=2] {'y','zl'}, dimensions={0} | all-to-all | bytes 65536 | tf_op jit(solution)/shard_map/all_to_all | solution.py:277
  84.7 0.5 shard_map.118
  85.2 13.1 %all_to_all.23 = f32[16,16,128]{2,1,0:T(8,128)S(1)} all-to-all(f32[16,16,128]{2,1,0:T(8,128)S(1)} %get-tuple-element.59), channel_id=1, replica_groups=mesh['zh'=4,'x'=4,'c'=2,'y'=4,'zl'=2] {'zh','x'}, dimensions={0} | all-to-all | bytes 262144 | tf_op jit(solution)/shard_map/all_to_all | solution.py:277
  98.3 4.0 %collective-permute-start.16 = (f32[16,128]{1,0:T(8,128)S(1)}, f32[16,128]{1,0:T(8,128)S(1)}, u32[]{:S(2)}, u32[]{:S(2)}) collective-permute-start(f32[16,128]{1,0:T(8,128)S(1)} %reduce_sum.9), channel_id=1, source_target_pairs={{0,8},{8,0},{1,9},{9,1},{2,10},{10,2},{3,11},{11,3},{4,12},{12,4},... | collective-permute-start | bytes 24584 | tf_op jit(solution)/shard_map/ppermute | solution.py:268
  102.2 0.6 slice_bitcast_fusion
  102.8 0.2 collective-permute-done.16
  103.1 0.6 add_bitcast_fusion
  (15 shorter events, 0.1 us)
Async XLA Ops:
  2.3 16.3 %copy-start.1 = (bf16[1,272,128]{2,1,0:T(8,128)(2,1)S(1)}, bf16[1,272,128]{2,1,0:T(8,128)(2,1)}, u32[]{:S(2)}) copy-start(bf16[1,272,128]{2,1,0:T(8,128)(2,1)} %get-tuple-element.34) | copy-start | bytes 208900
  2.3 16.5 %copy-start = (bf16[1,272,128]{2,1,0:T(8,128)(2,1)S(1)}, bf16[1,272,128]{2,1,0:T(8,128)(2,1)}, u32[]{:S(2)}) copy-start(bf16[1,272,128]{2,1,0:T(8,128)(2,1)} %get-tuple-element.33) | copy-start | bytes 208900
  2.3 16.3 %collective-permute-start.2 = (bf16[1,272,128]{2,1,0:T(8,128)(2,1)}, bf16[1,272,128]{2,1,0:T(8,128)(2,1)S(1)}, u32[]{:S(2)}, u32[]{:S(2)}) collective-permute-start(bf16[1,272,128]{2,1,0:T(8,128)(2,1)} %get-tuple-element.33), channel_id=1, source_target_pairs={{0,192},{64,128},{128,64},{192,0},{1,193},{65,129},{129,65},{193,1... | collective-permute-start | bytes 208904 | tf_op jit(solution)/shard_map/ppermute | solution.py:268
  9.2 9.3 %collective-permute-start.1 = (bf16[1,272,128]{2,1,0:T(8,128)(2,1)}, bf16[1,272,128]{2,1,0:T(8,128)(2,1)S(1)}, u32[]{:S(2)}, u32[]{:S(2)}) collective-permute-start(bf16[1,272,128]{2,1,0:T(8,128)(2,1)} %get-tuple-element.33), channel_id=1, source_target_pairs={{0,64},{64,0},{128,192},{192,128},{1,65},{65,1},{129,193},{193,129... | collective-permute-start | bytes 208904 | tf_op jit(solution)/shard_map/ppermute | solution.py:268
  10.4 8.3 %collective-permute-start = (bf16[1,272,128]{2,1,0:T(8,128)(2,1)}, bf16[1,272,128]{2,1,0:T(8,128)(2,1)S(1)}, u32[]{:S(2)}, u32[]{:S(2)}) collective-permute-start(bf16[1,272,128]{2,1,0:T(8,128)(2,1)} %get-tuple-element.33), channel_id=1, source_target_pairs={{0,128},{64,192},{128,0},{192,64},{1,129},{65,193},{129,1},{193,65... | collective-permute-start | bytes 208904 | tf_op jit(solution)/shard_map/ppermute | solution.py:268
  11.4 7.1 %collective-permute-start.3 = (bf16[1,272,128]{2,1,0:T(8,128)(2,1)}, bf16[1,272,128]{2,1,0:T(8,128)(2,1)S(1)}, u32[]{:S(2)}, u32[]{:S(2)}) collective-permute-start(bf16[1,272,128]{2,1,0:T(8,128)(2,1)} %get-tuple-element.34), channel_id=1, source_target_pairs={{0,1},{1,0},{2,3},{3,2},{4,5},{5,4},{6,7},{7,6},{8,9},{9,8},{10,11... | collective-permute-start | bytes 208904 | tf_op jit(solution)/shard_map/ppermute | solution.py:268
  18.8 6.7 %collective-permute-start.9 = (bf16[2,272,128]{2,1,0:T(8,128)(2,1)S(1)}, bf16[2,272,128]{2,1,0:T(8,128)(2,1)S(1)}, u32[]{:S(2)}, u32[]{:S(2)}) collective-permute-start(bf16[2,272,128]{2,1,0:T(8,128)(2,1)S(1)} %pad_maximum_fusion.2.own0), channel_id=1, source_target_pairs={{0,6},{2,4},{4,2},{6,0},{1,7},{3,5},{5,3},{7,1},{8,14},{10,12},{12... | collective-permute-start | bytes 417800 | tf_op jit(solution)/shard_map/ppermute | solution.py:268
  21.6 12.5 %collective-permute-start.6 = (bf16[4,272,128]{2,1,0:T(8,128)(2,1)S(1)}, bf16[4,272,128]{2,1,0:T(8,128)(2,1)S(1)}, u32[]{:S(2)}, u32[]{:S(2)}) collective-permute-start(bf16[4,272,128]{2,1,0:T(8,128)(2,1)S(1)} %pad_maximum_fusion.1.own0), channel_id=1, source_target_pairs={{0,48},{16,32},{32,16},{48,0},{1,49},{17,33},{33,17},{49,1},{2,50}... | collective-permute-start | bytes 835592 | tf_op jit(solution)/shard_map/ppermute | solution.py:268
  24.1 10.0 %collective-permute-start.5 = (bf16[4,272,128]{2,1,0:T(8,128)(2,1)S(1)}, bf16[4,272,128]{2,1,0:T(8,128)(2,1)S(1)}, u32[]{:S(2)}, u32[]{:S(2)}) collective-permute-start(bf16[4,272,128]{2,1,0:T(8,128)(2,1)S(1)} %pad_maximum_fusion.1.own0), channel_id=1, source_target_pairs={{0,16},{16,0},{32,48},{48,32},{1,17},{17,1},{33,49},{49,33},{2,18}... | collective-permute-start | bytes 835592 | tf_op jit(solution)/shard_map/ppermute | solution.py:268
  24.1 11.0 %collective-permute-start.4 = (bf16[4,272,128]{2,1,0:T(8,128)(2,1)S(1)}, bf16[4,272,128]{2,1,0:T(8,128)(2,1)S(1)}, u32[]{:S(2)}, u32[]{:S(2)}) collective-permute-start(bf16[4,272,128]{2,1,0:T(8,128)(2,1)S(1)} %pad_maximum_fusion.1.own0), channel_id=1, source_target_pairs={{0,32},{16,48},{32,0},{48,16},{1,33},{17,49},{33,1},{49,17},{2,34}... | collective-permute-start | bytes 835592 | tf_op jit(solution)/shard_map/ppermute | solution.py:268
  25.5 4.2 %collective-permute-start.8 = (bf16[2,272,128]{2,1,0:T(8,128)(2,1)S(1)}, bf16[2,272,128]{2,1,0:T(8,128)(2,1)S(1)}, u32[]{:S(2)}, u32[]{:S(2)}) collective-permute-start(bf16[2,272,128]{2,1,0:T(8,128)(2,1)S(1)} %pad_maximum_fusion.2.own0), channel_id=1, source_target_pairs={{0,2},{2,0},{4,6},{6,4},{1,3},{3,1},{5,7},{7,5},{8,10},{10,8},{12,... | collective-permute-start | bytes 417800 | tf_op jit(solution)/shard_map/ppermute | solution.py:268
  25.5 8.6 %collective-permute-start.7 = (bf16[2,272,128]{2,1,0:T(8,128)(2,1)S(1)}, bf16[2,272,128]{2,1,0:T(8,128)(2,1)S(1)}, u32[]{:S(2)}, u32[]{:S(2)}) collective-permute-start(bf16[2,272,128]{2,1,0:T(8,128)(2,1)S(1)} %pad_maximum_fusion.2.own0), channel_id=1, source_target_pairs={{0,4},{2,6},{4,0},{6,2},{1,5},{3,7},{5,1},{7,3},{8,12},{10,14},{12... | collective-permute-start | bytes 417800 | tf_op jit(solution)/shard_map/ppermute | solution.py:268
  29.7 13.0 %collective-permute-start.11 = (bf16[4,272,128]{2,1,0:T(8,128)(2,1)S(1)}, bf16[4,272,128]{2,1,0:T(8,128)(2,1)S(1)}, u32[]{:S(2)}, u32[]{:S(2)}) collective-permute-start(bf16[4,272,128]{2,1,0:T(8,128)(2,1)S(1)} %pad_maximum_fusion.1.own0), channel_id=1, source_target_pairs={{0,8},{8,0},{1,9},{9,1},{2,10},{10,2},{3,11},{11,3},{4,12},{12,4},... | collective-permute-start | bytes 835592 | tf_op jit(solution)/shard_map/ppermute | solution.py:268
  35.2 7.5 %collective-permute-start.12 = (bf16[4,272,128]{2,1,0:T(8,128)(2,1)S(1)}, bf16[4,272,128]{2,1,0:T(8,128)(2,1)S(1)}, u32[]{:S(2)}, u32[]{:S(2)}) collective-permute-start(bf16[4,272,128]{2,1,0:T(8,128)(2,1)S(1)} %collective-permute-done.4.own1), channel_id=1, source_target_pairs={{0,8},{8,0},{1,9},{9,1},{2,10},{10,2},{3,11},{11,3},{4,12},{12,4},... | collective-permute-start | bytes 835592 | tf_op jit(solution)/shard_map/ppermute | solution.py:268
  39.2 3.5 %collective-permute-start.13 = (bf16[4,272,128]{2,1,0:T(8,128)(2,1)S(1)}, bf16[4,272,128]{2,1,0:T(8,128)(2,1)S(1)}, u32[]{:S(2)}, u32[]{:S(2)}) collective-permute-start(bf16[4,272,128]{2,1,0:T(8,128)(2,1)S(1)} %collective-permute-done.5.own2), channel_id=1, source_target_pairs={{0,8},{8,0},{1,9},{9,1},{2,10},{10,2},{3,11},{11,3},{4,12},{12,4},... | collective-permute-start | bytes 835592 | tf_op jit(solution)/shard_map/ppermute | solution.py:268
  39.4 3.3 %collective-permute-start.14 = (bf16[4,272,128]{2,1,0:T(8,128)(2,1)S(1)}, bf16[4,272,128]{2,1,0:T(8,128)(2,1)S(1)}, u32[]{:S(2)}, u32[]{:S(2)}) collective-permute-start(bf16[4,272,128]{2,1,0:T(8,128)(2,1)S(1)} %collective-permute-done.6.own3), channel_id=1, source_target_pairs={{0,8},{8,0},{1,9},{9,1},{2,10},{10,2},{3,11},{11,3},{4,12},{12,4},... | collective-permute-start | bytes 835592 | tf_op jit(solution)/shard_map/ppermute | solution.py:268
  40.0 2.7 %collective-permute-start.10 = (s32[16]{0:T(128)S(1)}, s32[16]{0:T(128)S(1)}, u32[]{:S(2)}, u32[]{:S(2)}) collective-permute-start(s32[16]{0:T(128)S(1)} %maximum_convert_fusion.own_links), channel_id=1, source_target_pairs={{0,8},{8,0},{1,9},{9,1},{2,10},{10,2},{3,11},{11,3},{4,12},{12,4},... | collective-permute-start | bytes 200 | tf_op jit(solution)/shard_map/ppermute | solution.py:268
  58.9 2.5 %collective-permute-start.15 = (f32[16,128]{1,0:T(8,128)S(1)}, f32[16,128]{1,0:T(8,128)S(1)}, u32[]{:S(2)}, u32[]{:S(2)}) collective-permute-start(f32[16,128]{1,0:T(8,128)S(1)} %get-tuple-element.53), channel_id=1, source_target_pairs={{0,8},{8,0},{1,9},{9,1},{2,10},{10,2},{3,11},{11,3},{4,12},{12,4},... | collective-permute-start | bytes 24584 | tf_op jit(solution)/shard_map/ppermute | solution.py:268
  98.3 4.8 %collective-permute-start.16 = (f32[16,128]{1,0:T(8,128)S(1)}, f32[16,128]{1,0:T(8,128)S(1)}, u32[]{:S(2)}, u32[]{:S(2)}) collective-permute-start(f32[16,128]{1,0:T(8,128)S(1)} %reduce_sum.9), channel_id=1, source_target_pairs={{0,8},{8,0},{1,9},{9,1},{2,10},{10,2},{3,11},{11,3},{4,12},{12,4},... | collective-permute-start | bytes 24584 | tf_op jit(solution)/shard_map/ppermute | solution.py:268

commit v6 on v5

--- a/solution.py
+++ b/solution.py
@@ -11,12 +11,14 @@
 D = 384
 PART = 64
 PACK = 272
-ROWS = 512
-COLS = 2048
+OWN_ROWS = 512
+BLOCK = 2048
+ROWS = 1024
+COLS = 1024
 LANES = 128
 ROW_BLOCKS = ROWS // LANES
 COL_BLOCKS = COLS // LANES
-N_TGT = 8
+N_ROW_PEERS = 16
 STEP = 512
 N_PEERS = 16
 LOG_N = math.log(16384.0)
@@ -54,7 +56,7 @@
     )(*arrays)
 
 
-def graph_layers(packed, first, second, weights, x_ref, s_ref, h_ref, emit):
+def graph_layers(packed, first, second, weights, x_ref, s_ref, h_ref, emit, wanted):
     count = x_ref.shape[0] // PART
     for k in range(count):
         ref, at = packed(k)
@@ -63,7 +65,7 @@
                 at, piece * PART : (piece + 1) * PART, :
             ]
 
-    def neighbour_sums(src):
+    def neighbour_sums(src, count):
         for k in range(count):
             ref, at = packed(k)
             near = src[pl.ds(first(k) * PART, PART), :]
@@ -78,11 +80,11 @@
         right = weights[layer * 2 * D : (layer + 1) * 2 * D, :]
         return jnp.dot(left, right, preferred_element_type=jnp.float32)
 
-    neighbour_sums(x_ref)
+    neighbour_sums(x_ref, count)
     for at in range(0, count * PART, STEP):
         h_ref[at : at + STEP, :] = jnp.maximum(mix(x_ref, at, 0), 0.0).astype(jnp.bfloat16)
-    neighbour_sums(h_ref)
-    for at in range(0, count * PART, STEP):
+    neighbour_sums(h_ref, wanted)
+    for at in range(0, wanted * PART, STEP):
         emit(at, mix(h_ref, at, 1).astype(jnp.bfloat16))
 
 
@@ -112,7 +114,7 @@
         lambda k: (pieces[k // 2], k % 2),
         lambda k: k ^ 7,
         lambda k: (turn((links[k] ^ me) >> 1) << 1) | ((links[k] ^ me) & 1),
-        weights, x_ref, s_ref, h_ref, emit,
+        weights, x_ref, s_ref, h_ref, emit, 8,
     )
 
 
@@ -123,32 +125,37 @@
 def target_kernel(
     place, own_links, other_links,
     own0, own1, own2, own3, other0, other1, other2, other3,
-    weights, emb_source,
-    scores, send,
-    x_ref, s_ref, h_ref, e_ref,
+    weights,
+    out, x_ref, s_ref, h_ref,
 ):
     me = place[0]
     pieces = (own0, own1, own2, own3, other0, other1, other2, other3)
 
     def emit(at, value):
         for piece in range(value.shape[0] // PART):
-            q = me ^ slot_xor(at // PART + piece)
-            e_ref[pl.ds(pl.multiple_of(q * PART, PART), PART), :] = value[piece * PART : (piece + 1) * PART, :]
+            i = (me ^ slot_xor(at // PART + piece)) >> 1
+            row = (i & 7) * LANES + (i >> 3) * PART
+            out[pl.ds(pl.multiple_of(row, PART), PART), :] = value[piece * PART : (piece + 1) * PART, :]
 
     graph_layers(
         lambda k: (pieces[k // 4], k % 4),
         lambda k: k ^ 31,
         lambda k: slot_of((own_links[k] if k < 16 else other_links[k - 16]) ^ me),
-        weights, x_ref, s_ref, h_ref, emit,
-    )
-
+        weights, x_ref, s_ref, h_ref, emit, 16,
+    )
+
+
+def score_kernel(place, own_source, other_source, emb_target, scores, send, e_ref):
+    core = place[0] & 1
+    e_ref[pl.ds(pl.multiple_of(core * OWN_ROWS, OWN_ROWS), OWN_ROWS), :] = own_source[...]
+    e_ref[pl.ds(pl.multiple_of((1 - core) * OWN_ROWS, OWN_ROWS), OWN_ROWS), :] = other_source[...]
     for at in range(0, ROWS, 256):
         rows = pl.ds(at, 256)
         top = None
         for i in range(COL_BLOCKS // 2):
             part = lax.dot_general(
-                emb_source[rows, :],
-                e_ref[i * 256 : (i + 1) * 256, :],
+                e_ref[rows, :],
+                emb_target[i * 256 : (i + 1) * 256, :],
                 (((1,), (1,)), ((), ())),
                 preferred_element_type=jnp.float32,
             )
@@ -166,22 +173,21 @@
             part_total = jnp.transpose(total[half * LANES : (half + 1) * LANES])
             larger = jnp.max(part_top, axis=0, keepdims=True)
             part_total = jnp.sum(part_total * jnp.exp(part_top - larger), axis=0, keepdims=True)
-            for d in range(N_TGT):
+            for d in range(N_ROW_PEERS):
                 send[d, b : b + 1, :] = larger
-                send[d, b + 4 : b + 5, :] = part_total
-
-
-def column_kernel(scores, got, weights, tops, lse, potential, shift):
-    top, total = got[0, 0:4, :], got[0, 4:8, :]
+                send[d, ROW_BLOCKS + b : ROW_BLOCKS + b + 1, :] = part_total
+
+
+def column_kernel(scores, got, weights, tops, send, potential, shift):
+    top, total = got[0, 0:ROW_BLOCKS, :], got[0, ROW_BLOCKS:, :]
     larger = top
-    for d in range(1, N_TGT):
-        larger = jnp.maximum(larger, got[d, 0:4, :])
+    for d in range(1, N_ROW_PEERS):
+        larger = jnp.maximum(larger, got[d, 0:ROW_BLOCKS, :])
     total = total * jnp.exp(top - larger)
-    for d in range(1, N_TGT):
-        total += got[d, 4:8, :] * jnp.exp(got[d, 0:4, :] - larger)
+    for d in range(1, N_ROW_PEERS):
+        total += got[d, ROW_BLOCKS:, :] * jnp.exp(got[d, 0:ROW_BLOCKS, :] - larger)
     source = LOG_N - (larger + jnp.log(total))
-    potential[0:4, :] = source
-    potential[4:8, :] = source
+    potential[...] = source
     for b in range(ROW_BLOCKS):
         shift[pl.ds(b * LANES, LANES), :] = spread(source[b : b + 1, :])
 
@@ -203,7 +209,9 @@
         tops[i] = top
         larger = jnp.max(top, axis=0, keepdims=True)
         total = jnp.sum(total * jnp.exp(top - larger), axis=0, keepdims=True)
-        lse[i : i + 1, :] = larger + jnp.log(total)
+        total = larger + jnp.log(total)
+        for d in range(N_PEERS):
+            send[d, i : i + 1, :] = total
 
 
 def row_kernel(weights, tops, got, send, potential, scale):
@@ -224,18 +232,15 @@
             total += weights[i, rows, :].reshape(LANES // 8, 8, LANES) * scale[i][None]
         total = jnp.transpose(total.reshape(LANES, LANES))
         total = jnp.sum(total, axis=0, keepdims=True)
-        for d in range(N_TGT):
+        for d in range(N_ROW_PEERS):
             send[d, b : b + 1, :] = total
-            send[d, b + 4 : b + 5, :] = total
 
 
 def last_kernel(weights, scale, got, before, sums, potential, factor):
-    total = got[0, 0:4, :]
-    for d in range(1, N_TGT):
-        total += got[d, 0:4, :]
-    source = before[0:4, :] + (LOG_N - jnp.log(total))
-    potential[0:4, :] = source
-    potential[4:8, :] = source
+    total = got[0]
+    for d in range(1, N_ROW_PEERS):
+        total += got[d]
+    potential[...] = before[...] + (LOG_N - jnp.log(total))
     ratio = 16384.0 / total
     for b in range(ROW_BLOCKS):
         factor[pl.ds(b * LANES, LANES), :] = spread(ratio[b : b + 1, :])
@@ -302,8 +307,8 @@
 
     (emb_source,) = call(
         source_kernel,
-        [((ROWS, D), bf16)],
-        [pltpu.VMEM((ROWS, D), bf16)] * 3,
+        [((OWN_ROWS, D), bf16)],
+        [pltpu.VMEM((OWN_ROWS, D), bf16)] * 3,
         [SMEM()] * 2 + [VMEM()] * 5,
         pl.CostEstimate(flops=700_000_000, bytes_accessed=2_000_000, transcendentals=0),
     )(
@@ -312,48 +317,63 @@
         *source,
         weights,
     )
+    other_source = swap(emb_source, "c", 2, 1)
+
+    (emb_target,) = call(
+        target_kernel,
+        [((COLS, D), bf16)],
+        [pltpu.VMEM((BLOCK, D), bf16)] * 3,
+        [SMEM()] * 3 + [VMEM()] * 9,
+        pl.CostEstimate(flops=2_400_000_000, bytes_accessed=4_000_000, transcendentals=0),
+    )(me[None], own_links, other_links, *own, *other, weights)
 
     scores, send = call(
-        target_kernel,
-        [((COL_BLOCKS, ROWS, LANES), f32), ((N_TGT, 8, LANES), f32)],
-        [pltpu.VMEM((COLS, D), bf16)] * 4,
-        [SMEM()] * 3 + [VMEM()] * 10,
-    )(me[None], own_links, other_links, *own, *other, weights, emb_source)
-
-    got = exchange(send, ("y", "zl"))
-    spread_weights, tops, lse, source_first = call(
+        score_kernel,
+        [((COL_BLOCKS, ROWS, LANES), f32), ((N_ROW_PEERS, 2 * ROW_BLOCKS, LANES), f32)],
+        [pltpu.VMEM((ROWS, D), bf16)],
+        [SMEM()] + [VMEM()] * 3,
+    )(me[None], emb_source, other_source, emb_target)
+
+    got = exchange(send, ("c", "y", "zl"))
+    spread_weights, tops, send, source_first = call(
         column_kernel,
         [
             ((COL_BLOCKS, ROWS, LANES), f32),
             ((COL_BLOCKS, 8, LANES), f32),
-            ((COL_BLOCKS, LANES), f32),
-            ((8, LANES), f32),
+            ((N_PEERS, COL_BLOCKS, LANES), f32),
+            ((ROW_BLOCKS, LANES), f32),
         ],
         [pltpu.VMEM((ROWS, LANES), f32)],
         [VMEM()] * 2,
     )(scores, got)
 
-    lse = jnp.logaddexp(lse, swap(lse, "c", 2, 1))
-    got = exchange(jnp.broadcast_to(lse, (N_PEERS, COL_BLOCKS, LANES)), ("zh", "x"))
+    got = exchange(send, ("zh", "x"))
     send, target_first, scale = call(
         row_kernel,
-        [((N_TGT, 8, LANES), f32), ((COL_BLOCKS, LANES), f32), ((COL_BLOCKS, 8, LANES), f32)],
+        [((N_ROW_PEERS, ROW_BLOCKS, LANES), f32), ((COL_BLOCKS, LANES), f32), ((COL_BLOCKS, 8, LANES), f32)],
         [],
         [VMEM()] * 3,
     )(spread_weights, tops, got)
 
-    got = exchange(send, ("y", "zl"))
+    got = exchange(send, ("c", "y", "zl"))
     sums, source_potential = call(
         last_kernel,
-        [((N_PEERS, COL_BLOCKS, LANES), f32), ((8, LANES), f32)],
+        [((N_PEERS, COL_BLOCKS, LANES), f32), ((ROW_BLOCKS, LANES), f32)],
         [pltpu.VMEM((ROWS, LANES), f32)],
         [VMEM()] * 4,
     )(spread_weights, scale, got, source_first)
 
     total = jnp.sum(exchange(sums, ("zh", "x")), axis=0)
-    total = total + swap(total, "c", 2, 1)
-    target_potential = target_first + (LOG_N - jnp.log(total))
-    return source_potential[0:4].reshape(ROWS), target_potential.reshape(COLS)
+    half = target_first + (LOG_N - jnp.log(total))
+    other_half = swap(half, "c", 2, 1)
+    first = (me & 1) == 0
+    even, odd = jnp.where(first, half, other_half), jnp.where(first, other_half, half)
+    target_potential = jnp.concatenate(
+        [jnp.concatenate([v[:, at : at + PART] for v in (even, odd)], axis=1) for at in (0, PART)], axis=0
+    )
+    rows = ROW_BLOCKS // 2
+    source_potential = jnp.where(first, source_potential[:rows], source_potential[rows:])
+    return source_potential.reshape(OWN_ROWS), target_potential.reshape(BLOCK)
 
 
 def solution(mesh):

time: 104 us -> 105 us (level)
  blocking collectives: 43.4 us -> 34.1 us
  waiting for transfers between devices: 10.1 us -> 18.9 us
  local copies, waits for them, and re-layouts: 1.15 us -> 2.37 us
    all_to_all x4 -> x3, blocking collectives: 43.4 us -> 34.1 us  [exchange(): return lax.all_to_all(value, axes, 0, 0)]
    all_to_all x0 -> x1, waiting for transfers between devices: none -> 8.87 us  [exchange(): return lax.all_to_all(value, axes, 0, 0)]
    all_to_all x0 -> x1, starting transfers between devices: none -> 3.48 us  [exchange(): return lax.all_to_all(value, axes, 0, 0)]
    ppermute x17, starting transfers between devices: 32.8 us -> 29.5 us  [swap(): return lax.ppermute(value, axis, [(i, i ^ xor) for i in range(size)])]
    unnamed x4 -> x8, local copies, waits for them, and re-layouts: 0.01 us -> 1.67 us
    pallas_call x4 -> x5, Pallas kernels: 10.5 us -> 10.4 us  [the longest x1 5.06 us: on_device(): call(target_kernel, [((COLS, D), bf16)], [pltpu.VMEM((BLOCK, D), bf16)] *...]
  transfers between devices with their start and end apart: 17 -> 18, of which waited for: 6 -> 7; matrix products, arithmetic and copies ran while one was open for 3% -> 3% of each run, Pallas kernels for 2% -> 7%
where the time goes in v6:
time: 105 us
  blocking collectives  34.1 us (32%)
  starting transfers between devices  33 us (31%)
  waiting for transfers between devices  18.9 us (18%)
  Pallas kernels  13.1 us (12%)
  other arithmetic  2.85 us (3%)
  local copies, waits for them, and re-layouts  2.37 us (2%)
    all_to_all x3, blocking collectives, exchange(): return lax.all_to_all(value, axes, 0, 0)  34.1 us
    ppermute x17, starting transfers between devices, swap(): return lax.ppermute(value, axis, [(i, i ^ xor) for i in range(size)])  29.5 us
    ppermute x17, waiting for transfers between devices, swap(): return lax.ppermute(value, axis, [(i, i ^ xor) for i in range(size)])  10 us
    all_to_all x1, waiting for transfers between devices, exchange(): return lax.all_to_all(value, axes, 0, 0)  8.87 us
    pallas_call x1, Pallas kernels, on_device(): call(target_kernel, [((COLS, D), bf16)], [pltpu.VMEM((BLOCK, D), bf16)] *...  5.06 us
    all_to_all x1, starting transfers between devices, exchange(): return lax.all_to_all(value, axes, 0, 0)  3.48 us
  transfers between devices with their start and end apart: 18, of which 7 were waited for; matrix products, arithmetic and copies ran while one was open for 3% of the time, Pallas kernels for 7%

profile of v6, /device:TPU:1, one launch (start us, length us, event | category | flops | bytes accessed | tf_op | source)
XLA Modules:
  0.0 105.0 jit_solution(2469811408113292669)
XLA Ops:
  0.6 1.6 %shard_map.113 = (bf16[1,272,128]{2,1,0:T(8,128)(2,1)}, bf16[1,272,128]{2,1,0:T(8,128)(2,1)}) custom-call(bf16[1,64,384]{2,1,0:T(8,128)(2,1)} %refs_0_.1, bf16[1,64,128]{2,1,0:T(8,128)(2,1)} %refs_1_.1, s32[1,1,2]{2,1,0:T(1,128)} %refs_2_.1, bf16[1,64,384]{2,1,0:T(8,128)(2,1)} %refs_3_.1, bf16[1,64,128]{2,1,0:T(8,128)(2,1)} %refs_4_.1, s32[1,1,2]{2,1,0:T(1,128)} %refs_5_.1), custom_call_target="tpu_custom_call" | custom-call | tf_op jit(solution)/shard_map/pallas_call | solution.py:50
  2.3 6.9 %collective-permute-start.2 = (bf16[1,272,128]{2,1,0:T(8,128)(2,1)}, bf16[1,272,128]{2,1,0:T(8,128)(2,1)S(1)}, u32[]{:S(2)}, u32[]{:S(2)}) collective-permute-start(bf16[1,272,128]{2,1,0:T(8,128)(2,1)} %get-tuple-element.33), channel_id=1, source_target_pairs={{0,192},{64,128},{128,64},{192,0},{1,193},{65,129},{129,65},{193,1... | collective-permute-start | bytes 208904 | tf_op jit(solution)/shard_map/ppermute | solution.py:273
  9.2 1.2 %collective-permute-start.1 = (bf16[1,272,128]{2,1,0:T(8,128)(2,1)}, bf16[1,272,128]{2,1,0:T(8,128)(2,1)S(1)}, u32[]{:S(2)}, u32[]{:S(2)}) collective-permute-start(bf16[1,272,128]{2,1,0:T(8,128)(2,1)} %get-tuple-element.33), channel_id=1, source_target_pairs={{0,64},{64,0},{128,192},{192,128},{1,65},{65,1},{129,193},{193,129... | collective-permute-start | bytes 208904 | tf_op jit(solution)/shard_map/ppermute | solution.py:273
  10.4 1.0 collective-permute-start
  11.4 0.7 collective-permute-start.3
  12.2 1.3 %pad_maximum_fusion.weights = bf16[1536,384]{1,0:T(8,128)(2,1)S(1)} fusion(bf16[384,384]{1,0:T(8,128)(2,1)} %param.19, bf16[384,384]{1,0:T(8,128)(2,1)} %param.18, bf16[384,384]{1,0:T(8,128)(2,1)} %param.17, bf16[384,384]{1,0:T(8,128)(2,1)} %param.16), kind=kLoop, calls=%fused_computation | loop fusion | flops 4718592 | bytes 2359296 | tf_op jit(solution)/shard_map/concatenate | solution.py:297
  13.5 5.0 %collective-permute-done.3 = bf16[1,272,128]{2,1,0:T(8,128)(2,1)S(1)} collective-permute-done((bf16[1,272,128]{2,1,0:T(8,128)(2,1)}, bf16[1,272,128]{2,1,0:T(8,128)(2,1)S(1)}, u32[]{:S(2)}, u32[]{:S(2)}) %collective-permute-start.3) | collective-permute-done | bytes 69664 | tf_op jit(solution)/shard_map/ppermute | solution.py:273
  18.6 0.0 collective-permute-done.2
  18.6 0.2 collective-permute-done
  18.8 2.8 %collective-permute-start.9 = (bf16[2,272,128]{2,1,0:T(8,128)(2,1)S(1)}, bf16[2,272,128]{2,1,0:T(8,128)(2,1)S(1)}, u32[]{:S(2)}, u32[]{:S(2)}) collective-permute-start(bf16[2,272,128]{2,1,0:T(8,128)(2,1)S(1)} %pad_maximum_fusion.2.own0), channel_id=1, source_target_pairs={{0,6},{2,4},{4,2},{6,0},{1,7},{3,5},{5,3},{7,1},{8,14},{10,12},{12... | collective-permute-start | bytes 417800 | tf_op jit(solution)/shard_map/ppermute | solution.py:273
  21.6 2.5 %collective-permute-start.6 = (bf16[4,272,128]{2,1,0:T(8,128)(2,1)S(1)}, bf16[4,272,128]{2,1,0:T(8,128)(2,1)S(1)}, u32[]{:S(2)}, u32[]{:S(2)}) collective-permute-start(bf16[4,272,128]{2,1,0:T(8,128)(2,1)S(1)} %pad_maximum_fusion.1.own0), channel_id=1, source_target_pairs={{0,48},{16,32},{32,16},{48,0},{1,49},{17,33},{33,17},{49,1},{2,50}... | collective-permute-start | bytes 835592 | tf_op jit(solution)/shard_map/ppermute | solution.py:273
  24.1 1.4 %collective-permute-start.4 = (bf16[4,272,128]{2,1,0:T(8,128)(2,1)S(1)}, bf16[4,272,128]{2,1,0:T(8,128)(2,1)S(1)}, u32[]{:S(2)}, u32[]{:S(2)}) collective-permute-start(bf16[4,272,128]{2,1,0:T(8,128)(2,1)S(1)} %pad_maximum_fusion.1.own0), channel_id=1, source_target_pairs={{0,32},{16,48},{32,0},{48,16},{1,33},{17,49},{33,1},{49,17},{2,34}... | collective-permute-start | bytes 835592 | tf_op jit(solution)/shard_map/ppermute | solution.py:273
  25.5 1.3 %collective-permute-start.7 = (bf16[2,272,128]{2,1,0:T(8,128)(2,1)S(1)}, bf16[2,272,128]{2,1,0:T(8,128)(2,1)S(1)}, u32[]{:S(2)}, u32[]{:S(2)}) collective-permute-start(bf16[2,272,128]{2,1,0:T(8,128)(2,1)S(1)} %pad_maximum_fusion.2.own0), channel_id=1, source_target_pairs={{0,4},{2,6},{4,0},{6,2},{1,5},{3,7},{5,1},{7,3},{8,12},{10,14},{12... | collective-permute-start | bytes 417800 | tf_op jit(solution)/shard_map/ppermute | solution.py:273
  26.8 0.1 slice_reduce_fusion.3
  26.9 2.8 %collective-permute-done.8.own2 = bf16[2,272,128]{2,1,0:T(8,128)(2,1)S(1)} collective-permute-done((bf16[2,272,128]{2,1,0:T(8,128)(2,1)S(1)}, bf16[2,272,128]{2,1,0:T(8,128)(2,1)S(1)}, u32[]{:S(2)}, u32[]{:S(2)}) %collective-permute-start.8) | collective-permute-done | bytes 139296 | tf_op jit(solution)/shard_map/ppermute | solution.py:273
  29.7 4.4 %collective-permute-start.12 = (bf16[4,272,128]{2,1,0:T(8,128)(2,1)S(1)}, bf16[4,272,128]{2,1,0:T(8,128)(2,1)S(1)}, u32[]{:S(2)}, u32[]{:S(2)}) collective-permute-start(bf16[4,272,128]{2,1,0:T(8,128)(2,1)S(1)} %pad_maximum_fusion.1.own0), channel_id=1, source_target_pairs={{0,8},{8,0},{1,9},{9,1},{2,10},{10,2},{3,11},{11,3},{4,12},{12,4},... | collective-permute-start | bytes 835592 | tf_op jit(solution)/shard_map/ppermute | solution.py:273
  34.1 1.0 collective-permute-done.4.own1
  35.1 4.0 %collective-permute-start.14 = (bf16[4,272,128]{2,1,0:T(8,128)(2,1)S(1)}, bf16[4,272,128]{2,1,0:T(8,128)(2,1)}, u32[]{:S(2)}, u32[]{:S(2)}) collective-permute-start(bf16[4,272,128]{2,1,0:T(8,128)(2,1)S(1)} %collective-permute-done.5.own2), channel_id=1, source_target_pairs={{0,8},{8,0},{1,9},{9,1},{2,10},{10,2},{3,11},{11,3},{4,12},{12,4},... | collective-permute-start | bytes 835592 | tf_op jit(solution)/shard_map/ppermute | solution.py:273
  39.0 0.1 slice_reduce_fusion
  39.2 0.1 collective-permute-start.15
  39.3 0.5 collective-permute-start.13
  39.8 0.1 slice_reduce_fusion.6
  39.9 0.1 slice_reduce_fusion.4
  40.0 0.1 maximum_convert_fusion.links
  40.0 2.1 %shard_map.114.own_source = bf16[512,384]{1,0:T(8,128)(2,1)S(1)} custom-call(s32[1]{0:T(128)} %bitcast.1.place, s32[8]{0:T(128)S(1)} %maximum_convert_fusion.links, bf16[2,272,128]{2,1,0:T(8,128)(2,1)S(1)} %pad_maximum_fusion.2.own0, bf16[2,272,128]{2,1,0:T(8,128)(2,1)S(1)} %collective-permute-done.7.own1, ...), custom_call_target="tpu_custom_call" | custom-call | flops 700000000 | bytes 2000000 | tf_op jit(solution)/shard_map/pallas_call | solution.py:308
  42.1 0.2 collective-permute-start.10
  42.3 0.1 slice_reduce_fusion.2
  42.4 0.1 maximum_convert_fusion.1.own_links
  42.5 0.7 copy-done
  43.2 0.4 collective-permute-start.11
  43.6 0.8 collective-permute-done.11.other_links
  44.5 0.9 copy-done.1
  45.4 5.1 %shard_map.115.emb_target = bf16[1024,384]{1,0:T(8,128)(2,1)S(1)} custom-call(s32[1]{0:T(128)} %bitcast.place, s32[16]{0:T(128)S(1)} %maximum_convert_fusion.1.own_links, s32[16]{0:T(128)S(1)} %collective-permute-done.11.other_links, bf16[4,272,128]{2,1,0:T(8,128)(2,1)S(1)} %pad_maximum_fusion.1.own0, bf16[4,272,128]{2,1,0:T(8,128)(2,1)S(1)} %collective-permute-done.4.own1, ...), custom_call_target="tpu_custom_call" | custom-call | flops 2400000000 | bytes 4000000 | tf_op jit(solution)/shard_map/pallas_call | solution.py:322
  50.5 1.8 %shard_map.116 = (f32[8,1024,128]{2,1,0:T(8,128)S(1)}, f32[16,16,128]{2,1,0:T(8,128)S(1)}) custom-call(s32[1]{0:T(128)} %bitcast.place, bf16[512,384]{1,0:T(8,128)(2,1)S(1)} %shard_map.114.own_source, bf16[512,384]{1,0:T(8,128)(2,1)S(1)} %collective-permute-done.10.other_source, bf16[1024,384]{1,0:T(8,128)(2,1)S(1)} %shard_map.115.emb_target), custom_call_target="tpu_custom_call" | custom-call | tf_op jit(solution)/shard_map/pallas_call | solution.py:330
  52.3 8.5 %all_to_all.20.got = f32[16,16,128]{2,1,0:T(8,128)S(1)} all-to-all(f32[16,16,128]{2,1,0:T(8,128)S(1)} %get-tuple-element.50), channel_id=1, replica_groups=mesh['zh'=4,'x'=4,'c'=2,'y'=4,'zl'=2] {'c','y','zl'}, dimensions={0} | all-to-all | bytes 262144 | tf_op jit(solution)/shard_map/all_to_all | solution.py:282
  60.8 1.1 %shard_map.117 = (f32[8,1024,128]{2,1,0:T(8,128)S(1)}, f32[8,8,128]{2,1,0:T(8,128)S(1)}, f32[16,8,128]{2,1,0:T(8,128)S(1)}, f32[8,128]{1,0:T(8,128)S(1)}) custom-call(f32[8,1024,128]{2,1,0:T(8,128)S(1)} %get-tuple-element.49.scores, f32[16,16,128]{2,1,0:T(8,128)S(1)} %all_to_all.20.got), custom_call_target="tpu_custom_call" | custom-call | tf_op jit(solution)/shard_map/pallas_call | solution.py:338
  61.9 15.0 %all_to_all.21.got = f32[16,8,128]{2,1,0:T(8,128)S(1)} all-to-all(f32[16,8,128]{2,1,0:T(8,128)S(1)} %get-tuple-element.53), channel_id=1, replica_groups=mesh['zh'=4,'x'=4,'c'=2,'y'=4,'zl'=2] {'zh','x'}, dimensions={0} | all-to-all | bytes 131072 | tf_op jit(solution)/shard_map/all_to_all | solution.py:282
  76.9 0.4 shard_map.118
  77.3 10.5 %all_to_all.22.got = f32[16,8,128]{2,1,0:T(8,128)S(1)} all-to-all(f32[16,8,128]{2,1,0:T(8,128)S(1)} %get-tuple-element.55), channel_id=1, replica_groups=mesh['zh'=4,'x'=4,'c'=2,'y'=4,'zl'=2] {'c','y','zl'}, dimensions={0} | all-to-all | bytes 131072 | tf_op jit(solution)/shard_map/all_to_all | solution.py:282
  87.8 1.0 shard_map.119
  88.9 3.5 %all-to-all-start.3 = ((f32[16,8,128]{2,1,0:T(8,128)}), f32[16,8,128]{2,1,0:T(8,128)S(1)}, u32[]{:S(2)}, u32[]{:S(2)}) async-start(f32[16,8,128]{2,1,0:T(8,128)} %get-tuple-element.59), calls=%async_computation.3 | async-start | bytes 131072 | tf_op jit(solution)/shard_map/all_to_all | solution.py:282
  92.4 8.9 %all-to-all-done.3 = f32[16,8,128]{2,1,0:T(8,128)S(1)} async-done(((f32[16,8,128]{2,1,0:T(8,128)}), f32[16,8,128]{2,1,0:T(8,128)S(1)}, u32[]{:S(2)}, u32[]{:S(2)}) %all-to-all-start.3) | async-done | bytes 65568 | tf_op jit(solution)/shard_map/all_to_all | solution.py:282
  101.3 2.1 %collective-permute-start.16 = (f32[8,128]{1,0:T(8,128)S(1)}, f32[8,128]{1,0:T(8,128)S(1)}, u32[]{:S(2)}, u32[]{:S(2)}) collective-permute-start(f32[8,128]{1,0:T(8,128)S(1)} %subtract_add_fusion), channel_id=1, source_target_pairs={{0,8},{8,0},{1,9},{9,1},{2,10},{10,2},{3,11},{11,3},{4,12},{12,4},... | collective-permute-start | bytes 12296 | tf_op jit(solution)/shard_map/ppermute | solution.py:273
  103.4 0.6 select_bitcast_fusion
  104.0 0.2 collective-permute-done.16
  104.2 0.1 fusion
  104.3 0.1 fusion.1
  104.4 0.7 maximum_bitcast_fusion
  (23 shorter events, 0.1 us)
Async XLA Ops:
  2.3 16.3 %copy-start.3 = (bf16[1,272,128]{2,1,0:T(8,128)(2,1)S(1)}, bf16[1,272,128]{2,1,0:T(8,128)(2,1)}, u32[]{:S(2)}) copy-start(bf16[1,272,128]{2,1,0:T(8,128)(2,1)} %get-tuple-element.34) | copy-start | bytes 208900
  2.3 16.5 %copy-start.2 = (bf16[1,272,128]{2,1,0:T(8,128)(2,1)S(1)}, bf16[1,272,128]{2,1,0:T(8,128)(2,1)}, u32[]{:S(2)}) copy-start(bf16[1,272,128]{2,1,0:T(8,128)(2,1)} %get-tuple-element.33) | copy-start | bytes 208900
  2.3 16.3 %collective-permute-start.2 = (bf16[1,272,128]{2,1,0:T(8,128)(2,1)}, bf16[1,272,128]{2,1,0:T(8,128)(2,1)S(1)}, u32[]{:S(2)}, u32[]{:S(2)}) collective-permute-start(bf16[1,272,128]{2,1,0:T(8,128)(2,1)} %get-tuple-element.33), channel_id=1, source_target_pairs={{0,192},{64,128},{128,64},{192,0},{1,193},{65,129},{129,65},{193,1... | collective-permute-start | bytes 208904 | tf_op jit(solution)/shard_map/ppermute | solution.py:273
  9.2 9.3 %collective-permute-start.1 = (bf16[1,272,128]{2,1,0:T(8,128)(2,1)}, bf16[1,272,128]{2,1,0:T(8,128)(2,1)S(1)}, u32[]{:S(2)}, u32[]{:S(2)}) collective-permute-start(bf16[1,272,128]{2,1,0:T(8,128)(2,1)} %get-tuple-element.33), channel_id=1, source_target_pairs={{0,64},{64,0},{128,192},{192,128},{1,65},{65,1},{129,193},{193,129... | collective-permute-start | bytes 208904 | tf_op jit(solution)/shard_map/ppermute | solution.py:273
  10.4 8.3 %collective-permute-start = (bf16[1,272,128]{2,1,0:T(8,128)(2,1)}, bf16[1,272,128]{2,1,0:T(8,128)(2,1)S(1)}, u32[]{:S(2)}, u32[]{:S(2)}) collective-permute-start(bf16[1,272,128]{2,1,0:T(8,128)(2,1)} %get-tuple-element.33), channel_id=1, source_target_pairs={{0,128},{64,192},{128,0},{192,64},{1,129},{65,193},{129,1},{193,65... | collective-permute-start | bytes 208904 | tf_op jit(solution)/shard_map/ppermute | solution.py:273
  11.4 7.1 %collective-permute-start.3 = (bf16[1,272,128]{2,1,0:T(8,128)(2,1)}, bf16[1,272,128]{2,1,0:T(8,128)(2,1)S(1)}, u32[]{:S(2)}, u32[]{:S(2)}) collective-permute-start(bf16[1,272,128]{2,1,0:T(8,128)(2,1)} %get-tuple-element.34), channel_id=1, source_target_pairs={{0,1},{1,0},{2,3},{3,2},{4,5},{5,4},{6,7},{7,6},{8,9},{9,8},{10,11... | collective-permute-start | bytes 208904 | tf_op jit(solution)/shard_map/ppermute | solution.py:273
  18.8 6.7 %collective-permute-start.9 = (bf16[2,272,128]{2,1,0:T(8,128)(2,1)S(1)}, bf16[2,272,128]{2,1,0:T(8,128)(2,1)S(1)}, u32[]{:S(2)}, u32[]{:S(2)}) collective-permute-start(bf16[2,272,128]{2,1,0:T(8,128)(2,1)S(1)} %pad_maximum_fusion.2.own0), channel_id=1, source_target_pairs={{0,6},{2,4},{4,2},{6,0},{1,7},{3,5},{5,3},{7,1},{8,14},{10,12},{12... | collective-permute-start | bytes 417800 | tf_op jit(solution)/shard_map/ppermute | solution.py:273
  21.6 12.5 %collective-permute-start.6 = (bf16[4,272,128]{2,1,0:T(8,128)(2,1)S(1)}, bf16[4,272,128]{2,1,0:T(8,128)(2,1)S(1)}, u32[]{:S(2)}, u32[]{:S(2)}) collective-permute-start(bf16[4,272,128]{2,1,0:T(8,128)(2,1)S(1)} %pad_maximum_fusion.1.own0), channel_id=1, source_target_pairs={{0,48},{16,32},{32,16},{48,0},{1,49},{17,33},{33,17},{49,1},{2,50}... | collective-permute-start | bytes 835592 | tf_op jit(solution)/shard_map/ppermute | solution.py:273
  24.1 10.0 %collective-permute-start.5 = (bf16[4,272,128]{2,1,0:T(8,128)(2,1)S(1)}, bf16[4,272,128]{2,1,0:T(8,128)(2,1)S(1)}, u32[]{:S(2)}, u32[]{:S(2)}) collective-permute-start(bf16[4,272,128]{2,1,0:T(8,128)(2,1)S(1)} %pad_maximum_fusion.1.own0), channel_id=1, source_target_pairs={{0,16},{16,0},{32,48},{48,32},{1,17},{17,1},{33,49},{49,33},{2,18}... | collective-permute-start | bytes 835592 | tf_op jit(solution)/shard_map/ppermute | solution.py:273
  24.1 11.0 %collective-permute-start.4 = (bf16[4,272,128]{2,1,0:T(8,128)(2,1)S(1)}, bf16[4,272,128]{2,1,0:T(8,128)(2,1)S(1)}, u32[]{:S(2)}, u32[]{:S(2)}) collective-permute-start(bf16[4,272,128]{2,1,0:T(8,128)(2,1)S(1)} %pad_maximum_fusion.1.own0), channel_id=1, source_target_pairs={{0,32},{16,48},{32,0},{48,16},{1,33},{17,49},{33,1},{49,17},{2,34}... | collective-permute-start | bytes 835592 | tf_op jit(solution)/shard_map/ppermute | solution.py:273
  25.5 4.2 %collective-permute-start.8 = (bf16[2,272,128]{2,1,0:T(8,128)(2,1)S(1)}, bf16[2,272,128]{2,1,0:T(8,128)(2,1)S(1)}, u32[]{:S(2)}, u32[]{:S(2)}) collective-permute-start(bf16[2,272,128]{2,1,0:T(8,128)(2,1)S(1)} %pad_maximum_fusion.2.own0), channel_id=1, source_target_pairs={{0,2},{2,0},{4,6},{6,4},{1,3},{3,1},{5,7},{7,5},{8,10},{10,8},{12,... | collective-permute-start | bytes 417800 | tf_op jit(solution)/shard_map/ppermute | solution.py:273
  25.5 8.6 %collective-permute-start.7 = (bf16[2,272,128]{2,1,0:T(8,128)(2,1)S(1)}, bf16[2,272,128]{2,1,0:T(8,128)(2,1)S(1)}, u32[]{:S(2)}, u32[]{:S(2)}) collective-permute-start(bf16[2,272,128]{2,1,0:T(8,128)(2,1)S(1)} %pad_maximum_fusion.2.own0), channel_id=1, source_target_pairs={{0,4},{2,6},{4,0},{6,2},{1,5},{3,7},{5,1},{7,3},{8,12},{10,14},{12... | collective-permute-start | bytes 417800 | tf_op jit(solution)/shard_map/ppermute | solution.py:273
  29.7 12.9 %collective-permute-start.12 = (bf16[4,272,128]{2,1,0:T(8,128)(2,1)S(1)}, bf16[4,272,128]{2,1,0:T(8,128)(2,1)S(1)}, u32[]{:S(2)}, u32[]{:S(2)}) collective-permute-start(bf16[4,272,128]{2,1,0:T(8,128)(2,1)S(1)} %pad_maximum_fusion.1.own0), channel_id=1, source_target_pairs={{0,8},{8,0},{1,9},{9,1},{2,10},{10,2},{3,11},{11,3},{4,12},{12,4},... | collective-permute-start | bytes 835592 | tf_op jit(solution)/shard_map/ppermute | solution.py:273
  35.1 9.4 %collective-permute-start.14 = (bf16[4,272,128]{2,1,0:T(8,128)(2,1)S(1)}, bf16[4,272,128]{2,1,0:T(8,128)(2,1)}, u32[]{:S(2)}, u32[]{:S(2)}) collective-permute-start(bf16[4,272,128]{2,1,0:T(8,128)(2,1)S(1)} %collective-permute-done.5.own2), channel_id=1, source_target_pairs={{0,8},{8,0},{1,9},{9,1},{2,10},{10,2},{3,11},{11,3},{4,12},{12,4},... | collective-permute-start | bytes 835592 | tf_op jit(solution)/shard_map/ppermute | solution.py:273
  39.2 5.3 %collective-permute-start.15 = (bf16[4,272,128]{2,1,0:T(8,128)(2,1)S(1)}, bf16[4,272,128]{2,1,0:T(8,128)(2,1)}, u32[]{:S(2)}, u32[]{:S(2)}) collective-permute-start(bf16[4,272,128]{2,1,0:T(8,128)(2,1)S(1)} %collective-permute-done.6.own3), channel_id=1, source_target_pairs={{0,8},{8,0},{1,9},{9,1},{2,10},{10,2},{3,11},{11,3},{4,12},{12,4},... | collective-permute-start | bytes 835592 | tf_op jit(solution)/shard_map/ppermute | solution.py:273
  39.3 5.2 %collective-permute-start.13 = (bf16[4,272,128]{2,1,0:T(8,128)(2,1)S(1)}, bf16[4,272,128]{2,1,0:T(8,128)(2,1)}, u32[]{:S(2)}, u32[]{:S(2)}) collective-permute-start(bf16[4,272,128]{2,1,0:T(8,128)(2,1)S(1)} %collective-permute-done.4.own1), channel_id=1, source_target_pairs={{0,8},{8,0},{1,9},{9,1},{2,10},{10,2},{3,11},{11,3},{4,12},{12,4},... | collective-permute-start | bytes 835592 | tf_op jit(solution)/shard_map/ppermute | solution.py:273
  42.1 8.4 %collective-permute-start.10 = (bf16[512,384]{1,0:T(8,128)(2,1)S(1)}, bf16[512,384]{1,0:T(8,128)(2,1)S(1)}, u32[]{:S(2)}, u32[]{:S(2)}) collective-permute-start(bf16[512,384]{1,0:T(8,128)(2,1)S(1)} %shard_map.114.own_source), channel_id=1, source_target_pairs={{0,8},{8,0},{1,9},{9,1},{2,10},{10,2},{3,11},{11,3},{4,12},{12,4},... | collective-permute-start | bytes 1179656 | tf_op jit(solution)/shard_map/ppermute | solution.py:273
  42.5 0.7 copy-start
  43.2 1.2 %collective-permute-start.11 = (s32[16]{0:T(128)S(1)}, s32[16]{0:T(128)S(1)}, u32[]{:S(2)}, u32[]{:S(2)}) collective-permute-start(s32[16]{0:T(128)S(1)} %maximum_convert_fusion.1.own_links), channel_id=1, source_target_pairs={{0,8},{8,0},{1,9},{9,1},{2,10},{10,2},{3,11},{11,3},{4,12},{12,4},... | collective-permute-start | bytes 200 | tf_op jit(solution)/shard_map/ppermute | solution.py:273
  44.5 1.0 copy-start.1
  88.9 12.4 %all-to-all-start.3 = ((f32[16,8,128]{2,1,0:T(8,128)}), f32[16,8,128]{2,1,0:T(8,128)S(1)}, u32[]{:S(2)}, u32[]{:S(2)}) async-start(f32[16,8,128]{2,1,0:T(8,128)} %get-tuple-element.59), calls=%async_computation.3 | async-start | bytes 131072 | tf_op jit(solution)/shard_map/all_to_all | solution.py:282
  101.3 2.9 %collective-permute-start.16 = (f32[8,128]{1,0:T(8,128)S(1)}, f32[8,128]{1,0:T(8,128)S(1)}, u32[]{:S(2)}, u32[]{:S(2)}) collective-permute-start(f32[8,128]{1,0:T(8,128)S(1)} %subtract_add_fusion), channel_id=1, source_target_pairs={{0,8},{8,0},{1,9},{9,1},{2,10},{10,2},{3,11},{11,3},{4,12},{12,4},... | collective-permute-start | bytes 12296 | tf_op jit(solution)/shard_map/ppermute | solution.py:273

commit v7 on v6

--- a/solution.py
+++ b/solution.py
@@ -22,7 +22,7 @@
 STEP = 512
 N_PEERS = 16
 LOG_N = math.log(16384.0)
-VMEM_LIMIT = 32 * 1024 * 1024
+VMEM_LIMIT = 18 * 1024 * 1024
 PACK_LIMIT = 60 * 1024 * 1024
 
 VMEM = functools.partial(pl.BlockSpec, memory_space=pltpu.VMEM)
@@ -56,20 +56,30 @@
     )(*arrays)
 
 
-def graph_layers(packed, first, second, weights, x_ref, s_ref, h_ref, emit, wanted):
+def graph_layers(packed, first, second, weights, x_ref, s_ref, h_ref, row_ref, link_ref, sem, emit, wanted):
     count = x_ref.shape[0] // PART
+    lane = lax.broadcasted_iota(jnp.int32, (8, LANES), 1)
+    row = jnp.zeros((8, LANES), jnp.int32)
+    for k in range(count):
+        ref, at = packed(k)
+        link = ref[at, 4 * PART : PACK, :].astype(jnp.float32)[0:8]
+        row = jnp.where(lane == k, link.astype(jnp.int32), row)
+    row_ref[...] = row
+    copy = pltpu.make_async_copy(row_ref, link_ref, sem)
+    copy.start()
     for k in range(count):
         ref, at = packed(k)
         for piece in range(D // LANES):
             x_ref[k * PART : (k + 1) * PART, piece * LANES : (piece + 1) * LANES] = ref[
                 at, piece * PART : (piece + 1) * PART, :
             ]
+    copy.wait()
 
     def neighbour_sums(src, count):
         for k in range(count):
             ref, at = packed(k)
             near = src[pl.ds(first(k) * PART, PART), :]
-            other = src[pl.ds(pl.multiple_of(second(k) * PART, PART), PART), :]
+            other = src[pl.ds(pl.multiple_of(second(link_ref[0, k]) * PART, PART), PART), :]
             panel = ref[at, 3 * PART : 4 * PART, :]
             both = jnp.concatenate([near, other], axis=0)
             total = jnp.dot(panel, both, preferred_element_type=jnp.float32)
@@ -100,7 +110,7 @@
     return turn(v >> 3) | (turn((v >> 1) & 3) << 2) | ((v & 1) << 4)
 
 
-def source_kernel(place, links, own0, own1, own2, own3, weights, out, x_ref, s_ref, h_ref):
+def source_kernel(place, own0, own1, own2, own3, weights, out, *scratch):
     me = place[0]
     pieces = (own0, own1, own2, own3)
 
@@ -113,8 +123,8 @@
     graph_layers(
         lambda k: (pieces[k // 2], k % 2),
         lambda k: k ^ 7,
-        lambda k: (turn((links[k] ^ me) >> 1) << 1) | ((links[k] ^ me) & 1),
-        weights, x_ref, s_ref, h_ref, emit, 8,
+        lambda link: (turn((link ^ me) >> 1) << 1) | ((link ^ me) & 1),
+        weights, *scratch, emit, 8,
     )
 
 
@@ -123,10 +133,7 @@
 
 
 def target_kernel(
-    place, own_links, other_links,
-    own0, own1, own2, own3, other0, other1, other2, other3,
-    weights,
-    out, x_ref, s_ref, h_ref,
+    place, own0, own1, own2, own3, other0, other1, other2, other3, weights, out, *scratch
 ):
     me = place[0]
     pieces = (own0, own1, own2, own3, other0, other1, other2, other3)
@@ -140,8 +147,8 @@
     graph_layers(
         lambda k: (pieces[k // 4], k % 4),
         lambda k: k ^ 31,
-        lambda k: slot_of((own_links[k] if k < 16 else other_links[k - 16]) ^ me),
-        weights, x_ref, s_ref, h_ref, emit, 16,
+        lambda link: slot_of(link ^ me),
+        weights, *scratch, emit, 16,
     )
 
 
@@ -178,7 +185,7 @@
                 send[d, ROW_BLOCKS + b : ROW_BLOCKS + b + 1, :] = part_total
 
 
-def column_kernel(scores, got, weights, tops, send, potential, shift):
+def column_kernel(scores, got, weights, tops, send, potential):
     top, total = got[0, 0:ROW_BLOCKS, :], got[0, ROW_BLOCKS:, :]
     larger = top
     for d in range(1, N_ROW_PEERS):
@@ -188,18 +195,18 @@
         total += got[d, ROW_BLOCKS:, :] * jnp.exp(got[d, 0:ROW_BLOCKS, :] - larger)
     source = LOG_N - (larger + jnp.log(total))
     potential[...] = source
+    peaks = [None] * COL_BLOCKS
     for b in range(ROW_BLOCKS):
-        shift[pl.ds(b * LANES, LANES), :] = spread(source[b : b + 1, :])
-
+        rows = pl.ds(b * LANES, LANES)
+        shift = spread(source[b : b + 1, :])
+        for i in range(COL_BLOCKS):
+            x = scores[i, rows, :] + shift
+            weights[i, rows, :] = x
+            peak = jnp.max(x.reshape(LANES // 8, 8, LANES), axis=0)
+            peaks[i] = peak if b == 0 else jnp.maximum(peaks[i], peak)
     step = 64
     for i in range(COL_BLOCKS):
-        top = None
-        for at in range(0, ROWS, step):
-            rows = pl.ds(at, step)
-            x = scores[i, rows, :] + shift[rows, :]
-            weights[i, rows, :] = x
-            larger = jnp.max(x.reshape(step // 8, 8, LANES), axis=0)
-            top = larger if top is None else jnp.maximum(top, larger)
+        top = peaks[i]
         total = jnp.zeros((8, LANES), jnp.float32)
         for at in range(0, ROWS, step):
             rows = pl.ds(at, step)
@@ -236,23 +243,21 @@
             send[d, b : b + 1, :] = total
 
 
-def last_kernel(weights, scale, got, before, sums, potential, factor):
+def last_kernel(weights, scale, got, before, sums, potential):
     total = got[0]
     for d in range(1, N_ROW_PEERS):
         total += got[d]
     potential[...] = before[...] + (LOG_N - jnp.log(total))
     ratio = 16384.0 / total
+    parts = [jnp.zeros((8, LANES), jnp.float32)] * COL_BLOCKS
     for b in range(ROW_BLOCKS):
-        factor[pl.ds(b * LANES, LANES), :] = spread(ratio[b : b + 1, :])
-
-    step = 64
+        rows = pl.ds(b * LANES, LANES)
+        factor = spread(ratio[b : b + 1, :])
+        for i in range(COL_BLOCKS):
+            e = (weights[i, rows, :] * factor).reshape(LANES // 8, 8, LANES)
+            parts[i] += jnp.sum(e, axis=0)
     for i in range(COL_BLOCKS):
-        total = jnp.zeros((8, LANES), jnp.float32)
-        for at in range(0, ROWS, step):
-            rows = pl.ds(at, step)
-            e = weights[i, rows, :] * factor[rows, :]
-            total += jnp.sum(e.reshape(step // 8, 8, LANES), axis=0)
-        total = jnp.sum(total * scale[i], axis=0, keepdims=True)
+        total = jnp.sum(parts[i] * scale[i], axis=0, keepdims=True)
         for d in range(N_PEERS):
             sums[d, i : i + 1, :] = total
 
@@ -269,6 +274,14 @@
     )
 
 
+def graph_scratch(rows):
+    return [pltpu.VMEM((rows, D), jnp.bfloat16)] * 3 + [
+        pltpu.VMEM((8, LANES), jnp.int32),
+        pltpu.SMEM((8, LANES), jnp.int32),
+        pltpu.SemaphoreType.DMA,
+    ]
+
+
 def swap(value, axis, size, xor):
     return lax.ppermute(value, axis, [(i, i ^ xor) for i in range(size)])
 
@@ -302,18 +315,15 @@
     own = direct(held, "x")
     own[1:], source = lax.optimization_barrier((own[1:], source))
     other = [swap(piece, "c", 2, 1) for piece in own]
-    own_links = jnp.concatenate([piece[:, 4 * PART, 0] for piece in own]).astype(jnp.int32)
-    other_links = swap(own_links, "c", 2, 1)
 
     (emb_source,) = call(
         source_kernel,
         [((OWN_ROWS, D), bf16)],
-        [pltpu.VMEM((OWN_ROWS, D), bf16)] * 3,
-        [SMEM()] * 2 + [VMEM()] * 5,
+        graph_scratch(OWN_ROWS),
+        [SMEM()] + [VMEM()] * 5,
         pl.CostEstimate(flops=700_000_000, bytes_accessed=2_000_000, transcendentals=0),
     )(
         me_source[None],
-        jnp.concatenate([piece[:, 4 * PART, 0] for piece in source]).astype(jnp.int32),
         *source,
         weights,
     )
@@ -322,10 +332,10 @@
     (emb_target,) = call(
         target_kernel,
         [((COLS, D), bf16)],
-        [pltpu.VMEM((BLOCK, D), bf16)] * 3,
-        [SMEM()] * 3 + [VMEM()] * 9,
+        graph_scratch(BLOCK),
+        [SMEM()] + [VMEM()] * 9,
         pl.CostEstimate(flops=2_400_000_000, bytes_accessed=4_000_000, transcendentals=0),
-    )(me[None], own_links, other_links, *own, *other, weights)
+    )(me[None], *own, *other, weights)
 
     scores, send = call(
         score_kernel,
@@ -343,7 +353,7 @@
             ((N_PEERS, COL_BLOCKS, LANES), f32),
             ((ROW_BLOCKS, LANES), f32),
         ],
-        [pltpu.VMEM((ROWS, LANES), f32)],
+        [],
         [VMEM()] * 2,
     )(scores, got)
 
@@ -359,7 +369,7 @@
     sums, source_potential = call(
         last_kernel,
         [((N_PEERS, COL_BLOCKS, LANES), f32), ((ROW_BLOCKS, LANES), f32)],
-        [pltpu.VMEM((ROWS, LANES), f32)],
+        [],
         [VMEM()] * 4,
     )(spread_weights, scale, got, source_first)
 

time: 105 us -> 103 us (0.981)
  waiting for transfers between devices: 18.9 us -> 17.5 us
    ppermute x17 -> x16, waiting for transfers between devices: 10 us -> 8.67 us  [swap(): return lax.ppermute(value, axis, [(i, i ^ xor) for i in range(size)])]
    ppermute x17 -> x16, starting transfers between devices: 29.5 us -> 29.1 us  [swap(): return lax.ppermute(value, axis, [(i, i ^ xor) for i in range(size)])]
  transfers between devices with their start and end apart: 18 -> 17, of which waited for: 7 -> 6; matrix products, arithmetic and copies ran while one was open for 3% -> 2% of each run, Pallas kernels for 7% -> 7%
where the time goes in v7:
time: 103 us
  blocking collectives  34.2 us (33%)
  starting transfers between devices  32.6 us (32%)
  waiting for transfers between devices  17.5 us (17%)
  Pallas kernels  13.4 us (13%)
  other arithmetic  2.69 us (3%)
  local copies, waits for them, and re-layouts  1.65 us (2%)
    all_to_all x3, blocking collectives, exchange(): return lax.all_to_all(value, axes, 0, 0)  34.2 us
    ppermute x16, starting transfers between devices, swap(): return lax.ppermute(value, axis, [(i, i ^ xor) for i in range(size)])  29.1 us
    all_to_all x1, waiting for transfers between devices, exchange(): return lax.all_to_all(value, axes, 0, 0)  8.87 us
    ppermute x16, waiting for transfers between devices, swap(): return lax.ppermute(value, axis, [(i, i ^ xor) for i in range(size)])  8.67 us
    pallas_call x1, Pallas kernels, on_device(): call(target_kernel, [((COLS, D), bf16)], graph_scratch(BLOCK), [SMEM()] +...  5.42 us
    all_to_all x1, starting transfers between devices, exchange(): return lax.all_to_all(value, axes, 0, 0)  3.5 us
    pallas_call x1, Pallas kernels, on_device(): call(source_kernel, [((OWN_ROWS, D), bf16)], graph_scratch(OWN_ROWS), [SM...  2.1 us
  transfers between devices with their start and end apart: 17, of which 6 were waited for; matrix products, arithmetic and copies ran while one was open for 2% of the time, Pallas kernels for 7%

profile of v7, /device:TPU:1, one launch (start us, length us, event | category | flops | bytes accessed | tf_op | source)
XLA Modules:
  0.0 103.0 jit_solution(14852510422086187305)
XLA Ops:
  0.6 1.6 %shard_map.113 = (bf16[1,272,128]{2,1,0:T(8,128)(2,1)}, bf16[1,272,128]{2,1,0:T(8,128)(2,1)}) custom-call(bf16[1,64,384]{2,1,0:T(8,128)(2,1)} %refs_0_.1, bf16[1,64,128]{2,1,0:T(8,128)(2,1)} %refs_1_.1, s32[1,1,2]{2,1,0:T(1,128)} %refs_2_.1, bf16[1,64,384]{2,1,0:T(8,128)(2,1)} %refs_3_.1, bf16[1,64,128]{2,1,0:T(8,128)(2,1)} %refs_4_.1, s32[1,1,2]{2,1,0:T(1,128)} %refs_5_.1), custom_call_target="tpu_custom_call" | custom-call | tf_op jit(solution)/shard_map/pallas_call | solution.py:50
  2.3 6.9 %collective-permute-start.2 = (bf16[1,272,128]{2,1,0:T(8,128)(2,1)}, bf16[1,272,128]{2,1,0:T(8,128)(2,1)S(1)}, u32[]{:S(2)}, u32[]{:S(2)}) collective-permute-start(bf16[1,272,128]{2,1,0:T(8,128)(2,1)} %get-tuple-element.33), channel_id=1, source_target_pairs={{0,192},{64,128},{128,64},{192,0},{1,193},{65,129},{129,65},{193,1... | collective-permute-start | bytes 208904 | tf_op jit(solution)/shard_map/ppermute | solution.py:286
  9.2 1.2 %collective-permute-start.1 = (bf16[1,272,128]{2,1,0:T(8,128)(2,1)}, bf16[1,272,128]{2,1,0:T(8,128)(2,1)S(1)}, u32[]{:S(2)}, u32[]{:S(2)}) collective-permute-start(bf16[1,272,128]{2,1,0:T(8,128)(2,1)} %get-tuple-element.33), channel_id=1, source_target_pairs={{0,64},{64,0},{128,192},{192,128},{1,65},{65,1},{129,193},{193,129... | collective-permute-start | bytes 208904 | tf_op jit(solution)/shard_map/ppermute | solution.py:286
  10.4 1.0 collective-permute-start
  11.4 0.7 collective-permute-start.3
  12.2 1.3 %pad_maximum_fusion.weights = bf16[1536,384]{1,0:T(8,128)(2,1)S(1)} fusion(bf16[384,384]{1,0:T(8,128)(2,1)} %param.19, bf16[384,384]{1,0:T(8,128)(2,1)} %param.18, bf16[384,384]{1,0:T(8,128)(2,1)} %param.17, bf16[384,384]{1,0:T(8,128)(2,1)} %param.16), kind=kLoop, calls=%fused_computation | loop fusion | flops 4718592 | bytes 2359296 | tf_op jit(solution)/shard_map/concatenate | solution.py:310
  13.5 5.0 %collective-permute-done.3 = bf16[1,272,128]{2,1,0:T(8,128)(2,1)S(1)} collective-permute-done((bf16[1,272,128]{2,1,0:T(8,128)(2,1)}, bf16[1,272,128]{2,1,0:T(8,128)(2,1)S(1)}, u32[]{:S(2)}, u32[]{:S(2)}) %collective-permute-start.3) | collective-permute-done | bytes 69664 | tf_op jit(solution)/shard_map/ppermute | solution.py:286
  18.6 0.0 collective-permute-done.2
  18.6 0.0 collective-permute-done.1
  18.6 0.2 collective-permute-done
  18.8 2.8 %collective-permute-start.9 = (bf16[2,272,128]{2,1,0:T(8,128)(2,1)S(1)}, bf16[2,272,128]{2,1,0:T(8,128)(2,1)S(1)}, u32[]{:S(2)}, u32[]{:S(2)}) collective-permute-start(bf16[2,272,128]{2,1,0:T(8,128)(2,1)S(1)} %pad_maximum_fusion.2.own0), channel_id=1, source_target_pairs={{0,6},{2,4},{4,2},{6,0},{1,7},{3,5},{5,3},{7,1},{8,14},{10,12},{12... | collective-permute-start | bytes 417800 | tf_op jit(solution)/shard_map/ppermute | solution.py:286
  21.6 2.5 %collective-permute-start.6 = (bf16[4,272,128]{2,1,0:T(8,128)(2,1)S(1)}, bf16[4,272,128]{2,1,0:T(8,128)(2,1)S(1)}, u32[]{:S(2)}, u32[]{:S(2)}) collective-permute-start(bf16[4,272,128]{2,1,0:T(8,128)(2,1)S(1)} %pad_maximum_fusion.1.own0), channel_id=1, source_target_pairs={{0,48},{16,32},{32,16},{48,0},{1,49},{17,33},{33,17},{49,1},{2,50}... | collective-permute-start | bytes 835592 | tf_op jit(solution)/shard_map/ppermute | solution.py:286
  24.1 0.0 collective-permute-start.5
  24.1 1.4 %collective-permute-start.4 = (bf16[4,272,128]{2,1,0:T(8,128)(2,1)S(1)}, bf16[4,272,128]{2,1,0:T(8,128)(2,1)S(1)}, u32[]{:S(2)}, u32[]{:S(2)}) collective-permute-start(bf16[4,272,128]{2,1,0:T(8,128)(2,1)S(1)} %pad_maximum_fusion.1.own0), channel_id=1, source_target_pairs={{0,32},{16,48},{32,0},{48,16},{1,33},{17,49},{33,1},{49,17},{2,34}... | collective-permute-start | bytes 835592 | tf_op jit(solution)/shard_map/ppermute | solution.py:286
  25.5 0.0 collective-permute-start.8
  25.5 0.0 collective-permute-done.9.own3
  25.5 1.3 %collective-permute-start.7 = (bf16[2,272,128]{2,1,0:T(8,128)(2,1)S(1)}, bf16[2,272,128]{2,1,0:T(8,128)(2,1)S(1)}, u32[]{:S(2)}, u32[]{:S(2)}) collective-permute-start(bf16[2,272,128]{2,1,0:T(8,128)(2,1)S(1)} %pad_maximum_fusion.2.own0), channel_id=1, source_target_pairs={{0,4},{2,6},{4,0},{6,2},{1,5},{3,7},{5,1},{7,3},{8,12},{10,14},{12... | collective-permute-start | bytes 417800 | tf_op jit(solution)/shard_map/ppermute | solution.py:286
  26.8 2.9 %collective-permute-done.8.own2 = bf16[2,272,128]{2,1,0:T(8,128)(2,1)S(1)} collective-permute-done((bf16[2,272,128]{2,1,0:T(8,128)(2,1)S(1)}, bf16[2,272,128]{2,1,0:T(8,128)(2,1)S(1)}, u32[]{:S(2)}, u32[]{:S(2)}) %collective-permute-start.8) | collective-permute-done | bytes 139296 | tf_op jit(solution)/shard_map/ppermute | solution.py:286
  29.7 4.4 %collective-permute-start.11 = (bf16[4,272,128]{2,1,0:T(8,128)(2,1)S(1)}, bf16[4,272,128]{2,1,0:T(8,128)(2,1)S(1)}, u32[]{:S(2)}, u32[]{:S(2)}) collective-permute-start(bf16[4,272,128]{2,1,0:T(8,128)(2,1)S(1)} %pad_maximum_fusion.1.own0), channel_id=1, source_target_pairs={{0,8},{8,0},{1,9},{9,1},{2,10},{10,2},{3,11},{11,3},{4,12},{12,4},... | collective-permute-start | bytes 835592 | tf_op jit(solution)/shard_map/ppermute | solution.py:286
  34.1 0.0 collective-permute-done.7.own1
  34.1 0.7 copy-done
  34.8 0.0 collective-permute-done.6.own3
  34.8 0.0 collective-permute-done.5.own2
  34.8 0.3 collective-permute-done.4.own1
  35.1 4.0 %collective-permute-start.12 = (bf16[4,272,128]{2,1,0:T(8,128)(2,1)S(1)}, bf16[4,272,128]{2,1,0:T(8,128)(2,1)}, u32[]{:S(2)}, u32[]{:S(2)}) collective-permute-start(bf16[4,272,128]{2,1,0:T(8,128)(2,1)S(1)} %collective-permute-done.4.own1), channel_id=1, source_target_pairs={{0,8},{8,0},{1,9},{9,1},{2,10},{10,2},{3,11},{11,3},{4,12},{12,4},... | collective-permute-start | bytes 835592 | tf_op jit(solution)/shard_map/ppermute | solution.py:286
  39.1 0.0 collective-permute-start.13
  39.1 0.5 collective-permute-start.14
  39.6 0.9 copy-done.1
  40.5 2.1 %shard_map.114.own_source = bf16[512,384]{1,0:T(8,128)(2,1)S(1)} custom-call(s32[1]{0:T(128)} %bitcast.1.place, bf16[2,272,128]{2,1,0:T(8,128)(2,1)S(1)} %pad_maximum_fusion.2.own0, bf16[2,272,128]{2,1,0:T(8,128)(2,1)S(1)} %copy-done.1, bf16[2,272,128]{2,1,0:T(8,128)(2,1)S(1)} %collective-permute-done.8.own2, ...), custom_call_target="tpu_custom_call" | custom-call | flops 700000000 | bytes 2000000 | tf_op jit(solution)/shard_map/pallas_call | solution.py:319
  42.6 0.3 collective-permute-start.10
  42.9 0.0 collective-permute-done.11.other0
  42.9 0.0 collective-permute-done.12.other1
  42.9 0.0 collective-permute-done.14.other3
  42.9 5.4 %shard_map.115.emb_target = bf16[1024,384]{1,0:T(8,128)(2,1)S(1)} custom-call(s32[1]{0:T(128)} %bitcast.place, bf16[4,272,128]{2,1,0:T(8,128)(2,1)S(1)} %pad_maximum_fusion.1.own0, bf16[4,272,128]{2,1,0:T(8,128)(2,1)S(1)} %collective-permute-done.4.own1, bf16[4,272,128]{2,1,0:T(8,128)(2,1)S(1)} %collective-permute-done.5.own2, ...), custom_call_target="tpu_custom_call" | custom-call | flops 2400000000 | bytes 4000000 | tf_op jit(solution)/shard_map/pallas_call | solution.py:332
  48.3 1.7 %shard_map.116 = (f32[8,1024,128]{2,1,0:T(8,128)S(1)}, f32[16,16,128]{2,1,0:T(8,128)S(1)}) custom-call(s32[1]{0:T(128)} %bitcast.place, bf16[512,384]{1,0:T(8,128)(2,1)S(1)} %shard_map.114.own_source, bf16[512,384]{1,0:T(8,128)(2,1)S(1)} %collective-permute-done.10.other_source, bf16[1024,384]{1,0:T(8,128)(2,1)S(1)} %shard_map.115.emb_target), custom_call_target="tpu_custom_call" | custom-call | tf_op jit(solution)/shard_map/pallas_call | solution.py:340
  50.1 8.7 %all_to_all.20.got = f32[16,16,128]{2,1,0:T(8,128)S(1)} all-to-all(f32[16,16,128]{2,1,0:T(8,128)S(1)} %get-tuple-element.50), channel_id=1, replica_groups=mesh['zh'=4,'x'=4,'c'=2,'y'=4,'zl'=2] {'c','y','zl'}, dimensions={0} | all-to-all | bytes 262144 | tf_op jit(solution)/shard_map/all_to_all | solution.py:295
  58.8 1.1 %shard_map.117 = (f32[8,1024,128]{2,1,0:T(8,128)S(1)}, f32[8,8,128]{2,1,0:T(8,128)S(1)}, f32[16,8,128]{2,1,0:T(8,128)S(1)}, f32[8,128]{1,0:T(8,128)S(1)}) custom-call(f32[8,1024,128]{2,1,0:T(8,128)S(1)} %get-tuple-element.49.scores, f32[16,16,128]{2,1,0:T(8,128)S(1)} %all_to_all.20.got), custom_call_target="tpu_custom_call" | custom-call | tf_op jit(solution)/shard_map/pallas_call | solution.py:348
  59.8 15.0 %all_to_all.21.got = f32[16,8,128]{2,1,0:T(8,128)S(1)} all-to-all(f32[16,8,128]{2,1,0:T(8,128)S(1)} %get-tuple-element.53), channel_id=1, replica_groups=mesh['zh'=4,'x'=4,'c'=2,'y'=4,'zl'=2] {'zh','x'}, dimensions={0} | all-to-all | bytes 131072 | tf_op jit(solution)/shard_map/all_to_all | solution.py:295
  74.9 0.4 shard_map.118
  75.3 10.5 %all_to_all.22.got = f32[16,8,128]{2,1,0:T(8,128)S(1)} all-to-all(f32[16,8,128]{2,1,0:T(8,128)S(1)} %get-tuple-element.55), channel_id=1, replica_groups=mesh['zh'=4,'x'=4,'c'=2,'y'=4,'zl'=2] {'c','y','zl'}, dimensions={0} | all-to-all | bytes 131072 | tf_op jit(solution)/shard_map/all_to_all | solution.py:295
  85.8 1.0 %shard_map.119 = (f32[16,8,128]{2,1,0:T(8,128)}, f32[8,128]{1,0:T(8,128)S(1)}) custom-call(f32[8,1024,128]{2,1,0:T(8,128)S(1)} %get-tuple-element.51.weights, f32[8,8,128]{2,1,0:T(8,128)S(1)} %get-tuple-element.54.scale, f32[16,8,128]{2,1,0:T(8,128)S(1)} %all_to_all.22.got, f32[8,128]{1,0:T(8,128)S(1)} %get-tuple-element.56.before), custom_call_target="tpu_custom_call" | custom-call | tf_op jit(solution)/shard_map/pallas_call | solution.py:369
  86.9 3.5 %all-to-all-start.3 = ((f32[16,8,128]{2,1,0:T(8,128)}), f32[16,8,128]{2,1,0:T(8,128)S(1)}, u32[]{:S(2)}, u32[]{:S(2)}) async-start(f32[16,8,128]{2,1,0:T(8,128)} %get-tuple-element.59), calls=%async_computation.3 | async-start | bytes 131072 | tf_op jit(solution)/shard_map/all_to_all | solution.py:295
  90.4 8.9 %all-to-all-done.3 = f32[16,8,128]{2,1,0:T(8,128)S(1)} async-done(((f32[16,8,128]{2,1,0:T(8,128)}), f32[16,8,128]{2,1,0:T(8,128)S(1)}, u32[]{:S(2)}, u32[]{:S(2)}) %all-to-all-start.3) | async-done | bytes 65568 | tf_op jit(solution)/shard_map/all_to_all | solution.py:295
  99.3 2.1 %collective-permute-start.15 = (f32[8,128]{1,0:T(8,128)S(1)}, f32[8,128]{1,0:T(8,128)S(1)}, u32[]{:S(2)}, u32[]{:S(2)}) collective-permute-start(f32[8,128]{1,0:T(8,128)S(1)} %subtract_add_fusion), channel_id=1, source_target_pairs={{0,8},{8,0},{1,9},{9,1},{2,10},{10,2},{3,11},{11,3},{4,12},{12,4},... | collective-permute-start | bytes 12296 | tf_op jit(solution)/shard_map/ppermute | solution.py:286
  101.4 0.6 select_bitcast_fusion
  102.0 0.2 collective-permute-done.15
  102.2 0.1 fusion
  102.3 0.7 maximum_bitcast_fusion
  (13 shorter events, 0.1 us)
Async XLA Ops:
  2.3 16.3 %copy-start.3 = (bf16[1,272,128]{2,1,0:T(8,128)(2,1)S(1)}, bf16[1,272,128]{2,1,0:T(8,128)(2,1)}, u32[]{:S(2)}) copy-start(bf16[1,272,128]{2,1,0:T(8,128)(2,1)} %get-tuple-element.34) | copy-start | bytes 208900
  2.3 16.5 %copy-start.2 = (bf16[1,272,128]{2,1,0:T(8,128)(2,1)S(1)}, bf16[1,272,128]{2,1,0:T(8,128)(2,1)}, u32[]{:S(2)}) copy-start(bf16[1,272,128]{2,1,0:T(8,128)(2,1)} %get-tuple-element.33) | copy-start | bytes 208900
  2.3 16.3 %collective-permute-start.2 = (bf16[1,272,128]{2,1,0:T(8,128)(2,1)}, bf16[1,272,128]{2,1,0:T(8,128)(2,1)S(1)}, u32[]{:S(2)}, u32[]{:S(2)}) collective-permute-start(bf16[1,272,128]{2,1,0:T(8,128)(2,1)} %get-tuple-element.33), channel_id=1, source_target_pairs={{0,192},{64,128},{128,64},{192,0},{1,193},{65,129},{129,65},{193,1... | collective-permute-start | bytes 208904 | tf_op jit(solution)/shard_map/ppermute | solution.py:286
  9.2 9.3 %collective-permute-start.1 = (bf16[1,272,128]{2,1,0:T(8,128)(2,1)}, bf16[1,272,128]{2,1,0:T(8,128)(2,1)S(1)}, u32[]{:S(2)}, u32[]{:S(2)}) collective-permute-start(bf16[1,272,128]{2,1,0:T(8,128)(2,1)} %get-tuple-element.33), channel_id=1, source_target_pairs={{0,64},{64,0},{128,192},{192,128},{1,65},{65,1},{129,193},{193,129... | collective-permute-start | bytes 208904 | tf_op jit(solution)/shard_map/ppermute | solution.py:286
  10.4 8.3 %collective-permute-start = (bf16[1,272,128]{2,1,0:T(8,128)(2,1)}, bf16[1,272,128]{2,1,0:T(8,128)(2,1)S(1)}, u32[]{:S(2)}, u32[]{:S(2)}) collective-permute-start(bf16[1,272,128]{2,1,0:T(8,128)(2,1)} %get-tuple-element.33), channel_id=1, source_target_pairs={{0,128},{64,192},{128,0},{192,64},{1,129},{65,193},{129,1},{193,65... | collective-permute-start | bytes 208904 | tf_op jit(solution)/shard_map/ppermute | solution.py:286
  11.4 7.1 %collective-permute-start.3 = (bf16[1,272,128]{2,1,0:T(8,128)(2,1)}, bf16[1,272,128]{2,1,0:T(8,128)(2,1)S(1)}, u32[]{:S(2)}, u32[]{:S(2)}) collective-permute-start(bf16[1,272,128]{2,1,0:T(8,128)(2,1)} %get-tuple-element.34), channel_id=1, source_target_pairs={{0,1},{1,0},{2,3},{3,2},{4,5},{5,4},{6,7},{7,6},{8,9},{9,8},{10,11... | collective-permute-start | bytes 208904 | tf_op jit(solution)/shard_map/ppermute | solution.py:286
  18.8 6.7 %collective-permute-start.9 = (bf16[2,272,128]{2,1,0:T(8,128)(2,1)S(1)}, bf16[2,272,128]{2,1,0:T(8,128)(2,1)S(1)}, u32[]{:S(2)}, u32[]{:S(2)}) collective-permute-start(bf16[2,272,128]{2,1,0:T(8,128)(2,1)S(1)} %pad_maximum_fusion.2.own0), channel_id=1, source_target_pairs={{0,6},{2,4},{4,2},{6,0},{1,7},{3,5},{5,3},{7,1},{8,14},{10,12},{12... | collective-permute-start | bytes 417800 | tf_op jit(solution)/shard_map/ppermute | solution.py:286
  21.6 13.2 %collective-permute-start.6 = (bf16[4,272,128]{2,1,0:T(8,128)(2,1)S(1)}, bf16[4,272,128]{2,1,0:T(8,128)(2,1)S(1)}, u32[]{:S(2)}, u32[]{:S(2)}) collective-permute-start(bf16[4,272,128]{2,1,0:T(8,128)(2,1)S(1)} %pad_maximum_fusion.1.own0), channel_id=1, source_target_pairs={{0,48},{16,32},{32,16},{48,0},{1,49},{17,33},{33,17},{49,1},{2,50}... | collective-permute-start | bytes 835592 | tf_op jit(solution)/shard_map/ppermute | solution.py:286
  24.1 10.7 %collective-permute-start.5 = (bf16[4,272,128]{2,1,0:T(8,128)(2,1)S(1)}, bf16[4,272,128]{2,1,0:T(8,128)(2,1)S(1)}, u32[]{:S(2)}, u32[]{:S(2)}) collective-permute-start(bf16[4,272,128]{2,1,0:T(8,128)(2,1)S(1)} %pad_maximum_fusion.1.own0), channel_id=1, source_target_pairs={{0,16},{16,0},{32,48},{48,32},{1,17},{17,1},{33,49},{49,33},{2,18}... | collective-permute-start | bytes 835592 | tf_op jit(solution)/shard_map/ppermute | solution.py:286
  24.1 11.0 %collective-permute-start.4 = (bf16[4,272,128]{2,1,0:T(8,128)(2,1)S(1)}, bf16[4,272,128]{2,1,0:T(8,128)(2,1)S(1)}, u32[]{:S(2)}, u32[]{:S(2)}) collective-permute-start(bf16[4,272,128]{2,1,0:T(8,128)(2,1)S(1)} %pad_maximum_fusion.1.own0), channel_id=1, source_target_pairs={{0,32},{16,48},{32,0},{48,16},{1,33},{17,49},{33,1},{49,17},{2,34}... | collective-permute-start | bytes 835592 | tf_op jit(solution)/shard_map/ppermute | solution.py:286
  25.5 4.2 %collective-permute-start.8 = (bf16[2,272,128]{2,1,0:T(8,128)(2,1)S(1)}, bf16[2,272,128]{2,1,0:T(8,128)(2,1)S(1)}, u32[]{:S(2)}, u32[]{:S(2)}) collective-permute-start(bf16[2,272,128]{2,1,0:T(8,128)(2,1)S(1)} %pad_maximum_fusion.2.own0), channel_id=1, source_target_pairs={{0,2},{2,0},{4,6},{6,4},{1,3},{3,1},{5,7},{7,5},{8,10},{10,8},{12,... | collective-permute-start | bytes 417800 | tf_op jit(solution)/shard_map/ppermute | solution.py:286
  25.5 8.6 %collective-permute-start.7 = (bf16[2,272,128]{2,1,0:T(8,128)(2,1)S(1)}, bf16[2,272,128]{2,1,0:T(8,128)(2,1)S(1)}, u32[]{:S(2)}, u32[]{:S(2)}) collective-permute-start(bf16[2,272,128]{2,1,0:T(8,128)(2,1)S(1)} %pad_maximum_fusion.2.own0), channel_id=1, source_target_pairs={{0,4},{2,6},{4,0},{6,2},{1,5},{3,7},{5,1},{7,3},{8,12},{10,14},{12... | collective-permute-start | bytes 417800 | tf_op jit(solution)/shard_map/ppermute | solution.py:286
  29.7 13.2 %collective-permute-start.11 = (bf16[4,272,128]{2,1,0:T(8,128)(2,1)S(1)}, bf16[4,272,128]{2,1,0:T(8,128)(2,1)S(1)}, u32[]{:S(2)}, u32[]{:S(2)}) collective-permute-start(bf16[4,272,128]{2,1,0:T(8,128)(2,1)S(1)} %pad_maximum_fusion.1.own0), channel_id=1, source_target_pairs={{0,8},{8,0},{1,9},{9,1},{2,10},{10,2},{3,11},{11,3},{4,12},{12,4},... | collective-permute-start | bytes 835592 | tf_op jit(solution)/shard_map/ppermute | solution.py:286
  34.1 0.7 copy-start
  35.1 7.8 %collective-permute-start.12 = (bf16[4,272,128]{2,1,0:T(8,128)(2,1)S(1)}, bf16[4,272,128]{2,1,0:T(8,128)(2,1)}, u32[]{:S(2)}, u32[]{:S(2)}) collective-permute-start(bf16[4,272,128]{2,1,0:T(8,128)(2,1)S(1)} %collective-permute-done.4.own1), channel_id=1, source_target_pairs={{0,8},{8,0},{1,9},{9,1},{2,10},{10,2},{3,11},{11,3},{4,12},{12,4},... | collective-permute-start | bytes 835592 | tf_op jit(solution)/shard_map/ppermute | solution.py:286
  39.1 3.8 %collective-permute-start.13 = (bf16[4,272,128]{2,1,0:T(8,128)(2,1)S(1)}, bf16[4,272,128]{2,1,0:T(8,128)(2,1)}, u32[]{:S(2)}, u32[]{:S(2)}) collective-permute-start(bf16[4,272,128]{2,1,0:T(8,128)(2,1)S(1)} %collective-permute-done.5.own2), channel_id=1, source_target_pairs={{0,8},{8,0},{1,9},{9,1},{2,10},{10,2},{3,11},{11,3},{4,12},{12,4},... | collective-permute-start | bytes 835592 | tf_op jit(solution)/shard_map/ppermute | solution.py:286
  39.1 3.8 %collective-permute-start.14 = (bf16[4,272,128]{2,1,0:T(8,128)(2,1)S(1)}, bf16[4,272,128]{2,1,0:T(8,128)(2,1)}, u32[]{:S(2)}, u32[]{:S(2)}) collective-permute-start(bf16[4,272,128]{2,1,0:T(8,128)(2,1)S(1)} %collective-permute-done.6.own3), channel_id=1, source_target_pairs={{0,8},{8,0},{1,9},{9,1},{2,10},{10,2},{3,11},{11,3},{4,12},{12,4},... | collective-permute-start | bytes 835592 | tf_op jit(solution)/shard_map/ppermute | solution.py:286
  39.6 0.9 copy-start.1
  42.6 5.8 %collective-permute-start.10 = (bf16[512,384]{1,0:T(8,128)(2,1)S(1)}, bf16[512,384]{1,0:T(8,128)(2,1)S(1)}, u32[]{:S(2)}, u32[]{:S(2)}) collective-permute-start(bf16[512,384]{1,0:T(8,128)(2,1)S(1)} %shard_map.114.own_source), channel_id=1, source_target_pairs={{0,8},{8,0},{1,9},{9,1},{2,10},{10,2},{3,11},{11,3},{4,12},{12,4},... | collective-permute-start | bytes 1179656 | tf_op jit(solution)/shard_map/ppermute | solution.py:286
  86.9 12.4 %all-to-all-start.3 = ((f32[16,8,128]{2,1,0:T(8,128)}), f32[16,8,128]{2,1,0:T(8,128)S(1)}, u32[]{:S(2)}, u32[]{:S(2)}) async-start(f32[16,8,128]{2,1,0:T(8,128)} %get-tuple-element.59), calls=%async_computation.3 | async-start | bytes 131072 | tf_op jit(solution)/shard_map/all_to_all | solution.py:295
  99.3 2.9 %collective-permute-start.15 = (f32[8,128]{1,0:T(8,128)S(1)}, f32[8,128]{1,0:T(8,128)S(1)}, u32[]{:S(2)}, u32[]{:S(2)}) collective-permute-start(f32[8,128]{1,0:T(8,128)S(1)} %subtract_add_fusion), channel_id=1, source_target_pairs={{0,8},{8,0},{1,9},{9,1},{2,10},{10,2},{3,11},{11,3},{4,12},{12,4},... | collective-permute-start | bytes 12296 | tf_op jit(solution)/shard_map/ppermute | solution.py:286

commit v8 on v7

--- a/solution.py
+++ b/solution.py
@@ -99,7 +99,7 @@
 
 
 def turn(v):
-    return ((v & 1) << 1) | (v >> 1)
+    return v ^ (v >> 1)
 
 
 def slot_xor(k):
@@ -110,20 +110,25 @@
     return turn(v >> 3) | (turn((v >> 1) & 3) << 2) | ((v & 1) << 4)
 
 
-def source_kernel(place, own0, own1, own2, own3, weights, out, *scratch):
+def source_xor(k):
+    return (turn(k >> 1) << 1) | (k & 1)
+
+
+source_of = source_xor
+
+
+def source_kernel(place, packed, weights, out, *scratch):
     me = place[0]
-    pieces = (own0, own1, own2, own3)
 
     def emit(at, value):
         for k in range(value.shape[0] // PART):
-            slot = at // PART + k
-            q = me ^ ((turn(slot >> 1) << 1) | (slot & 1))
+            q = me ^ source_xor(at // PART + k)
             out[pl.ds(pl.multiple_of(q * PART, PART), PART), :] = value[k * PART : (k + 1) * PART, :]
 
     graph_layers(
-        lambda k: (pieces[k // 2], k % 2),
-        lambda k: k ^ 7,
-        lambda link: (turn((link ^ me) >> 1) << 1) | ((link ^ me) & 1),
+        lambda k: (packed, k),
+        lambda k: k ^ source_of(7),
+        lambda link: source_of(link ^ me),
         weights, *scratch, emit, 8,
     )
 
@@ -146,7 +151,7 @@
 
     graph_layers(
         lambda k: (pieces[k // 4], k % 4),
-        lambda k: k ^ 31,
+        lambda k: k ^ slot_of(31),
         lambda link: slot_of(link ^ me),
         weights, *scratch, emit, 16,
     )
@@ -287,8 +292,7 @@
 
 
 def direct(value, axis):
-    far, near, beyond = (swap(value, axis, 4, xor) for xor in (2, 1, 3))
-    return [value, far, near, beyond]
+    return [value] + [swap(value, axis, 4, xor) for xor in (1, 3, 2)]
 
 
 def exchange(value, axes):
@@ -313,6 +317,7 @@
     held, source, weights = lax.optimization_barrier((held, source, weights))
     source = direct(source, "y")
     own = direct(held, "x")
+    source = jnp.concatenate(source, axis=0)
     own[1:], source = lax.optimization_barrier((own[1:], source))
     other = [swap(piece, "c", 2, 1) for piece in own]
 
@@ -320,11 +325,11 @@
         source_kernel,
         [((OWN_ROWS, D), bf16)],
         graph_scratch(OWN_ROWS),
-        [SMEM()] + [VMEM()] * 5,
+        [SMEM()] + [VMEM()] * 2,
         pl.CostEstimate(flops=700_000_000, bytes_accessed=2_000_000, transcendentals=0),
     )(
         me_source[None],
-        *source,
+        source,
         weights,
     )
     other_source = swap(emb_source, "c", 2, 1)
@@ -337,6 +342,7 @@
         pl.CostEstimate(flops=2_400_000_000, bytes_accessed=4_000_000, transcendentals=0),
     )(me[None], *own, *other, weights)
 
+    emb_target, first = lax.optimization_barrier((emb_target, (me & 1) == 0))
     scores, send = call(
         score_kernel,
         [((COL_BLOCKS, ROWS, LANES), f32), ((N_ROW_PEERS, 2 * ROW_BLOCKS, LANES), f32)],
@@ -373,10 +379,12 @@
         [VMEM()] * 4,
     )(spread_weights, scale, got, source_first)
 
-    total = jnp.sum(exchange(sums, ("zh", "x")), axis=0)
-    half = target_first + (LOG_N - jnp.log(total))
+    got = exchange(sums, ("zh", "x"))
+    got, first, source_potential, target_first = lax.optimization_barrier(
+        (got, first, source_potential, target_first)
+    )
+    half = target_first + (LOG_N - jnp.log(jnp.sum(got, axis=0)))
     other_half = swap(half, "c", 2, 1)
-    first = (me & 1) == 0
     even, odd = jnp.where(first, half, other_half), jnp.where(first, other_half, half)
     target_potential = jnp.concatenate(
         [jnp.concatenate([v[:, at : at + PART] for v in (even, odd)], axis=1) for at in (0, PART)], axis=0

time: 103 us -> 101 us (0.981)
  blocking collectives: 34.2 us -> 46.3 us
  starting transfers between devices: 32.6 us -> 25 us
  waiting for transfers between devices: 17.5 us -> 12.7 us
  local copies, waits for them, and re-layouts: 1.65 us -> 0.08 us
    all_to_all x3 -> x4, blocking collectives: 34.2 us -> 46.3 us  [exchange(): return lax.all_to_all(value, axes, 0, 0)]
    all_to_all x1 -> x0, waiting for transfers between devices: 8.87 us -> none  [exchange(): return lax.all_to_all(value, axes, 0, 0)]
    ppermute x16, starting transfers between devices: 29.1 us -> 25 us  [swap(): return lax.ppermute(value, axis, [(i, i ^ xor) for i in range(size)])]
    ppermute x16, waiting for transfers between devices: 8.67 us -> 12.7 us  [swap(): return lax.ppermute(value, axis, [(i, i ^ xor) for i in range(size)])]
    all_to_all x1 -> x0, starting transfers between devices: 3.5 us -> none  [exchange(): return lax.all_to_all(value, axes, 0, 0)]
    unnamed x8 -> x4, local copies, waits for them, and re-layouts: 1.58 us -> 0.01 us
  transfers between devices with their start and end apart: 17 -> 16, of which waited for: 6 -> 4; matrix products, arithmetic and copies ran while one was open for 2% -> 2% of each run, Pallas kernels for 7% -> 7%
where the time goes in v8:
time: 101 us; the launch traced here: 100 us
  blocking collectives  46.3 us (46%)
  starting transfers between devices  25 us (25%)
  Pallas kernels  12.8 us (13%)
  waiting for transfers between devices  12.7 us (13%)
  other arithmetic  2.76 us (3%)
    all_to_all x4, blocking collectives, exchange(): return lax.all_to_all(value, axes, 0, 0)  46.3 us
    ppermute x16, starting transfers between devices, swap(): return lax.ppermute(value, axis, [(i, i ^ xor) for i in range(size)])  25 us
    ppermute x16, waiting for transfers between devices, swap(): return lax.ppermute(value, axis, [(i, i ^ xor) for i in range(size)])  12.7 us
    pallas_call x1, Pallas kernels, on_device(): call(target_kernel, [((COLS, D), bf16)], graph_scratch(BLOCK), [SMEM()] +...  5.42 us
    pallas_call x1, Pallas kernels, on_device(): call(source_kernel, [((OWN_ROWS, D), bf16)], graph_scratch(OWN_ROWS), [SM...  2.1 us
  transfers between devices with their start and end apart: 16, of which 4 were waited for; matrix products, arithmetic and copies ran while one was open for 2% of the time, Pallas kernels for 7%

profile of v8, /device:TPU:1, one launch (start us, length us, event | category | flops | bytes accessed | tf_op | source)
XLA Modules:
  0.0 100.5 jit_solution(3962488013348956825)
XLA Ops:
  0.6 1.6 %shard_map.113 = (bf16[1,272,128]{2,1,0:T(8,128)(2,1)}, bf16[1,272,128]{2,1,0:T(8,128)(2,1)}) custom-call(bf16[1,64,384]{2,1,0:T(8,128)(2,1)} %refs_0_.1, bf16[1,64,128]{2,1,0:T(8,128)(2,1)} %refs_1_.1, s32[1,1,2]{2,1,0:T(1,128)} %refs_2_.1, bf16[1,64,384]{2,1,0:T(8,128)(2,1)} %refs_3_.1, bf16[1,64,128]{2,1,0:T(8,128)(2,1)} %refs_4_.1, s32[1,1,2]{2,1,0:T(1,128)} %refs_5_.1), custom_call_target="tpu_custom_call" | custom-call | tf_op jit(solution)/shard_map/pallas_call | solution.py:50
  2.3 7.8 %collective-permute-start.2 = (bf16[1,272,128]{2,1,0:T(8,128)(2,1)}, bf16[1,272,128]{2,1,0:T(8,128)(2,1)S(1)}, u32[]{:S(2)}, u32[]{:S(2)}) collective-permute-start(bf16[1,272,128]{2,1,0:T(8,128)(2,1)} %get-tuple-element.36), channel_id=1, source_target_pairs={{0,128},{64,192},{128,0},{192,64},{1,129},{65,193},{129,1},{193,65... | collective-permute-start | bytes 208904 | tf_op jit(solution)/shard_map/ppermute | solution.py:291
  10.1 0.0 collective-permute-start.1
  10.1 1.2 %collective-permute-start = (bf16[1,272,128]{2,1,0:T(8,128)(2,1)}, bf16[1,272,128]{2,1,0:T(8,128)(2,1)S(1)}, u32[]{:S(2)}, u32[]{:S(2)}) collective-permute-start(bf16[1,272,128]{2,1,0:T(8,128)(2,1)} %get-tuple-element.36), channel_id=1, source_target_pairs={{0,64},{64,0},{128,192},{192,128},{1,65},{65,1},{129,193},{193,129... | collective-permute-start | bytes 208904 | tf_op jit(solution)/shard_map/ppermute | solution.py:291
  11.3 0.7 collective-permute-start.3
  12.1 1.3 %pad_maximum_fusion.weights = bf16[1536,384]{1,0:T(8,128)(2,1)S(1)} fusion(bf16[384,384]{1,0:T(8,128)(2,1)} %param.19, bf16[384,384]{1,0:T(8,128)(2,1)} %param.18, bf16[384,384]{1,0:T(8,128)(2,1)} %param.17, bf16[384,384]{1,0:T(8,128)(2,1)} %param.16), kind=kLoop, calls=%fused_computation | loop fusion | flops 4718592 | bytes 2359296 | tf_op jit(solution)/shard_map/concatenate | solution.py:314
  13.4 5.0 %collective-permute-done.3 = bf16[1,272,128]{2,1,0:T(8,128)(2,1)S(1)} collective-permute-done((bf16[1,272,128]{2,1,0:T(8,128)(2,1)}, bf16[1,272,128]{2,1,0:T(8,128)(2,1)S(1)}, u32[]{:S(2)}, u32[]{:S(2)}) %collective-permute-start.3) | collective-permute-done | bytes 69664 | tf_op jit(solution)/shard_map/ppermute | solution.py:291
  18.5 0.0 collective-permute-done.2
  18.5 0.0 collective-permute-done.1
  18.5 0.0 collective-permute-done
  18.5 3.0 %collective-permute-start.9 = (bf16[2,272,128]{2,1,0:T(8,128)(2,1)S(1)}, bf16[2,272,128]{2,1,0:T(8,128)(2,1)S(1)}, u32[]{:S(2)}, u32[]{:S(2)}) collective-permute-start(bf16[2,272,128]{2,1,0:T(8,128)(2,1)S(1)} %pad_maximum_fusion.3), channel_id=1, source_target_pairs={{0,4},{2,6},{4,0},{6,2},{1,5},{3,7},{5,1},{7,3},{8,12},{10,14},{12... | collective-permute-start | bytes 417800 | tf_op jit(solution)/shard_map/ppermute | solution.py:291
  21.6 2.7 %collective-permute-start.6 = (bf16[4,272,128]{2,1,0:T(8,128)(2,1)S(1)}, bf16[4,272,128]{2,1,0:T(8,128)(2,1)S(1)}, u32[]{:S(2)}, u32[]{:S(2)}) collective-permute-start(bf16[4,272,128]{2,1,0:T(8,128)(2,1)S(1)} %pad_maximum_fusion.2.own0), channel_id=1, source_target_pairs={{0,32},{16,48},{32,0},{48,16},{1,33},{17,49},{33,1},{49,17},{2,34}... | collective-permute-start | bytes 835592 | tf_op jit(solution)/shard_map/ppermute | solution.py:291
  24.3 0.9 collective-permute-start.5
  25.2 0.0 collective-permute-start.4
  25.2 0.8 collective-permute-start.8
  26.0 0.0 collective-permute-done.9
  26.0 0.0 collective-permute-start.7
  26.0 4.6 %collective-permute-done.8 = bf16[2,272,128]{2,1,0:T(8,128)(2,1)S(1)} collective-permute-done((bf16[2,272,128]{2,1,0:T(8,128)(2,1)S(1)}, bf16[2,272,128]{2,1,0:T(8,128)(2,1)S(1)}, u32[]{:S(2)}, u32[]{:S(2)}) %collective-permute-start.8) | collective-permute-done | bytes 139296 | tf_op jit(solution)/shard_map/ppermute | solution.py:291
  30.6 3.4 %collective-permute-start.11 = (bf16[4,272,128]{2,1,0:T(8,128)(2,1)S(1)}, bf16[4,272,128]{2,1,0:T(8,128)(2,1)S(1)}, u32[]{:S(2)}, u32[]{:S(2)}) collective-permute-start(bf16[4,272,128]{2,1,0:T(8,128)(2,1)S(1)} %pad_maximum_fusion.2.own0), channel_id=1, source_target_pairs={{0,8},{8,0},{1,9},{9,1},{2,10},{10,2},{3,11},{11,3},{4,12},{12,4},... | collective-permute-start | bytes 835592 | tf_op jit(solution)/shard_map/ppermute | solution.py:291
  34.0 0.0 collective-permute-done.7
  34.0 0.1 pad_maximum_fusion.1.packed
  34.1 0.0 collective-permute-done.6.own3
  34.1 2.7 %collective-permute-done.5.own2 = bf16[4,272,128]{2,1,0:T(8,128)(2,1)S(1)} collective-permute-done((bf16[4,272,128]{2,1,0:T(8,128)(2,1)S(1)}, bf16[4,272,128]{2,1,0:T(8,128)(2,1)S(1)}, u32[]{:S(2)}, u32[]{:S(2)}) %collective-permute-start.5) | collective-permute-done | bytes 278560 | tf_op jit(solution)/shard_map/ppermute | solution.py:291
  36.9 0.0 collective-permute-done.4.own1
  36.9 1.4 %collective-permute-start.12 = (bf16[4,272,128]{2,1,0:T(8,128)(2,1)S(1)}, bf16[4,272,128]{2,1,0:T(8,128)(2,1)}, u32[]{:S(2)}, u32[]{:S(2)}) collective-permute-start(bf16[4,272,128]{2,1,0:T(8,128)(2,1)S(1)} %collective-permute-done.4.own1), channel_id=1, source_target_pairs={{0,8},{8,0},{1,9},{9,1},{2,10},{10,2},{3,11},{11,3},{4,12},{12,4},... | collective-permute-start | bytes 835592 | tf_op jit(solution)/shard_map/ppermute | solution.py:291
  38.2 0.0 collective-permute-start.13
  38.2 0.5 collective-permute-start.14
  38.8 2.1 %shard_map.114.own_source = bf16[512,384]{1,0:T(8,128)(2,1)S(1)} custom-call(s32[1]{0:T(128)} %bitcast.1.place, bf16[8,272,128]{2,1,0:T(8,128)(2,1)S(1)} %pad_maximum_fusion.1.packed, bf16[1536,384]{1,0:T(8,128)(2,1)S(1)} %pad_maximum_fusion.weights), custom_call_target="tpu_custom_call" | custom-call | flops 700000000 | bytes 2000000 | tf_op jit(solution)/shard_map/pallas_call | solution.py:324
  40.9 0.3 collective-permute-start.10
  41.2 0.0 collective-permute-done.11.other0
  41.2 0.0 collective-permute-done.12.other1
  41.2 0.0 collective-permute-done.13.other2
  41.2 0.0 collective-permute-done.14.other3
  41.2 5.4 %shard_map.115.emb_target = bf16[1024,384]{1,0:T(8,128)(2,1)S(1)} custom-call(s32[1]{0:T(128)} %bitcast.place, bf16[4,272,128]{2,1,0:T(8,128)(2,1)S(1)} %pad_maximum_fusion.2.own0, bf16[4,272,128]{2,1,0:T(8,128)(2,1)S(1)} %collective-permute-done.4.own1, bf16[4,272,128]{2,1,0:T(8,128)(2,1)S(1)} %collective-permute-done.5.own2, ...), custom_call_target="tpu_custom_call" | custom-call | flops 2400000000 | bytes 4000000 | tf_op jit(solution)/shard_map/pallas_call | solution.py:337
  46.6 0.0 collective-permute-done.10.other_source
  46.6 1.7 %shard_map.116 = (f32[8,1024,128]{2,1,0:T(8,128)S(1)}, f32[16,16,128]{2,1,0:T(8,128)S(1)}) custom-call(s32[1]{0:T(128)} %bitcast.place, bf16[512,384]{1,0:T(8,128)(2,1)S(1)} %shard_map.114.own_source, bf16[512,384]{1,0:T(8,128)(2,1)S(1)} %collective-permute-done.10.other_source, bf16[1024,384]{1,0:T(8,128)(2,1)S(1)} %shard_map.115.emb_target), custom_call_target="tpu_custom_call" | custom-call | tf_op jit(solution)/shard_map/pallas_call | solution.py:346
  48.4 9.1 %all_to_all.20.got = f32[16,16,128]{2,1,0:T(8,128)S(1)} all-to-all(f32[16,16,128]{2,1,0:T(8,128)S(1)} %get-tuple-element.51), channel_id=1, replica_groups=mesh['zh'=4,'x'=4,'c'=2,'y'=4,'zl'=2] {'c','y','zl'}, dimensions={0} | all-to-all | bytes 262144 | tf_op jit(solution)/shard_map/all_to_all | solution.py:299
  57.5 1.1 %shard_map.117 = (f32[8,1024,128]{2,1,0:T(8,128)S(1)}, f32[8,8,128]{2,1,0:T(8,128)S(1)}, f32[16,8,128]{2,1,0:T(8,128)S(1)}, f32[8,128]{1,0:T(8,128)S(1)}) custom-call(f32[8,1024,128]{2,1,0:T(8,128)S(1)} %get-tuple-element.50.scores, f32[16,16,128]{2,1,0:T(8,128)S(1)} %all_to_all.20.got), custom_call_target="tpu_custom_call" | custom-call | tf_op jit(solution)/shard_map/pallas_call | solution.py:354
  58.6 15.1 %all_to_all.21.got = f32[16,8,128]{2,1,0:T(8,128)S(1)} all-to-all(f32[16,8,128]{2,1,0:T(8,128)S(1)} %get-tuple-element.54), channel_id=1, replica_groups=mesh['zh'=4,'x'=4,'c'=2,'y'=4,'zl'=2] {'zh','x'}, dimensions={0} | all-to-all | bytes 131072 | tf_op jit(solution)/shard_map/all_to_all | solution.py:299
  73.7 0.4 shard_map.118
  74.1 10.5 %all_to_all.22.got = f32[16,8,128]{2,1,0:T(8,128)S(1)} all-to-all(f32[16,8,128]{2,1,0:T(8,128)S(1)} %get-tuple-element.56), channel_id=1, replica_groups=mesh['zh'=4,'x'=4,'c'=2,'y'=4,'zl'=2] {'c','y','zl'}, dimensions={0} | all-to-all | bytes 131072 | tf_op jit(solution)/shard_map/all_to_all | solution.py:299
  84.6 0.4 shard_map.119
  85.1 11.5 %all_to_all.23 = f32[16,8,128]{2,1,0:T(8,128)S(1)} all-to-all(f32[16,8,128]{2,1,0:T(8,128)S(1)} %get-tuple-element.58), channel_id=1, replica_groups=mesh['zh'=4,'x'=4,'c'=2,'y'=4,'zl'=2] {'zh','x'}, dimensions={0} | all-to-all | bytes 131072 | tf_op jit(solution)/shard_map/all_to_all | solution.py:299
  96.6 2.2 %collective-permute-start.15 = (f32[8,128]{1,0:T(8,128)S(1)}, f32[8,128]{1,0:T(8,128)S(1)}, u32[]{:S(2)}, u32[]{:S(2)}) collective-permute-start(f32[8,128]{1,0:T(8,128)S(1)} %subtract_add_fusion), channel_id=1, source_target_pairs={{0,8},{8,0},{1,9},{9,1},{2,10},{10,2},{3,11},{11,3},{4,12},{12,4},... | collective-permute-start | bytes 12296 | tf_op jit(solution)/shard_map/ppermute | solution.py:291
  98.9 0.6 select_bitcast_fusion
  99.5 0.2 collective-permute-done.15
  99.7 0.1 fusion
  99.8 0.7 maximum_bitcast_fusion
  (9 shorter events, 0.1 us)
Async XLA Ops:
  2.3 16.2 %copy-start.1 = (bf16[1,272,128]{2,1,0:T(8,128)(2,1)S(1)}, bf16[1,272,128]{2,1,0:T(8,128)(2,1)}, u32[]{:S(2)}) copy-start(bf16[1,272,128]{2,1,0:T(8,128)(2,1)} %get-tuple-element.37) | copy-start | bytes 208900
  2.3 16.2 %copy-start = (bf16[1,272,128]{2,1,0:T(8,128)(2,1)S(1)}, bf16[1,272,128]{2,1,0:T(8,128)(2,1)}, u32[]{:S(2)}) copy-start(bf16[1,272,128]{2,1,0:T(8,128)(2,1)} %get-tuple-element.36) | copy-start | bytes 208900
  2.3 16.2 %collective-permute-start.2 = (bf16[1,272,128]{2,1,0:T(8,128)(2,1)}, bf16[1,272,128]{2,1,0:T(8,128)(2,1)S(1)}, u32[]{:S(2)}, u32[]{:S(2)}) collective-permute-start(bf16[1,272,128]{2,1,0:T(8,128)(2,1)} %get-tuple-element.36), channel_id=1, source_target_pairs={{0,128},{64,192},{128,0},{192,64},{1,129},{65,193},{129,1},{193,65... | collective-permute-start | bytes 208904 | tf_op jit(solution)/shard_map/ppermute | solution.py:291
  10.1 8.4 %collective-permute-start.1 = (bf16[1,272,128]{2,1,0:T(8,128)(2,1)}, bf16[1,272,128]{2,1,0:T(8,128)(2,1)S(1)}, u32[]{:S(2)}, u32[]{:S(2)}) collective-permute-start(bf16[1,272,128]{2,1,0:T(8,128)(2,1)} %get-tuple-element.36), channel_id=1, source_target_pairs={{0,192},{64,128},{128,64},{192,0},{1,193},{65,129},{129,65},{193,1... | collective-permute-start | bytes 208904 | tf_op jit(solution)/shard_map/ppermute | solution.py:291
  10.1 8.4 %collective-permute-start = (bf16[1,272,128]{2,1,0:T(8,128)(2,1)}, bf16[1,272,128]{2,1,0:T(8,128)(2,1)S(1)}, u32[]{:S(2)}, u32[]{:S(2)}) collective-permute-start(bf16[1,272,128]{2,1,0:T(8,128)(2,1)} %get-tuple-element.36), channel_id=1, source_target_pairs={{0,64},{64,0},{128,192},{192,128},{1,65},{65,1},{129,193},{193,129... | collective-permute-start | bytes 208904 | tf_op jit(solution)/shard_map/ppermute | solution.py:291
  11.3 7.1 %collective-permute-start.3 = (bf16[1,272,128]{2,1,0:T(8,128)(2,1)}, bf16[1,272,128]{2,1,0:T(8,128)(2,1)S(1)}, u32[]{:S(2)}, u32[]{:S(2)}) collective-permute-start(bf16[1,272,128]{2,1,0:T(8,128)(2,1)} %get-tuple-element.37), channel_id=1, source_target_pairs={{0,1},{1,0},{2,3},{3,2},{4,5},{5,4},{6,7},{7,6},{8,9},{9,8},{10,11... | collective-permute-start | bytes 208904 | tf_op jit(solution)/shard_map/ppermute | solution.py:291
  18.5 7.4 %collective-permute-start.9 = (bf16[2,272,128]{2,1,0:T(8,128)(2,1)S(1)}, bf16[2,272,128]{2,1,0:T(8,128)(2,1)S(1)}, u32[]{:S(2)}, u32[]{:S(2)}) collective-permute-start(bf16[2,272,128]{2,1,0:T(8,128)(2,1)S(1)} %pad_maximum_fusion.3), channel_id=1, source_target_pairs={{0,4},{2,6},{4,0},{6,2},{1,5},{3,7},{5,1},{7,3},{8,12},{10,14},{12... | collective-permute-start | bytes 417800 | tf_op jit(solution)/shard_map/ppermute | solution.py:291
  21.6 12.5 %collective-permute-start.6 = (bf16[4,272,128]{2,1,0:T(8,128)(2,1)S(1)}, bf16[4,272,128]{2,1,0:T(8,128)(2,1)S(1)}, u32[]{:S(2)}, u32[]{:S(2)}) collective-permute-start(bf16[4,272,128]{2,1,0:T(8,128)(2,1)S(1)} %pad_maximum_fusion.2.own0), channel_id=1, source_target_pairs={{0,32},{16,48},{32,0},{48,16},{1,33},{17,49},{33,1},{49,17},{2,34}... | collective-permute-start | bytes 835592 | tf_op jit(solution)/shard_map/ppermute | solution.py:291
  24.3 12.6 %collective-permute-start.5 = (bf16[4,272,128]{2,1,0:T(8,128)(2,1)S(1)}, bf16[4,272,128]{2,1,0:T(8,128)(2,1)S(1)}, u32[]{:S(2)}, u32[]{:S(2)}) collective-permute-start(bf16[4,272,128]{2,1,0:T(8,128)(2,1)S(1)} %pad_maximum_fusion.2.own0), channel_id=1, source_target_pairs={{0,48},{16,32},{32,16},{48,0},{1,49},{17,33},{33,17},{49,1},{2,50}... | collective-permute-start | bytes 835592 | tf_op jit(solution)/shard_map/ppermute | solution.py:291
  25.2 11.7 %collective-permute-start.4 = (bf16[4,272,128]{2,1,0:T(8,128)(2,1)S(1)}, bf16[4,272,128]{2,1,0:T(8,128)(2,1)S(1)}, u32[]{:S(2)}, u32[]{:S(2)}) collective-permute-start(bf16[4,272,128]{2,1,0:T(8,128)(2,1)S(1)} %pad_maximum_fusion.2.own0), channel_id=1, source_target_pairs={{0,16},{16,0},{32,48},{48,32},{1,17},{17,1},{33,49},{49,33},{2,18}... | collective-permute-start | bytes 835592 | tf_op jit(solution)/shard_map/ppermute | solution.py:291
  25.2 5.4 %collective-permute-start.8 = (bf16[2,272,128]{2,1,0:T(8,128)(2,1)S(1)}, bf16[2,272,128]{2,1,0:T(8,128)(2,1)S(1)}, u32[]{:S(2)}, u32[]{:S(2)}) collective-permute-start(bf16[2,272,128]{2,1,0:T(8,128)(2,1)S(1)} %pad_maximum_fusion.3), channel_id=1, source_target_pairs={{0,6},{2,4},{4,2},{6,0},{1,7},{3,5},{5,3},{7,1},{8,14},{10,12},{12... | collective-permute-start | bytes 417800 | tf_op jit(solution)/shard_map/ppermute | solution.py:291
  26.0 8.1 %collective-permute-start.7 = (bf16[2,272,128]{2,1,0:T(8,128)(2,1)S(1)}, bf16[2,272,128]{2,1,0:T(8,128)(2,1)S(1)}, u32[]{:S(2)}, u32[]{:S(2)}) collective-permute-start(bf16[2,272,128]{2,1,0:T(8,128)(2,1)S(1)} %pad_maximum_fusion.3), channel_id=1, source_target_pairs={{0,2},{2,0},{4,6},{6,4},{1,3},{3,1},{5,7},{7,5},{8,10},{10,8},{12,... | collective-permute-start | bytes 417800 | tf_op jit(solution)/shard_map/ppermute | solution.py:291
  30.6 10.6 %collective-permute-start.11 = (bf16[4,272,128]{2,1,0:T(8,128)(2,1)S(1)}, bf16[4,272,128]{2,1,0:T(8,128)(2,1)S(1)}, u32[]{:S(2)}, u32[]{:S(2)}) collective-permute-start(bf16[4,272,128]{2,1,0:T(8,128)(2,1)S(1)} %pad_maximum_fusion.2.own0), channel_id=1, source_target_pairs={{0,8},{8,0},{1,9},{9,1},{2,10},{10,2},{3,11},{11,3},{4,12},{12,4},... | collective-permute-start | bytes 835592 | tf_op jit(solution)/shard_map/ppermute | solution.py:291
  36.9 4.3 %collective-permute-start.12 = (bf16[4,272,128]{2,1,0:T(8,128)(2,1)S(1)}, bf16[4,272,128]{2,1,0:T(8,128)(2,1)}, u32[]{:S(2)}, u32[]{:S(2)}) collective-permute-start(bf16[4,272,128]{2,1,0:T(8,128)(2,1)S(1)} %collective-permute-done.4.own1), channel_id=1, source_target_pairs={{0,8},{8,0},{1,9},{9,1},{2,10},{10,2},{3,11},{11,3},{4,12},{12,4},... | collective-permute-start | bytes 835592 | tf_op jit(solution)/shard_map/ppermute | solution.py:291
  38.2 2.9 %collective-permute-start.13 = (bf16[4,272,128]{2,1,0:T(8,128)(2,1)S(1)}, bf16[4,272,128]{2,1,0:T(8,128)(2,1)}, u32[]{:S(2)}, u32[]{:S(2)}) collective-permute-start(bf16[4,272,128]{2,1,0:T(8,128)(2,1)S(1)} %collective-permute-done.5.own2), channel_id=1, source_target_pairs={{0,8},{8,0},{1,9},{9,1},{2,10},{10,2},{3,11},{11,3},{4,12},{12,4},... | collective-permute-start | bytes 835592 | tf_op jit(solution)/shard_map/ppermute | solution.py:291
  38.2 2.9 %collective-permute-start.14 = (bf16[4,272,128]{2,1,0:T(8,128)(2,1)S(1)}, bf16[4,272,128]{2,1,0:T(8,128)(2,1)}, u32[]{:S(2)}, u32[]{:S(2)}) collective-permute-start(bf16[4,272,128]{2,1,0:T(8,128)(2,1)S(1)} %collective-permute-done.6.own3), channel_id=1, source_target_pairs={{0,8},{8,0},{1,9},{9,1},{2,10},{10,2},{3,11},{11,3},{4,12},{12,4},... | collective-permute-start | bytes 835592 | tf_op jit(solution)/shard_map/ppermute | solution.py:291
  40.9 5.8 %collective-permute-start.10 = (bf16[512,384]{1,0:T(8,128)(2,1)S(1)}, bf16[512,384]{1,0:T(8,128)(2,1)S(1)}, u32[]{:S(2)}, u32[]{:S(2)}) collective-permute-start(bf16[512,384]{1,0:T(8,128)(2,1)S(1)} %shard_map.114.own_source), channel_id=1, source_target_pairs={{0,8},{8,0},{1,9},{9,1},{2,10},{10,2},{3,11},{11,3},{4,12},{12,4},... | collective-permute-start | bytes 1179656 | tf_op jit(solution)/shard_map/ppermute | solution.py:291
  96.6 3.1 %collective-permute-start.15 = (f32[8,128]{1,0:T(8,128)S(1)}, f32[8,128]{1,0:T(8,128)S(1)}, u32[]{:S(2)}, u32[]{:S(2)}) collective-permute-start(f32[8,128]{1,0:T(8,128)S(1)} %subtract_add_fusion), channel_id=1, source_target_pairs={{0,8},{8,0},{1,9},{9,1},{2,10},{10,2},{3,11},{11,3},{4,12},{12,4},... | collective-permute-start | bytes 12296 | tf_op jit(solution)/shard_map/ppermute | solution.py:291

commit v9 on v8

--- a/solution.py
+++ b/solution.py
@@ -56,30 +56,24 @@
     )(*arrays)
 
 
-def graph_layers(packed, first, second, weights, x_ref, s_ref, h_ref, row_ref, link_ref, sem, emit, wanted):
+def graph_layers(packed, first, second, weights, x_ref, s_ref, h_ref, emit, wanted):
     count = x_ref.shape[0] // PART
-    lane = lax.broadcasted_iota(jnp.int32, (8, LANES), 1)
-    row = jnp.zeros((8, LANES), jnp.int32)
+    links = []
     for k in range(count):
         ref, at = packed(k)
-        link = ref[at, 4 * PART : PACK, :].astype(jnp.float32)[0:8]
-        row = jnp.where(lane == k, link.astype(jnp.int32), row)
-    row_ref[...] = row
-    copy = pltpu.make_async_copy(row_ref, link_ref, sem)
-    copy.start()
+        links.append(ref[at, 4 * PART : PACK, :].astype(jnp.float32)[0, 0].astype(jnp.int32))
     for k in range(count):
         ref, at = packed(k)
         for piece in range(D // LANES):
             x_ref[k * PART : (k + 1) * PART, piece * LANES : (piece + 1) * LANES] = ref[
                 at, piece * PART : (piece + 1) * PART, :
             ]
-    copy.wait()
 
     def neighbour_sums(src, count):
         for k in range(count):
             ref, at = packed(k)
             near = src[pl.ds(first(k) * PART, PART), :]
-            other = src[pl.ds(pl.multiple_of(second(link_ref[0, k]) * PART, PART), PART), :]
+            other = src[pl.ds(pl.multiple_of(second(links[k]) * PART, PART), PART), :]
             panel = ref[at, 3 * PART : 4 * PART, :]
             both = jnp.concatenate([near, other], axis=0)
             total = jnp.dot(panel, both, preferred_element_type=jnp.float32)
@@ -138,10 +132,10 @@
 
 
 def target_kernel(
-    place, own0, own1, own2, own3, other0, other1, other2, other3, weights, out, *scratch
+    place, own_near, own_rest, other_near, other_rest, weights, out, *scratch
 ):
     me = place[0]
-    pieces = (own0, own1, own2, own3, other0, other1, other2, other3)
+    near, rest = (own_near, other_near), (own_rest, other_rest)
 
     def emit(at, value):
         for piece in range(value.shape[0] // PART):
@@ -150,7 +144,7 @@
             out[pl.ds(pl.multiple_of(row, PART), PART), :] = value[piece * PART : (piece + 1) * PART, :]
 
     graph_layers(
-        lambda k: (pieces[k // 4], k % 4),
+        lambda k: (near[k // 16], k % 16) if k % 16 < 4 else (rest[k // 16], k % 16 - 4),
         lambda k: k ^ slot_of(31),
         lambda link: slot_of(link ^ me),
         weights, *scratch, emit, 16,
@@ -280,11 +274,7 @@
 
 
 def graph_scratch(rows):
-    return [pltpu.VMEM((rows, D), jnp.bfloat16)] * 3 + [
-        pltpu.VMEM((8, LANES), jnp.int32),
-        pltpu.SMEM((8, LANES), jnp.int32),
-        pltpu.SemaphoreType.DMA,
-    ]
+    return [pltpu.VMEM((rows, D), jnp.bfloat16)] * 3
 
 
 def swap(value, axis, size, xor):
@@ -306,20 +296,24 @@
     f32, bf16 = jnp.float32, jnp.bfloat16
     me = lax.axis_index(("zh", "x", "c"))
     me_source = lax.axis_index(("y", "zl"))
+    first = (me & 1) == 0
 
     held, source = pack(target_feats, target_tiles, target_links, source_feats, source_tiles, source_links)
-    held, source, *weights = lax.optimization_barrier(
-        (held, source, near_first, self_first, near_second, self_second)
+    held, source, me, me_source, first, *weights = lax.optimization_barrier(
+        (held, source, me, me_source, first, near_first, self_first, near_second, self_second)
     )
     weights = jnp.concatenate(weights, axis=0)
     source = jnp.concatenate([source, swap(source, "zl", 2, 1)], axis=0)
     held = jnp.concatenate(direct(held, "zh"), axis=0)
+    source = jnp.concatenate([source, swap(source, "y", 4, 1)], axis=0)
     held, source, weights = lax.optimization_barrier((held, source, weights))
-    source = direct(source, "y")
+    source = [source, swap(source, "y", 4, 3)]
     own = direct(held, "x")
     source = jnp.concatenate(source, axis=0)
-    own[1:], source = lax.optimization_barrier((own[1:], source))
-    other = [swap(piece, "c", 2, 1) for piece in own]
+    own = [own[0], jnp.concatenate(own[1:], axis=0)]
+    other_near = swap(own[0], "c", 2, 1)
+    own[1], other_near, source = lax.optimization_barrier((own[1], other_near, source))
+    other = [other_near, swap(own[1], "c", 2, 1)]
 
     (emb_source,) = call(
         source_kernel,
@@ -338,11 +332,9 @@
         target_kernel,
         [((COLS, D), bf16)],
         graph_scratch(BLOCK),
-        [SMEM()] + [VMEM()] * 9,
-        pl.CostEstimate(flops=2_400_000_000, bytes_accessed=4_000_000, transcendentals=0),
+        [SMEM()] + [VMEM()] * 5,
     )(me[None], *own, *other, weights)
 
-    emb_target, first = lax.optimization_barrier((emb_target, (me & 1) == 0))
     scores, send = call(
         score_kernel,
         [((COL_BLOCKS, ROWS, LANES), f32), ((N_ROW_PEERS, 2 * ROW_BLOCKS, LANES), f32)],

time: 101 us -> 98.6 us (0.976)
  starting transfers between devices: 25 us -> 22.2 us
  waiting for transfers between devices: 12.7 us -> 15 us
  Pallas kernels: 12.8 us -> 10.8 us
    ppermute x16 -> x13, starting transfers between devices: 25 us -> 22.2 us  [swap(): return lax.ppermute(value, axis, [(i, i ^ xor) for i in range(size)])]
    ppermute x16 -> x13, waiting for transfers between devices: 12.7 us -> 15 us  [swap(): return lax.ppermute(value, axis, [(i, i ^ xor) for i in range(size)])]
    pallas_call x1, Pallas kernels: 5.42 us -> 4.02 us  [on_device(): call(target_kernel, [((COLS, D), bf16)], graph_scratch(BLOCK), [SMEM()] +...]
  transfers between devices with their start and end apart: 16 -> 13, of which waited for: 4 -> 7; matrix products, arithmetic and copies ran while one was open for 2% -> 3% of each run, Pallas kernels for 7% -> 6%
where the time goes in v9:
time: 98.6 us; the launch traced here: 98.2 us
  blocking collectives  45.6 us (46%)
  starting transfers between devices  22.2 us (23%)
  waiting for transfers between devices  15 us (15%)
  Pallas kernels  10.8 us (11%)
  other arithmetic  3.75 us (4%)
    all_to_all x4, blocking collectives, exchange(): return lax.all_to_all(value, axes, 0, 0)  45.6 us
    ppermute x13, starting transfers between devices, swap(): return lax.ppermute(value, axis, [(i, i ^ xor) for i in range(size)])  22.2 us
    ppermute x13, waiting for transfers between devices, swap(): return lax.ppermute(value, axis, [(i, i ^ xor) for i in range(size)])  15 us
    pallas_call x1, Pallas kernels, on_device(): call(target_kernel, [((COLS, D), bf16)], graph_scratch(BLOCK), [SMEM()] +...  4.02 us
  transfers between devices with their start and end apart: 13, of which 7 were waited for; matrix products, arithmetic and copies ran while one was open for 3% of the time, Pallas kernels for 6%

profile of v9, /device:TPU:1, one launch (start us, length us, event | category | flops | bytes accessed | tf_op | source)
XLA Modules:
  0.0 98.2 jit_solution(3050986161707114990)
XLA Ops:
  0.6 1.6 %shard_map.113 = (bf16[1,272,128]{2,1,0:T(8,128)(2,1)}, bf16[1,272,128]{2,1,0:T(8,128)(2,1)}) custom-call(bf16[1,64,384]{2,1,0:T(8,128)(2,1)} %refs_0_.1, bf16[1,64,128]{2,1,0:T(8,128)(2,1)} %refs_1_.1, s32[1,1,2]{2,1,0:T(1,128)} %refs_2_.1, bf16[1,64,384]{2,1,0:T(8,128)(2,1)} %refs_3_.1, bf16[1,64,128]{2,1,0:T(8,128)(2,1)} %refs_4_.1, s32[1,1,2]{2,1,0:T(1,128)} %refs_5_.1), custom_call_target="tpu_custom_call" | custom-call | tf_op jit(solution)/shard_map/pallas_call | solution.py:50
  2.3 0.0 copy-start.1
  2.3 0.0 copy-start
  2.3 2.6 %collective-permute-start.3 = (bf16[1,272,128]{2,1,0:T(8,128)(2,1)}, bf16[1,272,128]{2,1,0:T(8,128)(2,1)S(1)}, u32[]{:S(2)}, u32[]{:S(2)}) collective-permute-start(bf16[1,272,128]{2,1,0:T(8,128)(2,1)} %get-tuple-element.39), channel_id=1, source_target_pairs={{0,1},{1,0},{2,3},{3,2},{4,5},{5,4},{6,7},{7,6},{8,9},{9,8},{10,11... | collective-permute-start | bytes 208904 | tf_op jit(solution)/shard_map/ppermute | solution.py:281
  4.9 6.0 %collective-permute-start.2 = (bf16[1,272,128]{2,1,0:T(8,128)(2,1)}, bf16[1,272,128]{2,1,0:T(8,128)(2,1)S(1)}, u32[]{:S(2)}, u32[]{:S(2)}) collective-permute-start(bf16[1,272,128]{2,1,0:T(8,128)(2,1)} %get-tuple-element.38), channel_id=1, source_target_pairs={{0,128},{64,192},{128,0},{192,64},{1,129},{65,193},{129,1},{193,65... | collective-permute-start | bytes 208904 | tf_op jit(solution)/shard_map/ppermute | solution.py:281
  10.9 0.3 collective-permute-start.1
  11.1 0.9 collective-permute-start
  12.1 0.0 collective-permute-done.3
  12.1 0.9 pad_maximum_fusion.5
  13.0 1.4 %collective-permute-start.4 = (bf16[2,272,128]{2,1,0:T(8,128)(2,1)S(1)}, bf16[2,272,128]{2,1,0:T(8,128)(2,1)S(1)}, u32[]{:S(2)}, u32[]{:S(2)}) collective-permute-start(bf16[2,272,128]{2,1,0:T(8,128)(2,1)S(1)} %pad_maximum_fusion.5), channel_id=1, source_target_pairs={{0,2},{2,0},{4,6},{6,4},{1,3},{3,1},{5,7},{7,5},{8,10},{10,8},{12,... | collective-permute-start | bytes 417800 | tf_op jit(solution)/shard_map/ppermute | solution.py:281
  14.4 1.3 %pad_maximum_fusion.weights = bf16[1536,384]{1,0:T(8,128)(2,1)S(1)} fusion(bf16[384,384]{1,0:T(8,128)(2,1)} %param.19, bf16[384,384]{1,0:T(8,128)(2,1)} %param.18, bf16[384,384]{1,0:T(8,128)(2,1)} %param.17, bf16[384,384]{1,0:T(8,128)(2,1)} %param.16), kind=kLoop, calls=%fused_computation | loop fusion | flops 4718592 | bytes 2359296 | tf_op jit(solution)/shard_map/concatenate | solution.py:305
  15.7 0.0 collective-permute-done.2
  15.7 1.8 %collective-permute-done.1 = bf16[1,272,128]{2,1,0:T(8,128)(2,1)S(1)} collective-permute-done((bf16[1,272,128]{2,1,0:T(8,128)(2,1)}, bf16[1,272,128]{2,1,0:T(8,128)(2,1)S(1)}, u32[]{:S(2)}, u32[]{:S(2)}) %collective-permute-start.1) | collective-permute-done | bytes 69664 | tf_op jit(solution)/shard_map/ppermute | solution.py:281
  17.5 1.8 %collective-permute-done = bf16[1,272,128]{2,1,0:T(8,128)(2,1)S(1)} collective-permute-done((bf16[1,272,128]{2,1,0:T(8,128)(2,1)}, bf16[1,272,128]{2,1,0:T(8,128)(2,1)S(1)}, u32[]{:S(2)}, u32[]{:S(2)}) %collective-permute-start) | collective-permute-done | bytes 69664 | tf_op jit(solution)/shard_map/ppermute | solution.py:281
  19.3 0.0 copy-done.1
  19.3 0.0 collective-permute-done.4
  19.3 0.0 copy-done
  19.4 2.8 %collective-permute-start.9 = (bf16[4,272,128]{2,1,0:T(8,128)(2,1)S(1)}, bf16[4,272,128]{2,1,0:T(8,128)(2,1)S(1)}, u32[]{:S(2)}, u32[]{:S(2)}) collective-permute-start(bf16[4,272,128]{2,1,0:T(8,128)(2,1)S(1)} %pad_maximum_fusion.4), channel_id=1, source_target_pairs={{0,6},{2,4},{4,2},{6,0},{1,7},{3,5},{5,3},{7,1},{8,14},{10,12},{12... | collective-permute-start | bytes 835592 | tf_op jit(solution)/shard_map/ppermute | solution.py:281
  22.2 2.7 %collective-permute-start.7 = (bf16[4,272,128]{2,1,0:T(8,128)(2,1)S(1)}, bf16[4,272,128]{2,1,0:T(8,128)(2,1)S(1)}, u32[]{:S(2)}, u32[]{:S(2)}) collective-permute-start(bf16[4,272,128]{2,1,0:T(8,128)(2,1)S(1)} %pad_maximum_fusion.3.own_near), channel_id=1, source_target_pairs={{0,32},{16,48},{32,0},{48,16},{1,33},{17,49},{33,1},{49,17},{2,34}... | collective-permute-start | bytes 835592 | tf_op jit(solution)/shard_map/ppermute | solution.py:281
  24.9 0.9 collective-permute-start.6
  25.8 0.0 collective-permute-start.5
  25.8 1.4 %collective-permute-start.8 = (bf16[4,272,128]{2,1,0:T(8,128)(2,1)S(1)}, bf16[4,272,128]{2,1,0:T(8,128)(2,1)S(1)}, u32[]{:S(2)}, u32[]{:S(2)}) collective-permute-start(bf16[4,272,128]{2,1,0:T(8,128)(2,1)S(1)} %pad_maximum_fusion.3.own_near), channel_id=1, source_target_pairs={{0,8},{8,0},{1,9},{9,1},{2,10},{10,2},{3,11},{11,3},{4,12},{12,4},... | collective-permute-start | bytes 835592 | tf_op jit(solution)/shard_map/ppermute | solution.py:281
  27.2 1.3 %collective-permute-done.9 = bf16[4,272,128]{2,1,0:T(8,128)(2,1)S(1)} collective-permute-done((bf16[4,272,128]{2,1,0:T(8,128)(2,1)S(1)}, bf16[4,272,128]{2,1,0:T(8,128)(2,1)S(1)}, u32[]{:S(2)}, u32[]{:S(2)}) %collective-permute-start.9) | collective-permute-done | bytes 278560 | tf_op jit(solution)/shard_map/ppermute | solution.py:281
  28.5 0.1 pad_maximum_fusion.2.packed
  28.6 2.6 %collective-permute-done.7 = bf16[4,272,128]{2,1,0:T(8,128)(2,1)S(1)} collective-permute-done((bf16[4,272,128]{2,1,0:T(8,128)(2,1)S(1)}, bf16[4,272,128]{2,1,0:T(8,128)(2,1)S(1)}, u32[]{:S(2)}, u32[]{:S(2)}) %collective-permute-start.7) | collective-permute-done | bytes 278560 | tf_op jit(solution)/shard_map/ppermute | solution.py:281
  31.1 7.1 %collective-permute-done.6 = bf16[4,272,128]{2,1,0:T(8,128)(2,1)S(1)} collective-permute-done((bf16[4,272,128]{2,1,0:T(8,128)(2,1)S(1)}, bf16[4,272,128]{2,1,0:T(8,128)(2,1)S(1)}, u32[]{:S(2)}, u32[]{:S(2)}) %collective-permute-start.6) | collective-permute-done | bytes 278560 | tf_op jit(solution)/shard_map/ppermute | solution.py:281
  38.3 0.0 collective-permute-done.5
  38.3 0.1 pad_maximum_fusion.1.own_rest
  38.4 0.0 collective-permute-done.8.other_near
  38.4 0.7 collective-permute-start.11
  39.1 1.5 %shard_map.114.own_source = bf16[512,384]{1,0:T(8,128)(2,1)S(1)} custom-call(s32[1]{0:T(128)} %bitcast.1.place, bf16[8,272,128]{2,1,0:T(8,128)(2,1)S(1)} %pad_maximum_fusion.2.packed, bf16[1536,384]{1,0:T(8,128)(2,1)S(1)} %pad_maximum_fusion.weights), custom_call_target="tpu_custom_call" | custom-call | flops 700000000 | bytes 2000000 | tf_op jit(solution)/shard_map/pallas_call | solution.py:318
  40.6 0.3 collective-permute-start.10
  40.9 0.1 collective-permute-done.11.other_rest
  41.1 4.0 %shard_map.115.emb_target = bf16[1024,384]{1,0:T(8,128)(2,1)S(1)} custom-call(s32[1]{0:T(128)} %bitcast.place, bf16[4,272,128]{2,1,0:T(8,128)(2,1)S(1)} %pad_maximum_fusion.3.own_near, bf16[12,272,128]{2,1,0:T(8,128)(2,1)S(1)} %pad_maximum_fusion.1.own_rest, bf16[4,272,128]{2,1,0:T(8,128)(2,1)S(1)} %collective-permute-done.8.other_near, ...), custom_call_target="tpu_custom_call" | custom-call | tf_op jit(solution)/shard_map/pallas_call | solution.py:331
  45.1 0.0 collective-permute-done.10.other_source
  45.1 1.7 %shard_map.116 = (f32[8,1024,128]{2,1,0:T(8,128)S(1)}, f32[16,16,128]{2,1,0:T(8,128)S(1)}) custom-call(s32[1]{0:T(128)} %bitcast.place, bf16[512,384]{1,0:T(8,128)(2,1)S(1)} %shard_map.114.own_source, bf16[512,384]{1,0:T(8,128)(2,1)S(1)} %collective-permute-done.10.other_source, bf16[1024,384]{1,0:T(8,128)(2,1)S(1)} %shard_map.115.emb_target), custom_call_target="tpu_custom_call" | custom-call | tf_op jit(solution)/shard_map/pallas_call | solution.py:338
  46.8 8.6 %all_to_all.20.got = f32[16,16,128]{2,1,0:T(8,128)S(1)} all-to-all(f32[16,16,128]{2,1,0:T(8,128)S(1)} %get-tuple-element.51), channel_id=1, replica_groups=mesh['zh'=4,'x'=4,'c'=2,'y'=4,'zl'=2] {'c','y','zl'}, dimensions={0} | all-to-all | bytes 262144 | tf_op jit(solution)/shard_map/all_to_all | solution.py:289
  55.4 1.1 %shard_map.117 = (f32[8,1024,128]{2,1,0:T(8,128)S(1)}, f32[8,8,128]{2,1,0:T(8,128)S(1)}, f32[16,8,128]{2,1,0:T(8,128)S(1)}, f32[8,128]{1,0:T(8,128)S(1)}) custom-call(f32[8,1024,128]{2,1,0:T(8,128)S(1)} %get-tuple-element.50.scores, f32[16,16,128]{2,1,0:T(8,128)S(1)} %all_to_all.20.got), custom_call_target="tpu_custom_call" | custom-call | tf_op jit(solution)/shard_map/pallas_call | solution.py:346
  56.5 15.0 %all_to_all.21.got = f32[16,8,128]{2,1,0:T(8,128)S(1)} all-to-all(f32[16,8,128]{2,1,0:T(8,128)S(1)} %get-tuple-element.54), channel_id=1, replica_groups=mesh['zh'=4,'x'=4,'c'=2,'y'=4,'zl'=2] {'zh','x'}, dimensions={0} | all-to-all | bytes 131072 | tf_op jit(solution)/shard_map/all_to_all | solution.py:289
  71.5 0.4 shard_map.118
  71.9 10.5 %all_to_all.22.got = f32[16,8,128]{2,1,0:T(8,128)S(1)} all-to-all(f32[16,8,128]{2,1,0:T(8,128)S(1)} %get-tuple-element.56), channel_id=1, replica_groups=mesh['zh'=4,'x'=4,'c'=2,'y'=4,'zl'=2] {'c','y','zl'}, dimensions={0} | all-to-all | bytes 131072 | tf_op jit(solution)/shard_map/all_to_all | solution.py:289
  82.4 0.4 shard_map.119
  82.8 11.5 %all_to_all.23 = f32[16,8,128]{2,1,0:T(8,128)S(1)} all-to-all(f32[16,8,128]{2,1,0:T(8,128)S(1)} %get-tuple-element.58), channel_id=1, replica_groups=mesh['zh'=4,'x'=4,'c'=2,'y'=4,'zl'=2] {'zh','x'}, dimensions={0} | all-to-all | bytes 131072 | tf_op jit(solution)/shard_map/all_to_all | solution.py:289
  94.4 2.2 %collective-permute-start.12 = (f32[8,128]{1,0:T(8,128)S(1)}, f32[8,128]{1,0:T(8,128)S(1)}, u32[]{:S(2)}, u32[]{:S(2)}) collective-permute-start(f32[8,128]{1,0:T(8,128)S(1)} %subtract_add_fusion), channel_id=1, source_target_pairs={{0,8},{8,0},{1,9},{9,1},{2,10},{10,2},{3,11},{11,3},{4,12},{12,4},... | collective-permute-start | bytes 12296 | tf_op jit(solution)/shard_map/ppermute | solution.py:281
  96.7 0.6 select_bitcast_fusion
  97.2 0.2 collective-permute-done.12
  97.5 0.1 fusion
  97.6 0.7 maximum_bitcast_fusion
  (5 shorter events, 0.1 us)
Async XLA Ops:
  2.3 17.0 %copy-start.1 = (bf16[1,272,128]{2,1,0:T(8,128)(2,1)S(1)}, bf16[1,272,128]{2,1,0:T(8,128)(2,1)}, u32[]{:S(2)}) copy-start(bf16[1,272,128]{2,1,0:T(8,128)(2,1)} %get-tuple-element.38) | copy-start | bytes 208900
  2.3 17.0 %copy-start = (bf16[1,272,128]{2,1,0:T(8,128)(2,1)S(1)}, bf16[1,272,128]{2,1,0:T(8,128)(2,1)}, u32[]{:S(2)}) copy-start(bf16[1,272,128]{2,1,0:T(8,128)(2,1)} %get-tuple-element.39) | copy-start | bytes 208900
  2.3 9.8 %collective-permute-start.3 = (bf16[1,272,128]{2,1,0:T(8,128)(2,1)}, bf16[1,272,128]{2,1,0:T(8,128)(2,1)S(1)}, u32[]{:S(2)}, u32[]{:S(2)}) collective-permute-start(bf16[1,272,128]{2,1,0:T(8,128)(2,1)} %get-tuple-element.39), channel_id=1, source_target_pairs={{0,1},{1,0},{2,3},{3,2},{4,5},{5,4},{6,7},{7,6},{8,9},{9,8},{10,11... | collective-permute-start | bytes 208904 | tf_op jit(solution)/shard_map/ppermute | solution.py:281
  4.9 10.8 %collective-permute-start.2 = (bf16[1,272,128]{2,1,0:T(8,128)(2,1)}, bf16[1,272,128]{2,1,0:T(8,128)(2,1)S(1)}, u32[]{:S(2)}, u32[]{:S(2)}) collective-permute-start(bf16[1,272,128]{2,1,0:T(8,128)(2,1)} %get-tuple-element.38), channel_id=1, source_target_pairs={{0,128},{64,192},{128,0},{192,64},{1,129},{65,193},{129,1},{193,65... | collective-permute-start | bytes 208904 | tf_op jit(solution)/shard_map/ppermute | solution.py:281
  10.9 6.6 %collective-permute-start.1 = (bf16[1,272,128]{2,1,0:T(8,128)(2,1)}, bf16[1,272,128]{2,1,0:T(8,128)(2,1)S(1)}, u32[]{:S(2)}, u32[]{:S(2)}) collective-permute-start(bf16[1,272,128]{2,1,0:T(8,128)(2,1)} %get-tuple-element.38), channel_id=1, source_target_pairs={{0,192},{64,128},{128,64},{192,0},{1,193},{65,129},{129,65},{193,1... | collective-permute-start | bytes 208904 | tf_op jit(solution)/shard_map/ppermute | solution.py:281
  11.1 8.1 %collective-permute-start = (bf16[1,272,128]{2,1,0:T(8,128)(2,1)}, bf16[1,272,128]{2,1,0:T(8,128)(2,1)S(1)}, u32[]{:S(2)}, u32[]{:S(2)}) collective-permute-start(bf16[1,272,128]{2,1,0:T(8,128)(2,1)} %get-tuple-element.38), channel_id=1, source_target_pairs={{0,64},{64,0},{128,192},{192,128},{1,65},{65,1},{129,193},{193,129... | collective-permute-start | bytes 208904 | tf_op jit(solution)/shard_map/ppermute | solution.py:281
  13.0 6.4 %collective-permute-start.4 = (bf16[2,272,128]{2,1,0:T(8,128)(2,1)S(1)}, bf16[2,272,128]{2,1,0:T(8,128)(2,1)S(1)}, u32[]{:S(2)}, u32[]{:S(2)}) collective-permute-start(bf16[2,272,128]{2,1,0:T(8,128)(2,1)S(1)} %pad_maximum_fusion.5), channel_id=1, source_target_pairs={{0,2},{2,0},{4,6},{6,4},{1,3},{3,1},{5,7},{7,5},{8,10},{10,8},{12,... | collective-permute-start | bytes 417800 | tf_op jit(solution)/shard_map/ppermute | solution.py:281
  19.4 9.1 %collective-permute-start.9 = (bf16[4,272,128]{2,1,0:T(8,128)(2,1)S(1)}, bf16[4,272,128]{2,1,0:T(8,128)(2,1)S(1)}, u32[]{:S(2)}, u32[]{:S(2)}) collective-permute-start(bf16[4,272,128]{2,1,0:T(8,128)(2,1)S(1)} %pad_maximum_fusion.4), channel_id=1, source_target_pairs={{0,6},{2,4},{4,2},{6,0},{1,7},{3,5},{5,3},{7,1},{8,14},{10,12},{12... | collective-permute-start | bytes 835592 | tf_op jit(solution)/shard_map/ppermute | solution.py:281
  22.2 8.9 %collective-permute-start.7 = (bf16[4,272,128]{2,1,0:T(8,128)(2,1)S(1)}, bf16[4,272,128]{2,1,0:T(8,128)(2,1)S(1)}, u32[]{:S(2)}, u32[]{:S(2)}) collective-permute-start(bf16[4,272,128]{2,1,0:T(8,128)(2,1)S(1)} %pad_maximum_fusion.3.own_near), channel_id=1, source_target_pairs={{0,32},{16,48},{32,0},{48,16},{1,33},{17,49},{33,1},{49,17},{2,34}... | collective-permute-start | bytes 835592 | tf_op jit(solution)/shard_map/ppermute | solution.py:281
  24.9 13.3 %collective-permute-start.6 = (bf16[4,272,128]{2,1,0:T(8,128)(2,1)S(1)}, bf16[4,272,128]{2,1,0:T(8,128)(2,1)S(1)}, u32[]{:S(2)}, u32[]{:S(2)}) collective-permute-start(bf16[4,272,128]{2,1,0:T(8,128)(2,1)S(1)} %pad_maximum_fusion.3.own_near), channel_id=1, source_target_pairs={{0,48},{16,32},{32,16},{48,0},{1,49},{17,33},{33,17},{49,1},{2,50}... | collective-permute-start | bytes 835592 | tf_op jit(solution)/shard_map/ppermute | solution.py:281
  25.8 12.4 %collective-permute-start.5 = (bf16[4,272,128]{2,1,0:T(8,128)(2,1)S(1)}, bf16[4,272,128]{2,1,0:T(8,128)(2,1)S(1)}, u32[]{:S(2)}, u32[]{:S(2)}) collective-permute-start(bf16[4,272,128]{2,1,0:T(8,128)(2,1)S(1)} %pad_maximum_fusion.3.own_near), channel_id=1, source_target_pairs={{0,16},{16,0},{32,48},{48,32},{1,17},{17,1},{33,49},{49,33},{2,18}... | collective-permute-start | bytes 835592 | tf_op jit(solution)/shard_map/ppermute | solution.py:281
  25.8 12.5 %collective-permute-start.8 = (bf16[4,272,128]{2,1,0:T(8,128)(2,1)S(1)}, bf16[4,272,128]{2,1,0:T(8,128)(2,1)S(1)}, u32[]{:S(2)}, u32[]{:S(2)}) collective-permute-start(bf16[4,272,128]{2,1,0:T(8,128)(2,1)S(1)} %pad_maximum_fusion.3.own_near), channel_id=1, source_target_pairs={{0,8},{8,0},{1,9},{9,1},{2,10},{10,2},{3,11},{11,3},{4,12},{12,4},... | collective-permute-start | bytes 835592 | tf_op jit(solution)/shard_map/ppermute | solution.py:281
  38.4 2.7 %collective-permute-start.11 = (bf16[12,272,128]{2,1,0:T(8,128)(2,1)S(1)}, bf16[12,272,128]{2,1,0:T(8,128)(2,1)S(1)}, u32[]{:S(2)}, u32[]{:S(2)}) collective-permute-start(bf16[12,272,128]{2,1,0:T(8,128)(2,1)S(1)} %pad_maximum_fusion.1.own_rest), channel_id=1, source_target_pairs={{0,8},{8,0},{1,9},{9,1},{2,10},{10,2},{3,11},{11,3},{4,12},{12,4},... | collective-permute-start | bytes 2506760 | tf_op jit(solution)/shard_map/ppermute | solution.py:281
  40.6 4.5 %collective-permute-start.10 = (bf16[512,384]{1,0:T(8,128)(2,1)S(1)}, bf16[512,384]{1,0:T(8,128)(2,1)S(1)}, u32[]{:S(2)}, u32[]{:S(2)}) collective-permute-start(bf16[512,384]{1,0:T(8,128)(2,1)S(1)} %shard_map.114.own_source), channel_id=1, source_target_pairs={{0,8},{8,0},{1,9},{9,1},{2,10},{10,2},{3,11},{11,3},{4,12},{12,4},... | collective-permute-start | bytes 1179656 | tf_op jit(solution)/shard_map/ppermute | solution.py:281
  94.4 3.1 %collective-permute-start.12 = (f32[8,128]{1,0:T(8,128)S(1)}, f32[8,128]{1,0:T(8,128)S(1)}, u32[]{:S(2)}, u32[]{:S(2)}) collective-permute-start(f32[8,128]{1,0:T(8,128)S(1)} %subtract_add_fusion), channel_id=1, source_target_pairs={{0,8},{8,0},{1,9},{9,1},{2,10},{10,2},{3,11},{11,3},{4,12},{12,4},... | collective-permute-start | bytes 12296 | tf_op jit(solution)/shard_map/ppermute | solution.py:281

commit v10 on v9

--- a/solution.py
+++ b/solution.py
@@ -92,20 +92,28 @@
         emit(at, mix(h_ref, at, 1).astype(jnp.bfloat16))
 
 
-def turn(v):
-    return v ^ (v >> 1)
+Z_ORDER = (2, 3, 1)
+X_ORDER = (1, 3, 2)
+
+
+def turn(v, order):
+    return ((v & 1) * order[0]) ^ ((v >> 1) * order[1])
+
+
+def place_of(v, order):
+    return turn(v, (order.index(1) + 1, order.index(2) + 1))
 
 
 def slot_xor(k):
-    return (turn(k & 3) << 3) | (turn((k >> 2) & 3) << 1) | (k >> 4)
+    return (turn(k & 3, Z_ORDER) << 3) | (turn((k >> 2) & 3, X_ORDER) << 1) | (k >> 4)
 
 
 def slot_of(v):
-    return turn(v >> 3) | (turn((v >> 1) & 3) << 2) | ((v & 1) << 4)
+    return place_of(v >> 3, Z_ORDER) | (place_of((v >> 1) & 3, X_ORDER) << 2) | ((v & 1) << 4)
 
 
 def source_xor(k):
-    return (turn(k >> 1) << 1) | (k & 1)
+    return (turn(k >> 1, (1, 3)) << 1) | (k & 1)
 
 
 source_of = source_xor
@@ -281,8 +289,8 @@
     return lax.ppermute(value, axis, [(i, i ^ xor) for i in range(size)])
 
 
-def direct(value, axis):
-    return [value] + [swap(value, axis, 4, xor) for xor in (1, 3, 2)]
+def direct(value, axis, order):
+    return [value] + [swap(value, axis, 4, xor) for xor in order]
 
 
 def exchange(value, axes):
@@ -304,16 +312,14 @@
     )
     weights = jnp.concatenate(weights, axis=0)
     source = jnp.concatenate([source, swap(source, "zl", 2, 1)], axis=0)
-    held = jnp.concatenate(direct(held, "zh"), axis=0)
+    held = jnp.concatenate(direct(held, "zh", Z_ORDER), axis=0)
     source = jnp.concatenate([source, swap(source, "y", 4, 1)], axis=0)
     held, source, weights = lax.optimization_barrier((held, source, weights))
     source = [source, swap(source, "y", 4, 3)]
-    own = direct(held, "x")
+    own = direct(held, "x", X_ORDER)
     source = jnp.concatenate(source, axis=0)
     own = [own[0], jnp.concatenate(own[1:], axis=0)]
     other_near = swap(own[0], "c", 2, 1)
-    own[1], other_near, source = lax.optimization_barrier((own[1], other_near, source))
-    other = [other_near, swap(own[1], "c", 2, 1)]
 
     (emb_source,) = call(
         source_kernel,
@@ -326,6 +332,8 @@
         source,
         weights,
     )
+    own[1], other_near, emb_source = lax.optimization_barrier((own[1], other_near, emb_source))
+    other = [other_near, swap(own[1], "c", 2, 1)]
     other_source = swap(emb_source, "c", 2, 1)
 
     (emb_target,) = call(

time: 98.6 us -> 98.1 us (level)
  waiting for transfers between devices: 15 us -> 12.5 us
  starting transfers between devices: 22.2 us -> 24.5 us
    ppermute x13, waiting for transfers between devices: 15 us -> 12.5 us  [swap(): return lax.ppermute(value, axis, [(i, i ^ xor) for i in range(size)])]
    ppermute x13, starting transfers between devices: 22.2 us -> 24.5 us  [swap(): return lax.ppermute(value, axis, [(i, i ^ xor) for i in range(size)])]
  transfers between devices with their start and end apart: 13 -> 13, of which waited for: 7 -> 4; matrix products, arithmetic and copies ran while one was open for 3% -> 3% of each run, Pallas kernels for 6% -> 6%
where the time goes in v10:
time: 98.1 us; the launch traced here: 97.8 us
  blocking collectives  45.3 us (46%)
  starting transfers between devices  24.5 us (25%)
  waiting for transfers between devices  12.5 us (13%)
  Pallas kernels  10.8 us (11%)
  other arithmetic  3.74 us (4%)
    all_to_all x4, blocking collectives, exchange(): return lax.all_to_all(value, axes, 0, 0)  45.3 us
    ppermute x13, starting transfers between devices, swap(): return lax.ppermute(value, axis, [(i, i ^ xor) for i in range(size)])  24.5 us
    ppermute x13, waiting for transfers between devices, swap(): return lax.ppermute(value, axis, [(i, i ^ xor) for i in range(size)])  12.5 us
    pallas_call x1, Pallas kernels, on_device(): call(target_kernel, [((COLS, D), bf16)], graph_scratch(BLOCK), [SMEM()] +...  4.03 us
  transfers between devices with their start and end apart: 13, of which 4 were waited for; matrix products, arithmetic and copies ran while one was open for 3% of the time, Pallas kernels for 6%

profile of v10, /device:TPU:1, one launch (start us, length us, event | category | flops | bytes accessed | tf_op | source)
XLA Modules:
  0.0 97.8 jit_solution(14798861020175038270)
XLA Ops:
  0.6 1.6 %shard_map.113 = (bf16[1,272,128]{2,1,0:T(8,128)(2,1)}, bf16[1,272,128]{2,1,0:T(8,128)(2,1)}) custom-call(bf16[1,64,384]{2,1,0:T(8,128)(2,1)} %refs_0_.1, bf16[1,64,128]{2,1,0:T(8,128)(2,1)} %refs_1_.1, s32[1,1,2]{2,1,0:T(1,128)} %refs_2_.1, bf16[1,64,384]{2,1,0:T(8,128)(2,1)} %refs_3_.1, bf16[1,64,128]{2,1,0:T(8,128)(2,1)} %refs_4_.1, s32[1,1,2]{2,1,0:T(1,128)} %refs_5_.1), custom_call_target="tpu_custom_call" | custom-call | tf_op jit(solution)/shard_map/pallas_call | solution.py:50
  2.3 0.0 copy-start.1
  2.3 0.0 copy-start
  2.3 2.6 %collective-permute-start.3 = (bf16[1,272,128]{2,1,0:T(8,128)(2,1)}, bf16[1,272,128]{2,1,0:T(8,128)(2,1)S(1)}, u32[]{:S(2)}, u32[]{:S(2)}) collective-permute-start(bf16[1,272,128]{2,1,0:T(8,128)(2,1)} %get-tuple-element.38), channel_id=1, source_target_pairs={{0,1},{1,0},{2,3},{3,2},{4,5},{5,4},{6,7},{7,6},{8,9},{9,8},{10,11... | collective-permute-start | bytes 208904 | tf_op jit(solution)/shard_map/ppermute | solution.py:289
  4.9 3.0 %collective-permute-start.2 = (bf16[1,272,128]{2,1,0:T(8,128)(2,1)}, bf16[1,272,128]{2,1,0:T(8,128)(2,1)S(1)}, u32[]{:S(2)}, u32[]{:S(2)}) collective-permute-start(bf16[1,272,128]{2,1,0:T(8,128)(2,1)} %get-tuple-element.37), channel_id=1, source_target_pairs={{0,64},{64,0},{128,192},{192,128},{1,65},{65,1},{129,193},{193,129... | collective-permute-start | bytes 208904 | tf_op jit(solution)/shard_map/ppermute | solution.py:289
  7.9 3.3 %collective-permute-start.1 = (bf16[1,272,128]{2,1,0:T(8,128)(2,1)}, bf16[1,272,128]{2,1,0:T(8,128)(2,1)S(1)}, u32[]{:S(2)}, u32[]{:S(2)}) collective-permute-start(bf16[1,272,128]{2,1,0:T(8,128)(2,1)} %get-tuple-element.37), channel_id=1, source_target_pairs={{0,192},{64,128},{128,64},{192,0},{1,193},{65,129},{129,65},{193,1... | collective-permute-start | bytes 208904 | tf_op jit(solution)/shard_map/ppermute | solution.py:289
  11.2 0.9 collective-permute-start
  12.1 0.0 collective-permute-done.3
  12.1 0.9 pad_maximum_fusion.5
  13.0 1.4 %collective-permute-start.4 = (bf16[2,272,128]{2,1,0:T(8,128)(2,1)S(1)}, bf16[2,272,128]{2,1,0:T(8,128)(2,1)S(1)}, u32[]{:S(2)}, u32[]{:S(2)}) collective-permute-start(bf16[2,272,128]{2,1,0:T(8,128)(2,1)S(1)} %pad_maximum_fusion.5), channel_id=1, source_target_pairs={{0,2},{2,0},{4,6},{6,4},{1,3},{3,1},{5,7},{7,5},{8,10},{10,8},{12,... | collective-permute-start | bytes 417800 | tf_op jit(solution)/shard_map/ppermute | solution.py:289
  14.4 1.3 %pad_maximum_fusion.weights = bf16[1536,384]{1,0:T(8,128)(2,1)S(1)} fusion(bf16[384,384]{1,0:T(8,128)(2,1)} %param.19, bf16[384,384]{1,0:T(8,128)(2,1)} %param.18, bf16[384,384]{1,0:T(8,128)(2,1)} %param.17, bf16[384,384]{1,0:T(8,128)(2,1)} %param.16), kind=kLoop, calls=%fused_computation | loop fusion | flops 4718592 | bytes 2359296 | tf_op jit(solution)/shard_map/concatenate | solution.py:313
  15.7 0.0 collective-permute-done.2
  15.7 0.0 collective-permute-done.1
  15.7 3.5 %collective-permute-done = bf16[1,272,128]{2,1,0:T(8,128)(2,1)S(1)} collective-permute-done((bf16[1,272,128]{2,1,0:T(8,128)(2,1)}, bf16[1,272,128]{2,1,0:T(8,128)(2,1)S(1)}, u32[]{:S(2)}, u32[]{:S(2)}) %collective-permute-start) | collective-permute-done | bytes 69664 | tf_op jit(solution)/shard_map/ppermute | solution.py:289
  19.2 0.0 copy-done.1
  19.2 0.0 collective-permute-done.4
  19.2 0.0 copy-done
  19.3 2.8 %collective-permute-start.9 = (bf16[4,272,128]{2,1,0:T(8,128)(2,1)S(1)}, bf16[4,272,128]{2,1,0:T(8,128)(2,1)S(1)}, u32[]{:S(2)}, u32[]{:S(2)}) collective-permute-start(bf16[4,272,128]{2,1,0:T(8,128)(2,1)S(1)} %pad_maximum_fusion.4), channel_id=1, source_target_pairs={{0,6},{2,4},{4,2},{6,0},{1,7},{3,5},{5,3},{7,1},{8,14},{10,12},{12... | collective-permute-start | bytes 835592 | tf_op jit(solution)/shard_map/ppermute | solution.py:289
  22.1 2.7 %collective-permute-start.7 = (bf16[4,272,128]{2,1,0:T(8,128)(2,1)S(1)}, bf16[4,272,128]{2,1,0:T(8,128)(2,1)S(1)}, u32[]{:S(2)}, u32[]{:S(2)}) collective-permute-start(bf16[4,272,128]{2,1,0:T(8,128)(2,1)S(1)} %pad_maximum_fusion.3.own_near), channel_id=1, source_target_pairs={{0,32},{16,48},{32,0},{48,16},{1,33},{17,49},{33,1},{49,17},{2,34}... | collective-permute-start | bytes 835592 | tf_op jit(solution)/shard_map/ppermute | solution.py:289
  24.9 0.9 collective-permute-start.6
  25.7 0.0 collective-permute-start.5
  25.7 2.8 %collective-permute-start.8 = (bf16[4,272,128]{2,1,0:T(8,128)(2,1)S(1)}, bf16[4,272,128]{2,1,0:T(8,128)(2,1)S(1)}, u32[]{:S(2)}, u32[]{:S(2)}) collective-permute-start(bf16[4,272,128]{2,1,0:T(8,128)(2,1)S(1)} %pad_maximum_fusion.3.own_near), channel_id=1, source_target_pairs={{0,8},{8,0},{1,9},{9,1},{2,10},{10,2},{3,11},{11,3},{4,12},{12,4},... | collective-permute-start | bytes 835592 | tf_op jit(solution)/shard_map/ppermute | solution.py:289
  28.6 0.0 collective-permute-done.9
  28.6 0.1 pad_maximum_fusion.2.packed
  28.6 1.5 %shard_map.114.own_source = bf16[512,384]{1,0:T(8,128)(2,1)S(1)} custom-call(s32[1]{0:T(128)} %bitcast.1.place, bf16[8,272,128]{2,1,0:T(8,128)(2,1)S(1)} %pad_maximum_fusion.2.packed, bf16[1536,384]{1,0:T(8,128)(2,1)S(1)} %pad_maximum_fusion.weights), custom_call_target="tpu_custom_call" | custom-call | flops 700000000 | bytes 2000000 | tf_op jit(solution)/shard_map/pallas_call | solution.py:324
  30.2 0.0 collective-permute-done.7
  30.2 7.1 %collective-permute-done.6 = bf16[4,272,128]{2,1,0:T(8,128)(2,1)S(1)} collective-permute-done((bf16[4,272,128]{2,1,0:T(8,128)(2,1)S(1)}, bf16[4,272,128]{2,1,0:T(8,128)(2,1)S(1)}, u32[]{:S(2)}, u32[]{:S(2)}) %collective-permute-start.6) | collective-permute-done | bytes 278560 | tf_op jit(solution)/shard_map/ppermute | solution.py:289
  37.3 0.0 collective-permute-done.5
  37.3 0.1 pad_maximum_fusion.1.own_rest
  37.4 0.0 collective-permute-done.8.other_near
  37.4 1.6 %collective-permute-start.11 = (bf16[12,272,128]{2,1,0:T(8,128)(2,1)S(1)}, bf16[12,272,128]{2,1,0:T(8,128)(2,1)S(1)}, u32[]{:S(2)}, u32[]{:S(2)}) collective-permute-start(bf16[12,272,128]{2,1,0:T(8,128)(2,1)S(1)} %pad_maximum_fusion.1.own_rest), channel_id=1, source_target_pairs={{0,8},{8,0},{1,9},{9,1},{2,10},{10,2},{3,11},{11,3},{4,12},{12,4},... | collective-permute-start | bytes 2506760 | tf_op jit(solution)/shard_map/ppermute | solution.py:289
  39.0 0.3 collective-permute-start.10
  39.3 1.7 %collective-permute-done.11.other_rest = bf16[12,272,128]{2,1,0:T(8,128)(2,1)S(1)} collective-permute-done((bf16[12,272,128]{2,1,0:T(8,128)(2,1)S(1)}, bf16[12,272,128]{2,1,0:T(8,128)(2,1)S(1)}, u32[]{:S(2)}, u32[]{:S(2)}) %collective-permute-start.11) | collective-permute-done | bytes 835616 | tf_op jit(solution)/shard_map/ppermute | solution.py:289
  41.0 4.0 %shard_map.115.emb_target = bf16[1024,384]{1,0:T(8,128)(2,1)S(1)} custom-call(s32[1]{0:T(128)} %bitcast.place, bf16[4,272,128]{2,1,0:T(8,128)(2,1)S(1)} %pad_maximum_fusion.3.own_near, bf16[12,272,128]{2,1,0:T(8,128)(2,1)S(1)} %pad_maximum_fusion.1.own_rest, bf16[4,272,128]{2,1,0:T(8,128)(2,1)S(1)} %collective-permute-done.8.other_near, ...), custom_call_target="tpu_custom_call" | custom-call | tf_op jit(solution)/shard_map/pallas_call | solution.py:339
  45.0 0.0 collective-permute-done.10.other_source
  45.0 1.7 %shard_map.116 = (f32[8,1024,128]{2,1,0:T(8,128)S(1)}, f32[16,16,128]{2,1,0:T(8,128)S(1)}) custom-call(s32[1]{0:T(128)} %bitcast.place, bf16[512,384]{1,0:T(8,128)(2,1)S(1)} %shard_map.114.own_source, bf16[512,384]{1,0:T(8,128)(2,1)S(1)} %collective-permute-done.10.other_source, bf16[1024,384]{1,0:T(8,128)(2,1)S(1)} %shard_map.115.emb_target), custom_call_target="tpu_custom_call" | custom-call | tf_op jit(solution)/shard_map/pallas_call | solution.py:346
  46.7 8.6 %all_to_all.20.got = f32[16,16,128]{2,1,0:T(8,128)S(1)} all-to-all(f32[16,16,128]{2,1,0:T(8,128)S(1)} %get-tuple-element.51), channel_id=1, replica_groups=mesh['zh'=4,'x'=4,'c'=2,'y'=4,'zl'=2] {'c','y','zl'}, dimensions={0} | all-to-all | bytes 262144 | tf_op jit(solution)/shard_map/all_to_all | solution.py:297
  55.3 1.1 %shard_map.117 = (f32[8,1024,128]{2,1,0:T(8,128)S(1)}, f32[8,8,128]{2,1,0:T(8,128)S(1)}, f32[16,8,128]{2,1,0:T(8,128)S(1)}, f32[8,128]{1,0:T(8,128)S(1)}) custom-call(f32[8,1024,128]{2,1,0:T(8,128)S(1)} %get-tuple-element.50.scores, f32[16,16,128]{2,1,0:T(8,128)S(1)} %all_to_all.20.got), custom_call_target="tpu_custom_call" | custom-call | tf_op jit(solution)/shard_map/pallas_call | solution.py:354
  56.4 14.6 %all_to_all.21.got = f32[16,8,128]{2,1,0:T(8,128)S(1)} all-to-all(f32[16,8,128]{2,1,0:T(8,128)S(1)} %get-tuple-element.54), channel_id=1, replica_groups=mesh['zh'=4,'x'=4,'c'=2,'y'=4,'zl'=2] {'zh','x'}, dimensions={0} | all-to-all | bytes 131072 | tf_op jit(solution)/shard_map/all_to_all | solution.py:297
  71.0 0.4 shard_map.118
  71.4 10.6 %all_to_all.22.got = f32[16,8,128]{2,1,0:T(8,128)S(1)} all-to-all(f32[16,8,128]{2,1,0:T(8,128)S(1)} %get-tuple-element.56), channel_id=1, replica_groups=mesh['zh'=4,'x'=4,'c'=2,'y'=4,'zl'=2] {'c','y','zl'}, dimensions={0} | all-to-all | bytes 131072 | tf_op jit(solution)/shard_map/all_to_all | solution.py:297
  82.0 0.4 shard_map.119
  82.4 11.5 %all_to_all.23 = f32[16,8,128]{2,1,0:T(8,128)S(1)} all-to-all(f32[16,8,128]{2,1,0:T(8,128)S(1)} %get-tuple-element.58), channel_id=1, replica_groups=mesh['zh'=4,'x'=4,'c'=2,'y'=4,'zl'=2] {'zh','x'}, dimensions={0} | all-to-all | bytes 131072 | tf_op jit(solution)/shard_map/all_to_all | solution.py:297
  93.9 2.2 %collective-permute-start.12 = (f32[8,128]{1,0:T(8,128)S(1)}, f32[8,128]{1,0:T(8,128)S(1)}, u32[]{:S(2)}, u32[]{:S(2)}) collective-permute-start(f32[8,128]{1,0:T(8,128)S(1)} %subtract_add_fusion), channel_id=1, source_target_pairs={{0,8},{8,0},{1,9},{9,1},{2,10},{10,2},{3,11},{11,3},{4,12},{12,4},... | collective-permute-start | bytes 12296 | tf_op jit(solution)/shard_map/ppermute | solution.py:289
  96.2 0.6 select_bitcast_fusion
  96.8 0.2 collective-permute-done.12
  97.0 0.1 fusion
  97.1 0.7 maximum_bitcast_fusion
  (5 shorter events, 0.1 us)
Async XLA Ops:
  2.3 16.9 %copy-start.1 = (bf16[1,272,128]{2,1,0:T(8,128)(2,1)S(1)}, bf16[1,272,128]{2,1,0:T(8,128)(2,1)}, u32[]{:S(2)}) copy-start(bf16[1,272,128]{2,1,0:T(8,128)(2,1)} %get-tuple-element.37) | copy-start | bytes 208900
  2.3 17.0 %copy-start = (bf16[1,272,128]{2,1,0:T(8,128)(2,1)S(1)}, bf16[1,272,128]{2,1,0:T(8,128)(2,1)}, u32[]{:S(2)}) copy-start(bf16[1,272,128]{2,1,0:T(8,128)(2,1)} %get-tuple-element.38) | copy-start | bytes 208900
  2.3 9.8 %collective-permute-start.3 = (bf16[1,272,128]{2,1,0:T(8,128)(2,1)}, bf16[1,272,128]{2,1,0:T(8,128)(2,1)S(1)}, u32[]{:S(2)}, u32[]{:S(2)}) collective-permute-start(bf16[1,272,128]{2,1,0:T(8,128)(2,1)} %get-tuple-element.38), channel_id=1, source_target_pairs={{0,1},{1,0},{2,3},{3,2},{4,5},{5,4},{6,7},{7,6},{8,9},{9,8},{10,11... | collective-permute-start | bytes 208904 | tf_op jit(solution)/shard_map/ppermute | solution.py:289
  4.9 10.8 %collective-permute-start.2 = (bf16[1,272,128]{2,1,0:T(8,128)(2,1)}, bf16[1,272,128]{2,1,0:T(8,128)(2,1)S(1)}, u32[]{:S(2)}, u32[]{:S(2)}) collective-permute-start(bf16[1,272,128]{2,1,0:T(8,128)(2,1)} %get-tuple-element.37), channel_id=1, source_target_pairs={{0,64},{64,0},{128,192},{192,128},{1,65},{65,1},{129,193},{193,129... | collective-permute-start | bytes 208904 | tf_op jit(solution)/shard_map/ppermute | solution.py:289
  7.9 7.9 %collective-permute-start.1 = (bf16[1,272,128]{2,1,0:T(8,128)(2,1)}, bf16[1,272,128]{2,1,0:T(8,128)(2,1)S(1)}, u32[]{:S(2)}, u32[]{:S(2)}) collective-permute-start(bf16[1,272,128]{2,1,0:T(8,128)(2,1)} %get-tuple-element.37), channel_id=1, source_target_pairs={{0,192},{64,128},{128,64},{192,0},{1,193},{65,129},{129,65},{193,1... | collective-permute-start | bytes 208904 | tf_op jit(solution)/shard_map/ppermute | solution.py:289
  11.2 8.0 %collective-permute-start = (bf16[1,272,128]{2,1,0:T(8,128)(2,1)}, bf16[1,272,128]{2,1,0:T(8,128)(2,1)S(1)}, u32[]{:S(2)}, u32[]{:S(2)}) collective-permute-start(bf16[1,272,128]{2,1,0:T(8,128)(2,1)} %get-tuple-element.37), channel_id=1, source_target_pairs={{0,128},{64,192},{128,0},{192,64},{1,129},{65,193},{129,1},{193,65... | collective-permute-start | bytes 208904 | tf_op jit(solution)/shard_map/ppermute | solution.py:289
  13.0 6.3 %collective-permute-start.4 = (bf16[2,272,128]{2,1,0:T(8,128)(2,1)S(1)}, bf16[2,272,128]{2,1,0:T(8,128)(2,1)S(1)}, u32[]{:S(2)}, u32[]{:S(2)}) collective-permute-start(bf16[2,272,128]{2,1,0:T(8,128)(2,1)S(1)} %pad_maximum_fusion.5), channel_id=1, source_target_pairs={{0,2},{2,0},{4,6},{6,4},{1,3},{3,1},{5,7},{7,5},{8,10},{10,8},{12,... | collective-permute-start | bytes 417800 | tf_op jit(solution)/shard_map/ppermute | solution.py:289
  19.3 9.3 %collective-permute-start.9 = (bf16[4,272,128]{2,1,0:T(8,128)(2,1)S(1)}, bf16[4,272,128]{2,1,0:T(8,128)(2,1)S(1)}, u32[]{:S(2)}, u32[]{:S(2)}) collective-permute-start(bf16[4,272,128]{2,1,0:T(8,128)(2,1)S(1)} %pad_maximum_fusion.4), channel_id=1, source_target_pairs={{0,6},{2,4},{4,2},{6,0},{1,7},{3,5},{5,3},{7,1},{8,14},{10,12},{12... | collective-permute-start | bytes 835592 | tf_op jit(solution)/shard_map/ppermute | solution.py:289
  22.1 8.1 %collective-permute-start.7 = (bf16[4,272,128]{2,1,0:T(8,128)(2,1)S(1)}, bf16[4,272,128]{2,1,0:T(8,128)(2,1)S(1)}, u32[]{:S(2)}, u32[]{:S(2)}) collective-permute-start(bf16[4,272,128]{2,1,0:T(8,128)(2,1)S(1)} %pad_maximum_fusion.3.own_near), channel_id=1, source_target_pairs={{0,32},{16,48},{32,0},{48,16},{1,33},{17,49},{33,1},{49,17},{2,34}... | collective-permute-start | bytes 835592 | tf_op jit(solution)/shard_map/ppermute | solution.py:289
  24.9 12.4 %collective-permute-start.6 = (bf16[4,272,128]{2,1,0:T(8,128)(2,1)S(1)}, bf16[4,272,128]{2,1,0:T(8,128)(2,1)S(1)}, u32[]{:S(2)}, u32[]{:S(2)}) collective-permute-start(bf16[4,272,128]{2,1,0:T(8,128)(2,1)S(1)} %pad_maximum_fusion.3.own_near), channel_id=1, source_target_pairs={{0,48},{16,32},{32,16},{48,0},{1,49},{17,33},{33,17},{49,1},{2,50}... | collective-permute-start | bytes 835592 | tf_op jit(solution)/shard_map/ppermute | solution.py:289
  25.7 11.6 %collective-permute-start.5 = (bf16[4,272,128]{2,1,0:T(8,128)(2,1)S(1)}, bf16[4,272,128]{2,1,0:T(8,128)(2,1)S(1)}, u32[]{:S(2)}, u32[]{:S(2)}) collective-permute-start(bf16[4,272,128]{2,1,0:T(8,128)(2,1)S(1)} %pad_maximum_fusion.3.own_near), channel_id=1, source_target_pairs={{0,16},{16,0},{32,48},{48,32},{1,17},{17,1},{33,49},{49,33},{2,18}... | collective-permute-start | bytes 835592 | tf_op jit(solution)/shard_map/ppermute | solution.py:289
  25.7 11.6 %collective-permute-start.8 = (bf16[4,272,128]{2,1,0:T(8,128)(2,1)S(1)}, bf16[4,272,128]{2,1,0:T(8,128)(2,1)S(1)}, u32[]{:S(2)}, u32[]{:S(2)}) collective-permute-start(bf16[4,272,128]{2,1,0:T(8,128)(2,1)S(1)} %pad_maximum_fusion.3.own_near), channel_id=1, source_target_pairs={{0,8},{8,0},{1,9},{9,1},{2,10},{10,2},{3,11},{11,3},{4,12},{12,4},... | collective-permute-start | bytes 835592 | tf_op jit(solution)/shard_map/ppermute | solution.py:289
  37.4 3.6 %collective-permute-start.11 = (bf16[12,272,128]{2,1,0:T(8,128)(2,1)S(1)}, bf16[12,272,128]{2,1,0:T(8,128)(2,1)S(1)}, u32[]{:S(2)}, u32[]{:S(2)}) collective-permute-start(bf16[12,272,128]{2,1,0:T(8,128)(2,1)S(1)} %pad_maximum_fusion.1.own_rest), channel_id=1, source_target_pairs={{0,8},{8,0},{1,9},{9,1},{2,10},{10,2},{3,11},{11,3},{4,12},{12,4},... | collective-permute-start | bytes 2506760 | tf_op jit(solution)/shard_map/ppermute | solution.py:289
  39.0 6.0 %collective-permute-start.10 = (bf16[512,384]{1,0:T(8,128)(2,1)S(1)}, bf16[512,384]{1,0:T(8,128)(2,1)S(1)}, u32[]{:S(2)}, u32[]{:S(2)}) collective-permute-start(bf16[512,384]{1,0:T(8,128)(2,1)S(1)} %shard_map.114.own_source), channel_id=1, source_target_pairs={{0,8},{8,0},{1,9},{9,1},{2,10},{10,2},{3,11},{11,3},{4,12},{12,4},... | collective-permute-start | bytes 1179656 | tf_op jit(solution)/shard_map/ppermute | solution.py:289
  93.9 3.1 %collective-permute-start.12 = (f32[8,128]{1,0:T(8,128)S(1)}, f32[8,128]{1,0:T(8,128)S(1)}, u32[]{:S(2)}, u32[]{:S(2)}) collective-permute-start(f32[8,128]{1,0:T(8,128)S(1)} %subtract_add_fusion), channel_id=1, source_target_pairs={{0,8},{8,0},{1,9},{9,1},{2,10},{10,2},{3,11},{11,3},{4,12},{12,4},... | collective-permute-start | bytes 12296 | tf_op jit(solution)/shard_map/ppermute | solution.py:289

commit v11 on v10

--- a/solution.py
+++ b/solution.py
@@ -159,16 +159,14 @@
     )
 
 
-def score_kernel(place, own_source, other_source, emb_target, scores, send, e_ref):
-    core = place[0] & 1
-    e_ref[pl.ds(pl.multiple_of(core * OWN_ROWS, OWN_ROWS), OWN_ROWS), :] = own_source[...]
-    e_ref[pl.ds(pl.multiple_of((1 - core) * OWN_ROWS, OWN_ROWS), OWN_ROWS), :] = other_source[...]
+def score_kernel(own_source, other_source, emb_target, scores, send):
     for at in range(0, ROWS, 256):
         rows = pl.ds(at, 256)
+        half_ref, start = (own_source, at) if at < OWN_ROWS else (other_source, at - OWN_ROWS)
         top = None
         for i in range(COL_BLOCKS // 2):
             part = lax.dot_general(
-                e_ref[rows, :],
+                half_ref[start : start + 256, :],
                 emb_target[i * 256 : (i + 1) * 256, :],
                 (((1,), (1,)), ((), ())),
                 preferred_element_type=jnp.float32,
@@ -192,14 +190,28 @@
                 send[d, ROW_BLOCKS + b : ROW_BLOCKS + b + 1, :] = part_total
 
 
-def column_kernel(scores, got, weights, tops, send, potential):
-    top, total = got[0, 0:ROW_BLOCKS, :], got[0, ROW_BLOCKS:, :]
-    larger = top
-    for d in range(1, N_ROW_PEERS):
-        larger = jnp.maximum(larger, got[d, 0:ROW_BLOCKS, :])
-    total = total * jnp.exp(top - larger)
-    for d in range(1, N_ROW_PEERS):
-        total += got[d, ROW_BLOCKS:, :] * jnp.exp(got[d, 0:ROW_BLOCKS, :] - larger)
+def own_first(place, low, high):
+    same = place[0] & 1 == 0
+    mine, theirs = jnp.where(same, low, high), jnp.where(same, high, low)
+    half = ROW_BLOCKS // 2
+    return mine, jnp.concatenate([theirs[half:], theirs[:half]], axis=0)
+
+
+def column_kernel(place, scores, got, weights, tops, send, potential):
+    tops_of, totals_of = [], []
+    for start in (0, N_ROW_PEERS // 2):
+        peers = range(start, start + N_ROW_PEERS // 2)
+        larger = got[start, 0:ROW_BLOCKS, :]
+        for d in peers[1:]:
+            larger = jnp.maximum(larger, got[d, 0:ROW_BLOCKS, :])
+        total = jnp.zeros((ROW_BLOCKS, LANES), jnp.float32)
+        for d in peers:
+            total += got[d, ROW_BLOCKS:, :] * jnp.exp(got[d, 0:ROW_BLOCKS, :] - larger)
+        tops_of.append(larger)
+        totals_of.append(total)
+    tops_of, totals_of = own_first(place, *tops_of), own_first(place, *totals_of)
+    larger = jnp.maximum(*tops_of)
+    total = sum(part * jnp.exp(top - larger) for part, top in zip(totals_of, tops_of))
     source = LOG_N - (larger + jnp.log(total))
     potential[...] = source
     peaks = [None] * COL_BLOCKS
@@ -250,10 +262,14 @@
             send[d, b : b + 1, :] = total
 
 
-def last_kernel(weights, scale, got, before, sums, potential):
-    total = got[0]
-    for d in range(1, N_ROW_PEERS):
-        total += got[d]
+def last_kernel(place, weights, scale, got, before, sums, potential):
+    parts = []
+    for start in (0, N_ROW_PEERS // 2):
+        total = got[start]
+        for d in range(start + 1, start + N_ROW_PEERS // 2):
+            total += got[d]
+        parts.append(total)
+    total = sum(own_first(place, *parts))
     potential[...] = before[...] + (LOG_N - jnp.log(total))
     ratio = 16384.0 / total
     parts = [jnp.zeros((8, LANES), jnp.float32)] * COL_BLOCKS
@@ -346,9 +362,9 @@
     scores, send = call(
         score_kernel,
         [((COL_BLOCKS, ROWS, LANES), f32), ((N_ROW_PEERS, 2 * ROW_BLOCKS, LANES), f32)],
-        [pltpu.VMEM((ROWS, D), bf16)],
-        [SMEM()] + [VMEM()] * 3,
-    )(me[None], emb_source, other_source, emb_target)
+        [],
+        [VMEM()] * 3,
+    )(emb_source, other_source, emb_target)
 
     got = exchange(send, ("c", "y", "zl"))
     spread_weights, tops, send, source_first = call(
@@ -360,8 +376,8 @@
             ((ROW_BLOCKS, LANES), f32),
         ],
         [],
-        [VMEM()] * 2,
-    )(scores, got)
+        [SMEM()] + [VMEM()] * 2,
+    )(me[None], scores, got)
 
     got = exchange(send, ("zh", "x"))
     send, target_first, scale = call(
@@ -376,8 +392,8 @@
         last_kernel,
         [((N_PEERS, COL_BLOCKS, LANES), f32), ((ROW_BLOCKS, LANES), f32)],
         [],
-        [VMEM()] * 4,
-    )(spread_weights, scale, got, source_first)
+        [SMEM()] + [VMEM()] * 4,
+    )(me[None], spread_weights, scale, got, source_first)
 
     got = exchange(sums, ("zh", "x"))
     got, first, source_potential, target_first = lax.optimization_barrier(
@@ -390,8 +406,7 @@
         [jnp.concatenate([v[:, at : at + PART] for v in (even, odd)], axis=1) for at in (0, PART)], axis=0
     )
     rows = ROW_BLOCKS // 2
-    source_potential = jnp.where(first, source_potential[:rows], source_potential[rows:])
-    return source_potential.reshape(OWN_ROWS), target_potential.reshape(BLOCK)
+    return source_potential[:rows].reshape(OWN_ROWS), target_potential.reshape(BLOCK)
 
 
 def solution(mesh):

time: 98.1 us -> 98.1 us (level)
  no operation moved by 1% of the time
where the time goes in v11:
time: 98.1 us; the launch traced here: 97.8 us
  blocking collectives  45.3 us (46%)
  starting transfers between devices  24.5 us (25%)
  waiting for transfers between devices  12.5 us (13%)
  Pallas kernels  10.8 us (11%)
  other arithmetic  3.16 us (3%)
    all_to_all x4, blocking collectives, exchange(): return lax.all_to_all(value, axes, 0, 0)  45.3 us
    ppermute x13, starting transfers between devices, swap(): return lax.ppermute(value, axis, [(i, i ^ xor) for i in range(size)])  24.5 us
    ppermute x13, waiting for transfers between devices, swap(): return lax.ppermute(value, axis, [(i, i ^ xor) for i in range(size)])  12.5 us
    pallas_call x1, Pallas kernels, on_device(): call(target_kernel, [((COLS, D), bf16)], graph_scratch(BLOCK), [SMEM()] +...  4.03 us
  transfers between devices with their start and end apart: 13, of which 4 were waited for; matrix products, arithmetic and copies ran while one was open for 3% of the time, Pallas kernels for 6%

profile of v11, /device:TPU:1, one launch (start us, length us, event | category | flops | bytes accessed | tf_op | source)
XLA Modules:
  0.0 97.8 jit_solution(17305407307573126780)
XLA Ops:
  0.6 1.6 %shard_map.113 = (bf16[1,272,128]{2,1,0:T(8,128)(2,1)}, bf16[1,272,128]{2,1,0:T(8,128)(2,1)}) custom-call(bf16[1,64,384]{2,1,0:T(8,128)(2,1)} %refs_0_.1, bf16[1,64,128]{2,1,0:T(8,128)(2,1)} %refs_1_.1, s32[1,1,2]{2,1,0:T(1,128)} %refs_2_.1, bf16[1,64,384]{2,1,0:T(8,128)(2,1)} %refs_3_.1, bf16[1,64,128]{2,1,0:T(8,128)(2,1)} %refs_4_.1, s32[1,1,2]{2,1,0:T(1,128)} %refs_5_.1), custom_call_target="tpu_custom_call" | custom-call | tf_op jit(solution)/shard_map/pallas_call | solution.py:50
  2.3 0.0 copy-start.1
  2.3 0.0 copy-start
  2.3 2.6 %collective-permute-start.3 = (bf16[1,272,128]{2,1,0:T(8,128)(2,1)}, bf16[1,272,128]{2,1,0:T(8,128)(2,1)S(1)}, u32[]{:S(2)}, u32[]{:S(2)}) collective-permute-start(bf16[1,272,128]{2,1,0:T(8,128)(2,1)} %get-tuple-element.38), channel_id=1, source_target_pairs={{0,1},{1,0},{2,3},{3,2},{4,5},{5,4},{6,7},{7,6},{8,9},{9,8},{10,11... | collective-permute-start | bytes 208904 | tf_op jit(solution)/shard_map/ppermute | solution.py:305
  4.9 3.0 %collective-permute-start.2 = (bf16[1,272,128]{2,1,0:T(8,128)(2,1)}, bf16[1,272,128]{2,1,0:T(8,128)(2,1)S(1)}, u32[]{:S(2)}, u32[]{:S(2)}) collective-permute-start(bf16[1,272,128]{2,1,0:T(8,128)(2,1)} %get-tuple-element.37), channel_id=1, source_target_pairs={{0,64},{64,0},{128,192},{192,128},{1,65},{65,1},{129,193},{193,129... | collective-permute-start | bytes 208904 | tf_op jit(solution)/shard_map/ppermute | solution.py:305
  7.9 3.3 %collective-permute-start.1 = (bf16[1,272,128]{2,1,0:T(8,128)(2,1)}, bf16[1,272,128]{2,1,0:T(8,128)(2,1)S(1)}, u32[]{:S(2)}, u32[]{:S(2)}) collective-permute-start(bf16[1,272,128]{2,1,0:T(8,128)(2,1)} %get-tuple-element.37), channel_id=1, source_target_pairs={{0,192},{64,128},{128,64},{192,0},{1,193},{65,129},{129,65},{193,1... | collective-permute-start | bytes 208904 | tf_op jit(solution)/shard_map/ppermute | solution.py:305
  11.2 0.9 collective-permute-start
  12.1 0.0 collective-permute-done.3
  12.1 0.9 pad_maximum_fusion.5
  13.0 1.4 %collective-permute-start.4 = (bf16[2,272,128]{2,1,0:T(8,128)(2,1)S(1)}, bf16[2,272,128]{2,1,0:T(8,128)(2,1)S(1)}, u32[]{:S(2)}, u32[]{:S(2)}) collective-permute-start(bf16[2,272,128]{2,1,0:T(8,128)(2,1)S(1)} %pad_maximum_fusion.5), channel_id=1, source_target_pairs={{0,2},{2,0},{4,6},{6,4},{1,3},{3,1},{5,7},{7,5},{8,10},{10,8},{12,... | collective-permute-start | bytes 417800 | tf_op jit(solution)/shard_map/ppermute | solution.py:305
  14.4 1.3 %pad_maximum_fusion.weights = bf16[1536,384]{1,0:T(8,128)(2,1)S(1)} fusion(bf16[384,384]{1,0:T(8,128)(2,1)} %param.19, bf16[384,384]{1,0:T(8,128)(2,1)} %param.18, bf16[384,384]{1,0:T(8,128)(2,1)} %param.17, bf16[384,384]{1,0:T(8,128)(2,1)} %param.16), kind=kLoop, calls=%fused_computation | loop fusion | flops 4718592 | bytes 2359296 | tf_op jit(solution)/shard_map/concatenate | solution.py:329
  15.7 0.0 collective-permute-done.2
  15.7 0.0 collective-permute-done.1
  15.7 3.5 %collective-permute-done = bf16[1,272,128]{2,1,0:T(8,128)(2,1)S(1)} collective-permute-done((bf16[1,272,128]{2,1,0:T(8,128)(2,1)}, bf16[1,272,128]{2,1,0:T(8,128)(2,1)S(1)}, u32[]{:S(2)}, u32[]{:S(2)}) %collective-permute-start) | collective-permute-done | bytes 69664 | tf_op jit(solution)/shard_map/ppermute | solution.py:305
  19.2 0.0 copy-done.1
  19.2 0.0 collective-permute-done.4
  19.2 0.0 copy-done
  19.3 2.8 %collective-permute-start.9 = (bf16[4,272,128]{2,1,0:T(8,128)(2,1)S(1)}, bf16[4,272,128]{2,1,0:T(8,128)(2,1)S(1)}, u32[]{:S(2)}, u32[]{:S(2)}) collective-permute-start(bf16[4,272,128]{2,1,0:T(8,128)(2,1)S(1)} %pad_maximum_fusion.4), channel_id=1, source_target_pairs={{0,6},{2,4},{4,2},{6,0},{1,7},{3,5},{5,3},{7,1},{8,14},{10,12},{12... | collective-permute-start | bytes 835592 | tf_op jit(solution)/shard_map/ppermute | solution.py:305
  22.1 2.7 %collective-permute-start.7 = (bf16[4,272,128]{2,1,0:T(8,128)(2,1)S(1)}, bf16[4,272,128]{2,1,0:T(8,128)(2,1)S(1)}, u32[]{:S(2)}, u32[]{:S(2)}) collective-permute-start(bf16[4,272,128]{2,1,0:T(8,128)(2,1)S(1)} %pad_maximum_fusion.3.own_near), channel_id=1, source_target_pairs={{0,32},{16,48},{32,0},{48,16},{1,33},{17,49},{33,1},{49,17},{2,34}... | collective-permute-start | bytes 835592 | tf_op jit(solution)/shard_map/ppermute | solution.py:305
  24.9 0.9 collective-permute-start.6
  25.7 0.0 collective-permute-start.5
  25.7 2.8 %collective-permute-start.8 = (bf16[4,272,128]{2,1,0:T(8,128)(2,1)S(1)}, bf16[4,272,128]{2,1,0:T(8,128)(2,1)S(1)}, u32[]{:S(2)}, u32[]{:S(2)}) collective-permute-start(bf16[4,272,128]{2,1,0:T(8,128)(2,1)S(1)} %pad_maximum_fusion.3.own_near), channel_id=1, source_target_pairs={{0,8},{8,0},{1,9},{9,1},{2,10},{10,2},{3,11},{11,3},{4,12},{12,4},... | collective-permute-start | bytes 835592 | tf_op jit(solution)/shard_map/ppermute | solution.py:305
  28.6 0.0 collective-permute-done.9
  28.6 0.1 pad_maximum_fusion.2.packed
  28.6 1.5 %shard_map.114.own_source = bf16[512,384]{1,0:T(8,128)(2,1)S(1)} custom-call(s32[1]{0:T(128)} %bitcast.1.place, bf16[8,272,128]{2,1,0:T(8,128)(2,1)S(1)} %pad_maximum_fusion.2.packed, bf16[1536,384]{1,0:T(8,128)(2,1)S(1)} %pad_maximum_fusion.weights), custom_call_target="tpu_custom_call" | custom-call | flops 700000000 | bytes 2000000 | tf_op jit(solution)/shard_map/pallas_call | solution.py:340
  30.2 0.0 collective-permute-done.7
  30.2 7.1 %collective-permute-done.6 = bf16[4,272,128]{2,1,0:T(8,128)(2,1)S(1)} collective-permute-done((bf16[4,272,128]{2,1,0:T(8,128)(2,1)S(1)}, bf16[4,272,128]{2,1,0:T(8,128)(2,1)S(1)}, u32[]{:S(2)}, u32[]{:S(2)}) %collective-permute-start.6) | collective-permute-done | bytes 278560 | tf_op jit(solution)/shard_map/ppermute | solution.py:305
  37.3 0.0 collective-permute-done.5
  37.3 0.1 pad_maximum_fusion.1.own_rest
  37.4 0.0 collective-permute-done.8.other_near
  37.4 1.6 %collective-permute-start.11 = (bf16[12,272,128]{2,1,0:T(8,128)(2,1)S(1)}, bf16[12,272,128]{2,1,0:T(8,128)(2,1)S(1)}, u32[]{:S(2)}, u32[]{:S(2)}) collective-permute-start(bf16[12,272,128]{2,1,0:T(8,128)(2,1)S(1)} %pad_maximum_fusion.1.own_rest), channel_id=1, source_target_pairs={{0,8},{8,0},{1,9},{9,1},{2,10},{10,2},{3,11},{11,3},{4,12},{12,4},... | collective-permute-start | bytes 2506760 | tf_op jit(solution)/shard_map/ppermute | solution.py:305
  39.0 0.3 collective-permute-start.10
  39.3 1.7 %collective-permute-done.11.other_rest = bf16[12,272,128]{2,1,0:T(8,128)(2,1)S(1)} collective-permute-done((bf16[12,272,128]{2,1,0:T(8,128)(2,1)S(1)}, bf16[12,272,128]{2,1,0:T(8,128)(2,1)S(1)}, u32[]{:S(2)}, u32[]{:S(2)}) %collective-permute-start.11) | collective-permute-done | bytes 835616 | tf_op jit(solution)/shard_map/ppermute | solution.py:305
  41.0 4.0 %shard_map.115.emb_target = bf16[1024,384]{1,0:T(8,128)(2,1)S(1)} custom-call(s32[1]{0:T(128)} %bitcast.place, bf16[4,272,128]{2,1,0:T(8,128)(2,1)S(1)} %pad_maximum_fusion.3.own_near, bf16[12,272,128]{2,1,0:T(8,128)(2,1)S(1)} %pad_maximum_fusion.1.own_rest, bf16[4,272,128]{2,1,0:T(8,128)(2,1)S(1)} %collective-permute-done.8.other_near, ...), custom_call_target="tpu_custom_call" | custom-call | tf_op jit(solution)/shard_map/pallas_call | solution.py:355
  45.0 0.0 collective-permute-done.10.other_source
  45.0 1.7 %shard_map.116 = (f32[8,1024,128]{2,1,0:T(8,128)S(1)}, f32[16,16,128]{2,1,0:T(8,128)S(1)}) custom-call(bf16[512,384]{1,0:T(8,128)(2,1)S(1)} %shard_map.114.own_source, bf16[512,384]{1,0:T(8,128)(2,1)S(1)} %collective-permute-done.10.other_source, bf16[1024,384]{1,0:T(8,128)(2,1)S(1)} %shard_map.115.emb_target), custom_call_target="tpu_custom_call" | custom-call | tf_op jit(solution)/shard_map/pallas_call | solution.py:362
  46.8 8.6 %all_to_all.20.got = f32[16,16,128]{2,1,0:T(8,128)S(1)} all-to-all(f32[16,16,128]{2,1,0:T(8,128)S(1)} %get-tuple-element.51), channel_id=1, replica_groups=mesh['zh'=4,'x'=4,'c'=2,'y'=4,'zl'=2] {'c','y','zl'}, dimensions={0} | all-to-all | bytes 262144 | tf_op jit(solution)/shard_map/all_to_all | solution.py:313
  55.3 1.1 %shard_map.117 = (f32[8,1024,128]{2,1,0:T(8,128)S(1)}, f32[8,8,128]{2,1,0:T(8,128)S(1)}, f32[16,8,128]{2,1,0:T(8,128)S(1)}, f32[8,128]{1,0:T(8,128)S(1)}) custom-call(s32[1]{0:T(128)} %bitcast.place, f32[8,1024,128]{2,1,0:T(8,128)S(1)} %get-tuple-element.50.scores, f32[16,16,128]{2,1,0:T(8,128)S(1)} %all_to_all.20.got), custom_call_target="tpu_custom_call" | custom-call | tf_op jit(solution)/shard_map/pallas_call | solution.py:370
  56.4 14.5 %all_to_all.21.got = f32[16,8,128]{2,1,0:T(8,128)S(1)} all-to-all(f32[16,8,128]{2,1,0:T(8,128)S(1)} %get-tuple-element.54), channel_id=1, replica_groups=mesh['zh'=4,'x'=4,'c'=2,'y'=4,'zl'=2] {'zh','x'}, dimensions={0} | all-to-all | bytes 131072 | tf_op jit(solution)/shard_map/all_to_all | solution.py:313
  71.0 0.4 shard_map.118
  71.4 10.6 %all_to_all.22.got = f32[16,8,128]{2,1,0:T(8,128)S(1)} all-to-all(f32[16,8,128]{2,1,0:T(8,128)S(1)} %get-tuple-element.56), channel_id=1, replica_groups=mesh['zh'=4,'x'=4,'c'=2,'y'=4,'zl'=2] {'c','y','zl'}, dimensions={0} | all-to-all | bytes 131072 | tf_op jit(solution)/shard_map/all_to_all | solution.py:313
  82.0 0.4 shard_map.119
  82.4 11.5 %all_to_all.23 = f32[16,8,128]{2,1,0:T(8,128)S(1)} all-to-all(f32[16,8,128]{2,1,0:T(8,128)S(1)} %get-tuple-element.58), channel_id=1, replica_groups=mesh['zh'=4,'x'=4,'c'=2,'y'=4,'zl'=2] {'zh','x'}, dimensions={0} | all-to-all | bytes 131072 | tf_op jit(solution)/shard_map/all_to_all | solution.py:313
  93.9 2.2 %collective-permute-start.12 = (f32[8,128]{1,0:T(8,128)S(1)}, f32[8,128]{1,0:T(8,128)S(1)}, u32[]{:S(2)}, u32[]{:S(2)}) collective-permute-start(f32[8,128]{1,0:T(8,128)S(1)} %subtract_add_fusion), channel_id=1, source_target_pairs={{0,8},{8,0},{1,9},{9,1},{2,10},{10,2},{3,11},{11,3},{4,12},{12,4},... | collective-permute-start | bytes 12296 | tf_op jit(solution)/shard_map/ppermute | solution.py:305
  96.2 0.6 slice_bitcast_fusion
  96.8 0.2 collective-permute-done.12
  97.0 0.1 fusion
  97.1 0.7 maximum_bitcast_fusion
  (5 shorter events, 0.1 us)
Async XLA Ops:
  2.3 16.9 %copy-start.1 = (bf16[1,272,128]{2,1,0:T(8,128)(2,1)S(1)}, bf16[1,272,128]{2,1,0:T(8,128)(2,1)}, u32[]{:S(2)}) copy-start(bf16[1,272,128]{2,1,0:T(8,128)(2,1)} %get-tuple-element.37) | copy-start | bytes 208900
  2.3 17.0 %copy-start = (bf16[1,272,128]{2,1,0:T(8,128)(2,1)S(1)}, bf16[1,272,128]{2,1,0:T(8,128)(2,1)}, u32[]{:S(2)}) copy-start(bf16[1,272,128]{2,1,0:T(8,128)(2,1)} %get-tuple-element.38) | copy-start | bytes 208900
  2.3 9.8 %collective-permute-start.3 = (bf16[1,272,128]{2,1,0:T(8,128)(2,1)}, bf16[1,272,128]{2,1,0:T(8,128)(2,1)S(1)}, u32[]{:S(2)}, u32[]{:S(2)}) collective-permute-start(bf16[1,272,128]{2,1,0:T(8,128)(2,1)} %get-tuple-element.38), channel_id=1, source_target_pairs={{0,1},{1,0},{2,3},{3,2},{4,5},{5,4},{6,7},{7,6},{8,9},{9,8},{10,11... | collective-permute-start | bytes 208904 | tf_op jit(solution)/shard_map/ppermute | solution.py:305
  4.9 10.8 %collective-permute-start.2 = (bf16[1,272,128]{2,1,0:T(8,128)(2,1)}, bf16[1,272,128]{2,1,0:T(8,128)(2,1)S(1)}, u32[]{:S(2)}, u32[]{:S(2)}) collective-permute-start(bf16[1,272,128]{2,1,0:T(8,128)(2,1)} %get-tuple-element.37), channel_id=1, source_target_pairs={{0,64},{64,0},{128,192},{192,128},{1,65},{65,1},{129,193},{193,129... | collective-permute-start | bytes 208904 | tf_op jit(solution)/shard_map/ppermute | solution.py:305
  7.9 7.9 %collective-permute-start.1 = (bf16[1,272,128]{2,1,0:T(8,128)(2,1)}, bf16[1,272,128]{2,1,0:T(8,128)(2,1)S(1)}, u32[]{:S(2)}, u32[]{:S(2)}) collective-permute-start(bf16[1,272,128]{2,1,0:T(8,128)(2,1)} %get-tuple-element.37), channel_id=1, source_target_pairs={{0,192},{64,128},{128,64},{192,0},{1,193},{65,129},{129,65},{193,1... | collective-permute-start | bytes 208904 | tf_op jit(solution)/shard_map/ppermute | solution.py:305
  11.2 8.0 %collective-permute-start = (bf16[1,272,128]{2,1,0:T(8,128)(2,1)}, bf16[1,272,128]{2,1,0:T(8,128)(2,1)S(1)}, u32[]{:S(2)}, u32[]{:S(2)}) collective-permute-start(bf16[1,272,128]{2,1,0:T(8,128)(2,1)} %get-tuple-element.37), channel_id=1, source_target_pairs={{0,128},{64,192},{128,0},{192,64},{1,129},{65,193},{129,1},{193,65... | collective-permute-start | bytes 208904 | tf_op jit(solution)/shard_map/ppermute | solution.py:305
  13.0 6.3 %collective-permute-start.4 = (bf16[2,272,128]{2,1,0:T(8,128)(2,1)S(1)}, bf16[2,272,128]{2,1,0:T(8,128)(2,1)S(1)}, u32[]{:S(2)}, u32[]{:S(2)}) collective-permute-start(bf16[2,272,128]{2,1,0:T(8,128)(2,1)S(1)} %pad_maximum_fusion.5), channel_id=1, source_target_pairs={{0,2},{2,0},{4,6},{6,4},{1,3},{3,1},{5,7},{7,5},{8,10},{10,8},{12,... | collective-permute-start | bytes 417800 | tf_op jit(solution)/shard_map/ppermute | solution.py:305
  19.3 9.3 %collective-permute-start.9 = (bf16[4,272,128]{2,1,0:T(8,128)(2,1)S(1)}, bf16[4,272,128]{2,1,0:T(8,128)(2,1)S(1)}, u32[]{:S(2)}, u32[]{:S(2)}) collective-permute-start(bf16[4,272,128]{2,1,0:T(8,128)(2,1)S(1)} %pad_maximum_fusion.4), channel_id=1, source_target_pairs={{0,6},{2,4},{4,2},{6,0},{1,7},{3,5},{5,3},{7,1},{8,14},{10,12},{12... | collective-permute-start | bytes 835592 | tf_op jit(solution)/shard_map/ppermute | solution.py:305
  22.1 8.1 %collective-permute-start.7 = (bf16[4,272,128]{2,1,0:T(8,128)(2,1)S(1)}, bf16[4,272,128]{2,1,0:T(8,128)(2,1)S(1)}, u32[]{:S(2)}, u32[]{:S(2)}) collective-permute-start(bf16[4,272,128]{2,1,0:T(8,128)(2,1)S(1)} %pad_maximum_fusion.3.own_near), channel_id=1, source_target_pairs={{0,32},{16,48},{32,0},{48,16},{1,33},{17,49},{33,1},{49,17},{2,34}... | collective-permute-start | bytes 835592 | tf_op jit(solution)/shard_map/ppermute | solution.py:305
  24.9 12.4 %collective-permute-start.6 = (bf16[4,272,128]{2,1,0:T(8,128)(2,1)S(1)}, bf16[4,272,128]{2,1,0:T(8,128)(2,1)S(1)}, u32[]{:S(2)}, u32[]{:S(2)}) collective-permute-start(bf16[4,272,128]{2,1,0:T(8,128)(2,1)S(1)} %pad_maximum_fusion.3.own_near), channel_id=1, source_target_pairs={{0,48},{16,32},{32,16},{48,0},{1,49},{17,33},{33,17},{49,1},{2,50}... | collective-permute-start | bytes 835592 | tf_op jit(solution)/shard_map/ppermute | solution.py:305
  25.7 11.6 %collective-permute-start.5 = (bf16[4,272,128]{2,1,0:T(8,128)(2,1)S(1)}, bf16[4,272,128]{2,1,0:T(8,128)(2,1)S(1)}, u32[]{:S(2)}, u32[]{:S(2)}) collective-permute-start(bf16[4,272,128]{2,1,0:T(8,128)(2,1)S(1)} %pad_maximum_fusion.3.own_near), channel_id=1, source_target_pairs={{0,16},{16,0},{32,48},{48,32},{1,17},{17,1},{33,49},{49,33},{2,18}... | collective-permute-start | bytes 835592 | tf_op jit(solution)/shard_map/ppermute | solution.py:305
  25.7 11.6 %collective-permute-start.8 = (bf16[4,272,128]{2,1,0:T(8,128)(2,1)S(1)}, bf16[4,272,128]{2,1,0:T(8,128)(2,1)S(1)}, u32[]{:S(2)}, u32[]{:S(2)}) collective-permute-start(bf16[4,272,128]{2,1,0:T(8,128)(2,1)S(1)} %pad_maximum_fusion.3.own_near), channel_id=1, source_target_pairs={{0,8},{8,0},{1,9},{9,1},{2,10},{10,2},{3,11},{11,3},{4,12},{12,4},... | collective-permute-start | bytes 835592 | tf_op jit(solution)/shard_map/ppermute | solution.py:305
  37.4 3.6 %collective-permute-start.11 = (bf16[12,272,128]{2,1,0:T(8,128)(2,1)S(1)}, bf16[12,272,128]{2,1,0:T(8,128)(2,1)S(1)}, u32[]{:S(2)}, u32[]{:S(2)}) collective-permute-start(bf16[12,272,128]{2,1,0:T(8,128)(2,1)S(1)} %pad_maximum_fusion.1.own_rest), channel_id=1, source_target_pairs={{0,8},{8,0},{1,9},{9,1},{2,10},{10,2},{3,11},{11,3},{4,12},{12,4},... | collective-permute-start | bytes 2506760 | tf_op jit(solution)/shard_map/ppermute | solution.py:305
  39.0 6.0 %collective-permute-start.10 = (bf16[512,384]{1,0:T(8,128)(2,1)S(1)}, bf16[512,384]{1,0:T(8,128)(2,1)S(1)}, u32[]{:S(2)}, u32[]{:S(2)}) collective-permute-start(bf16[512,384]{1,0:T(8,128)(2,1)S(1)} %shard_map.114.own_source), channel_id=1, source_target_pairs={{0,8},{8,0},{1,9},{9,1},{2,10},{10,2},{3,11},{11,3},{4,12},{12,4},... | collective-permute-start | bytes 1179656 | tf_op jit(solution)/shard_map/ppermute | solution.py:305
  93.9 3.1 %collective-permute-start.12 = (f32[8,128]{1,0:T(8,128)S(1)}, f32[8,128]{1,0:T(8,128)S(1)}, u32[]{:S(2)}, u32[]{:S(2)}) collective-permute-start(f32[8,128]{1,0:T(8,128)S(1)} %subtract_add_fusion), channel_id=1, source_target_pairs={{0,8},{8,0},{1,9},{9,1},{2,10},{10,2},{3,11},{11,3},{4,12},{12,4},... | collective-permute-start | bytes 12296 | tf_op jit(solution)/shard_map/ppermute | solution.py:305
